TPU v7x, 32 devices: a whole 2x2x4 slice. The times are simulated.
32 devices in a mesh: box: 8 (over y, x, core), dir: 4 (over z).
Axes of the slice: x: 2, y: 2, z: 4, core: 2. Of those that a mesh axis runs over, the one named last changes fastest.
Arguments:
- currents: bfloat16 [512, 8, 128], P(('box', 'dir')), may hold values from -6 to 6
- positions: bfloat16 [512, 3, 128], P(('box', 'dir')), may hold values from -2 to 2
- radiation: bfloat16 [128, 256], replicated, may hold values from -0.5 to 0.5
- interp_index: int32 [512, 4], replicated, may hold values from 0 to 127
- interp_weight: float32 [512, 4], replicated, may hold values from -3 to 3
- child_phase: float32 [8, 512], replicated, may hold values from -3.140625 to 3.140625
- near_src: int32 [512, 27], P(('box', 'dir')), may hold values from 0 to 511, as said below
- trans_src: int32 [64, 32], P('box'), may hold values from 0 to 63, as said below
- trans_id: int32 [64, 32], P('box'), may hold values from 0 to 315
- trans_count: int32 [64], P('box'), may hold values from 16 to 32, as said below
- trans_table: float32 [316, 2, 512], replicated, may hold values from -0.009 to 0.009
Outputs:
- field: float32 [512, 8, 128], P(('box', 'dir'))
Inputs may be any that keep to these rules, and one draw needn't show every extreme that they name: `near_src`: entry 0 of row i is i itself; every entry lies in the block of 16 boxes that holds i or in a block beside it. `trans_src`: every entry lies in the block of 8 parents that holds the row's parent or in a block beside it. Entries at and after trans_count are ignored; some parent in every block of 8 has 32.
All inputs are finite; a program needn't handle non-finite values.
Results may differ from a plain program's by a relative error of at most 0.0045.
Values may be sent and summed in bfloat16 or wider, within the bound.
No kernel may reach another device: no remote copies, remote signals or barrier semaphores. Data moves between devices by JAX's collectives and lax.ppermute only.
A program may use at most 64 MiB of HBM per device.

v0:
```python
import functools
import math

import jax
import jax.numpy as jnp
from jax import lax
from jax.experimental import pallas as pl
from jax.experimental.pallas import tpu as pltpu
from jax.sharding import PartitionSpec as P

F32 = jnp.float32
BF16 = jnp.bfloat16

WAVENUMBER = 4.0
OFFSET = 0.5
TURN = WAVENUMBER / (2.0 * math.pi)
S0, S1, S2 = (-0.08849679958812066, 0.5822236432316782, -1.1456733260321648)
LEAD = -70.99877392901621
ITEMS = 4
ROWS = 32
STAGES = 4
FIRST_ITEMS = 2


def round_up(value, step):
    return -(-value // step) * step


def swapped(x, axis, pairs):
    return lax.ppermute(x, axis, [way for i, j in pairs for way in ((i, j), (j, i))])


def split3(x):
    high = x.astype(BF16).astype(F32)
    rest = x - high
    mid = rest.astype(BF16).astype(F32)
    return high, mid, rest - mid


def nt_dot(a, b):
    return lax.dot_general(a, b, (((1,), (1,)), ((), ())), preferred_element_type=F32)


def nn_dot(a, b):
    return jnp.dot(a, b, preferred_element_type=F32)


def code_bits(boxes, entries):
    return entries.bit_length(), (boxes - 1).bit_length(), (3 * boxes - 1).bit_length()


def list_places(boxes, entries):
    gap = 2 * ITEMS
    most = FIRST_ITEMS * boxes
    return most, most + gap, round_up(most + gap + boxes * entries // 2 + 2 * gap + 6, 128)


def list_items(near_src, block, here, size):
    boxes, entries = near_src.shape
    most, second_start, length = list_places(boxes, entries)
    count_bits, box_bits, source_bits = code_bits(boxes, entries)
    pair_bits = count_bits + box_bits + source_bits
    lanes = round_up(3 * boxes, 128)
    odd = (here & 1) == 1
    edge = (here == 0) | (here == size - 1)
    local = near_src - block * boxes
    below = local + jnp.where(odd, 2 * boxes, 3 * boxes)
    above = local + jnp.where(odd, boxes, 0)
    local = jnp.where(local < 0, below, jnp.where(local >= boxes, above, local))
    lane = lax.broadcasted_iota(jnp.int32, (boxes, lanes), 1)
    box = lax.broadcasted_iota(jnp.int32, (boxes, lanes), 0)
    count = jnp.zeros((boxes, lanes), jnp.int32)
    for e in range(entries):
        count = count + (local[:, e : e + 1] == lane).astype(jnp.int32)
    present = count > 0
    flags = present.astype(F32)
    box_row = lax.broadcasted_iota(jnp.int32, (boxes, boxes), 0)
    box_col = lax.broadcasted_iota(jnp.int32, (boxes, boxes), 1)
    rank = nn_dot((box_col < box_row).astype(F32).astype(BF16), flags.astype(BF16)).astype(jnp.int32)
    pairs = jnp.sum(flags, axis=0, keepdims=True)
    from_cross = (lane >= 2 * boxes) & edge
    cross_pairs = jnp.where(from_cross[:1], pairs, 0.0)
    group_pairs = jnp.where(from_cross[:1], 0.0, pairs)
    row = lax.broadcasted_iota(jnp.int32, (lanes, lanes), 0)
    col = lax.broadcasted_iota(jnp.int32, (lanes, lanes), 1)
    ahead = (row < col).astype(F32).astype(BF16)
    lists = jnp.concatenate([group_pairs, cross_pairs, jnp.zeros((6, lanes), F32)], axis=0)
    offset = nn_dot(lists.astype(BF16), ahead).astype(jnp.int32)
    own_pairs = jnp.where(lane[:1] < boxes, group_pairs, 0.0)

    def total(pairs):
        return jnp.sum(pairs, axis=1, keepdims=True).astype(jnp.int32)

    first_total = jnp.minimum(total(own_pairs), 2 * most)
    second_total = total(group_pairs) - first_total
    cross_total = total(cross_pairs)
    order = offset[0:1] + rank
    in_second = order >= first_total
    order = jnp.where(in_second, order - first_total, order)
    order = jnp.where(from_cross, offset[1:2] + rank, order)
    half = order >> 1
    place = jnp.where(from_cross, (length - 4) - half, jnp.where(in_second, second_start + half, half))
    place = jnp.where(present, place, -1)
    code = (lane << (count_bits + box_bits)) | (box << count_bits) | count
    code = jnp.where((order & 1) == 1, code << pair_bits, code)
    place_t = place.T
    code_t = code.T
    rows = 3 * boxes
    slot = lax.broadcasted_iota(jnp.int32, (rows, length), 1)
    found = jnp.zeros((rows, length), jnp.int32)
    for i in range(boxes):
        hit = place_t[:rows, i : i + 1] == slot
        found = found + jnp.where(hit, code_t[:rows, i : i + 1], 0)
    listed = jnp.sum(found, axis=0, keepdims=True)
    at = lax.broadcasted_iota(jnp.int32, (1, length), 1)
    for back, pairs in ((3, first_total), (2, second_total), (1, cross_total)):
        listed = jnp.where(at == length - back, (pairs + 1) >> 1, listed)
    return listed


def start_all(copies, sems):
    started = [pltpu.make_async_copy(src, dst, sems.at[k]) for k, (src, dst) in enumerate(copies)]
    for copy in started:
        copy.start()
    return started


def wait_all(started):
    for copy in started:
        copy.wait()


def outgoing_kernel(
    x_hbm, pos_hbm, rad_hbm, idx_hbm, wgt_hbm, phase_hbm, packet_ref, spectra_ref, imat_ref, cos_ref, sin_ref, rad_ref,
    x_ref, pos_ref, idx_ref, wgt_ref, phase_ref, sems
):
    wait_all(
        start_all(
            (
                (x_hbm, x_ref),
                (pos_hbm, pos_ref),
                (rad_hbm, rad_ref),
                (idx_hbm, idx_ref),
                (wgt_hbm, wgt_ref),
                (phase_hbm, phase_ref),
            ),
            sems,
        )
    )
    leaf_dirs, parent_dirs = imat_ref.shape
    x_rows, _, width = x_ref.shape
    axes, boxes, _ = pos_ref.shape
    waves = x_rows * 16 // boxes
    chunks = parent_dirs // 128
    own_rows = x_rows + axes * boxes // 16
    packet_ref[:x_rows] = x_ref[...]
    packet_ref[x_rows:own_rows] = pos_ref[...].reshape(axes * boxes // 16, 16, width)
    column = lax.broadcasted_iota(jnp.int32, (leaf_dirs, parent_dirs), 0)
    imat = jnp.zeros((leaf_dirs, parent_dirs), F32)
    for s in range(idx_ref.shape[0]):
        imat = imat + jnp.where(idx_ref[s : s + 1, :] == column, wgt_ref[s : s + 1, :], 0.0)
    imat = imat.astype(BF16)
    imat_ref[...] = imat
    cos_phase = jnp.cos(phase_ref[...])
    sin_phase = jnp.sin(phase_ref[...])
    cos_ref[...] = cos_phase
    sin_ref[...] = sin_phase
    leaf = nn_dot(x_ref[...].reshape(boxes * waves, width), rad_ref[...]).astype(BF16)
    up_re = nn_dot(leaf[:, :leaf_dirs], imat)
    up_im = nn_dot(leaf[:, leaf_dirs:], imat)
    for q in range(boxes // 8):
        re = jnp.zeros((waves, parent_dirs), F32)
        im = jnp.zeros((waves, parent_dirs), F32)
        for c in range(8):
            at = (q * 8 + c) * waves
            ure = up_re[at : at + waves]
            uim = up_im[at : at + waves]
            re = re + (cos_phase[c : c + 1] * ure - sin_phase[c : c + 1] * uim)
            im = im + (sin_phase[c : c + 1] * ure + cos_phase[c : c + 1] * uim)
        both = jnp.concatenate([re, im], axis=0).astype(BF16)
        for k in range(chunks):
            part = both[:, k * 128 : (k + 1) * 128]
            packet_ref[own_rows + q * chunks + k] = part
            spectra_ref[q * chunks + k] = part


def carries_packet(step):
    return step & (step + 1) == 0


def group_kernel(own_ref, *refs):
    *step_refs, _, group_ref = refs
    size = lax.axis_size("dir")
    rows = own_ref.shape[0]
    here = lax.axis_index("dir")
    group_ref[pl.ds(here * rows, rows)] = own_ref[...]
    for step, ref in enumerate(step_refs, 1):
        group_ref[pl.ds((here ^ step) * rows, rows)] = ref[ref.shape[0] - rows :]
    group_ref[size * rows :] = step_refs[-1][: step_refs[-1].shape[0] - rows]


def features(planes):
    rows, _, width = planes.shape
    boxes = rows * 16 // 3
    planes = planes.astype(F32).reshape(3, boxes, width)
    at = lax.broadcasted_iota(jnp.int32, (boxes, 8, width), 1)
    pos = jnp.zeros((boxes, 8, width), F32)
    for axis in range(3):
        pos = jnp.where(at == axis, planes[axis][:, None, :], pos)
    scale = TURN * TURN
    norm = split3(scale * jnp.sum(pos * pos, axis=1, keepdims=True))
    first = jnp.where(at < 3, pos, 1.0)
    first = jnp.where(at == 3, norm[0], jnp.where(at == 4, norm[1], jnp.where(at == 5, norm[2], first)))
    second = jnp.where(at == 3, 1.0, pos + pltpu.roll(pos, 4, 1))
    source = jnp.concatenate([first, second], axis=1).astype(BF16)
    cross = split3((-2.0 * scale) * pos)
    first = jnp.where(at < 3, cross[0], 1.0)
    first = jnp.where(at == 6, norm[0], jnp.where(at == 7, norm[1], first))
    second = jnp.where(at == 3, norm[2], cross[1] + pltpu.roll(cross[2], 4, 1))
    return source, jnp.concatenate([first, second], axis=1).astype(BF16)


def turn_sources(source, src_ref, start):
    boxes, rows, width = source.shape
    eye = lax.broadcasted_iota(jnp.int32, (width, width), 0) == lax.broadcasted_iota(jnp.int32, (width, width), 1)
    turned = nt_dot(eye.astype(F32).astype(BF16), source.reshape(boxes * rows, width))
    column = lax.broadcasted_iota(jnp.int32, (width, 128), 1)
    for b in range(boxes):
        at = b * rows
        lanes = turned[:, at // 128 * 128 : at // 128 * 128 + 128]
        for slot in range(2):
            shift = (slot * rows - at) % 128
            moved = pltpu.roll(lanes, shift, 1) if shift else lanes
            inside = (column >= slot * rows) & (column < (slot + 1) * rows)
            src_ref[slot, start + b] = jnp.where(inside, moved, 0.0).astype(BF16)


def take_currents(x_rows, win_ref, start):
    for k in range(x_rows.shape[0]):
        both = x_rows[k]
        wide = both.astype(F32)
        win_ref[start + 2 * k] = both
        win_ref[start + 2 * k + 1] = jnp.concatenate([wide[8:], wide[:8]], axis=0).astype(BF16)


def near_sum(entries, total, item_at, first_source, src_ref, win_ref, obs_ref, out_ref, scratch):
    u0_ref, u1_ref, t0_ref, t1_ref = scratch
    boxes, waves, width = out_ref.shape
    count_bits, box_bits, source_bits = code_bits(boxes, entries)
    pair_bits = count_bits + box_bits + source_bits
    t1_ref[...] = jnp.zeros(t1_ref.shape, BF16)
    upper = lax.broadcasted_iota(jnp.int32, (2 * waves, width), 0) < waves
    empty = jnp.zeros((16, width), BF16)

    def pair_at(chunk, g, slot):
        code = item_at(chunk * ITEMS + g) >> (slot * pair_bits)
        source = (code >> (count_bits + box_bits)) & ((1 << source_bits) - 1)
        if first_source:
            source = jnp.maximum(source - first_source, 0)
        return source, (code >> count_bits) & ((1 << box_bits) - 1), code & ((1 << count_bits) - 1)

    def distances(chunk, g, u_ref):
        source0, box0, _ = pair_at(chunk, g, 0)
        source1, box1, _ = pair_at(chunk, g, 1)
        sources = src_ref[0, source0] + src_ref[1, source1]
        observers = jnp.concatenate(
            [
                jnp.concatenate([obs_ref[box0], empty], axis=1),
                jnp.concatenate([empty, obs_ref[box1]], axis=1),
            ],
            axis=0,
        )
        u_ref[g] = nn_dot(sources[:, :32], observers)

    def tile(g, u_ref, t_ref):
        for at in range(0, width, ROWS):
            v = jnp.maximum(u_ref[g, at : at + ROWS], 1e-12)
            q = v * lax.rsqrt(v)
            t = q - jnp.round(q)
            x = 0.25 - jnp.abs(t)
            z = x * x
            cosine = x * (((z + S2) * z + S1) * z + S0)
            t_ref[g, at : at + ROWS] = (cosine * pltpu.reciprocal(q + OFFSET * TURN, approx=True)).astype(BF16)

    def product(chunk, g, t_ref):
        source0, box0, count0 = pair_at(chunk, g, 0)
        source1, box1, count1 = pair_at(chunk, g, 1)
        currents = jnp.where(upper, win_ref[source0].astype(F32), win_ref[source1 ^ 1].astype(F32)).astype(BF16)
        got = nn_dot(currents, t_ref[g])
        out_ref[box0] += count0.astype(F32) * got[:waves, :width]
        out_ref[box1] += count1.astype(F32) * got[waves:, width:]

    u_refs = (u0_ref, u1_ref)
    t_refs = (t0_ref, t1_ref)

    def stage(chunk, turn):
        for g in range(ITEMS):
            distances(chunk + 1, g, u_refs[1 - turn])
            product(jnp.maximum(chunk - 1, 0), g, t_refs[1 - turn])
            tile(g, u_refs[turn], t_refs[turn])

    def body(k, carry):
        for j in range(STAGES):
            stage(k * STAGES + j, j & 1)
        return carry

    def finish(turn):
        for g in range(ITEMS):
            product(jnp.maximum(chunks - 1, 0), g, t_refs[turn])

    chunks = (total + (ITEMS - 1)) // ITEMS
    rounds = chunks // STAGES
    for g in range(ITEMS):
        distances(0, g, u0_ref)
    lax.fori_loop(0, rounds, body, 0)
    for j in range(STAGES - 1):
        pl.when(rounds * STAGES + j < chunks)(functools.partial(stage, rounds * STAGES + j, j & 1))
    pl.when((chunks & 1) == 0)(functools.partial(finish, 1))
    pl.when((chunks & 1) == 1)(functools.partial(finish, 0))


def prepare_kernel(
    own_ref, near_hbm, src_hbm, id_hbm, count_hbm, table_hbm, out_ref, items_ref, obs_ref, src_ref, gain_ref, near_ref,
    trans_src_ref, trans_id_ref, trans_count_ref, rows_ref, list_ref, win_ref, u0_ref, u1_ref, t0_ref, t1_ref, sems
):
    boxes = obs_ref.shape[0]
    entries = near_ref.shape[1]
    length = list_ref.shape[1]
    parents, window = gain_ref.shape[:2]
    listed = src_hbm.shape[1]
    near_copy, *list_copies = start_all(
        (
            (near_hbm, near_ref),
            (src_hbm, trans_src_ref),
            (id_hbm, trans_id_ref),
            (count_hbm, trans_count_ref),
        ),
        sems,
    )
    gain_ref[...] = jnp.zeros(gain_ref.shape, F32)
    plane_rows = 3 * boxes // 16
    source, observer = features(own_ref[boxes // 2 : boxes // 2 + plane_rows])
    turn_sources(source, src_ref, 0)
    take_currents(own_ref[: boxes // 2], win_ref, 0)
    obs_ref[...] = observer
    wait_all(list_copies)
    row0 = lax.axis_index("dir") * parents
    for q in range(parents):
        for e in range(listed):
            pltpu.make_async_copy(
                table_hbm.at[trans_id_ref[row0 + q, e]], rows_ref.at[q * listed + e], sems.at[1]
            ).start()
    near_copy.wait()
    block = lax.axis_index(("box", "dir"))
    items_ref[...] = list_items(near_ref[...], block, lax.axis_index("dir"), lax.axis_size("dir"))
    fetch = pltpu.make_async_copy(items_ref, list_ref, sems.at[0])
    fetch.start()
    out_ref[...] = jnp.zeros(out_ref.shape, F32)
    pltpu.make_async_copy(rows_ref, rows_ref, sems.at[1]).wait()
    first = (lax.axis_index("box") - 1) * (window // 3)
    for q in range(parents):
        for e in range(listed):
            live = (e < trans_count_ref[row0 + q]).astype(F32)
            s = jnp.clip(trans_src_ref[row0 + q, e] - first, 0, window - 1)
            gain_ref[q, s] += rows_ref[q * listed + e] * live
    fetch.wait()
    near_sum(
        entries,
        list_ref[0, length - 3],
        lambda k: list_ref[0, k],
        0,
        src_ref,
        win_ref,
        obs_ref,
        out_ref,
        (u0_ref, u1_ref, t0_ref, t1_ref),
    )


def near_kernel(entries, items_ref, own_ref, *refs):
    *step_refs, obs_ref, own_src_ref, first_ref, out_ref, win_ref, src_ref, list_ref, u0_ref, u1_ref, t0_ref, t1_ref, sem = refs
    boxes, waves, width = out_ref.shape
    fetch = pltpu.make_async_copy(items_ref, list_ref, sem)
    fetch.start()
    length = list_ref.shape[1]
    here = lax.axis_index("dir")
    other_side = jnp.where((here & 1) == 0, here - 1, here + 1)
    x_rows = boxes // 2

    def take(ref, part):
        take_currents(ref[:x_rows], win_ref, part * boxes)
        source, _ = features(ref[x_rows : x_rows + 3 * boxes // 16])
        turn_sources(source, src_ref, part * boxes)

    take_currents(own_ref[:x_rows], win_ref, 0)
    src_ref[:, :boxes] = own_src_ref[...]
    take(step_refs[0], 1)
    for k, ref in enumerate(step_refs[1:], 2):
        pl.when((here ^ ((1 << k) - 1)) == other_side)(functools.partial(take, ref, 2))
    second_start = list_places(boxes, entries)[1]
    out_ref[...] = first_ref[...]
    fetch.wait()
    near_sum(
        entries,
        list_ref[0, length - 2],
        lambda k: list_ref[0, second_start + k],
        0,
        src_ref,
        win_ref,
        obs_ref,
        out_ref,
        (u0_ref, u1_ref, t0_ref, t1_ref),
    )


def incoming_kernel(
    entries, items_ref, even_ref, own_ref, odd_ref, gain_ref, cos_ref, sin_ref, imat_ref, rad_ref, obs_ref, near_ref, out_ref,
    sum_ref, win_ref, src_ref, down_re_ref, down_im_ref, list_ref, u0_ref, u1_ref, t0_ref, t1_ref, sem
):
    parents, window, _, parent_dirs = gain_ref.shape
    boxes, waves, width = near_ref.shape
    chunks = parent_dirs // 128
    group = window // 3
    fetch = pltpu.make_async_copy(items_ref, list_ref, sem)
    fetch.start()
    length = list_ref.shape[1]
    odd_box = lax.axis_index("box") & 1
    sum_ref[...] = near_ref[...]
    x_rows = boxes // 2
    packet_rows = x_rows + 3 * boxes // 16
    from_even = jnp.where(lax.axis_index("dir") == 0, 1, 0) == odd_box
    even_packet, odd_packet = (ref[ref.shape[0] - packet_rows :] for ref in (even_ref, odd_ref))
    packet = jnp.where(from_even, even_packet.astype(F32), odd_packet.astype(F32)).astype(BF16)
    take_currents(packet[:x_rows], win_ref, 0)
    source, _ = features(packet[x_rows:])
    turn_sources(source, src_ref, 0)
    fetch.wait()
    cos_phase = cos_ref[...]
    sin_phase = sin_ref[...]
    sums = tuple(jnp.zeros((waves, 128), F32) for _ in range(parents * chunks * 2))
    for part, ref in ((2 - 2 * odd_box, even_ref), (1, own_ref), (2 * odd_box, odd_ref)):

        def add_source(s, sums, part=part, ref=ref):
            sums = list(sums)
            gains = [gain_ref[q, part * group + s] for q in range(parents)]
            for k in range(chunks):
                spectrum = ref[s * chunks + k].astype(F32)
                sre, sim = spectrum[:waves], spectrum[waves:]
                for q in range(parents):
                    gre = gains[q][0:1, k * 128 : (k + 1) * 128]
                    gim = gains[q][1:2, k * 128 : (k + 1) * 128]
                    at = (q * chunks + k) * 2
                    sums[at] = sums[at] + (gre * sre - gim * sim)
                    sums[at + 1] = sums[at + 1] + (gre * sim + gim * sre)
            return tuple(sums)

        sums = lax.fori_loop(0, group, add_source, sums, unroll=8)
    for q in range(parents):
        for k in range(chunks):
            at = (q * chunks + k) * 2
            re = sums[at].astype(BF16).astype(F32)
            im = sums[at + 1].astype(BF16).astype(F32)
            lanes = slice(k * 128, (k + 1) * 128)
            for c in range(8):
                cos, sin = cos_phase[c : c + 1, lanes], sin_phase[c : c + 1, lanes]
                rows = slice((q * 8 + c) * waves, (q * 8 + c + 1) * waves)
                down_re_ref[rows, lanes] = cos * re + sin * im
                down_im_ref[rows, lanes] = cos * im - sin * re
    imat = imat_ref[...]
    in_re = nt_dot(down_re_ref[...].astype(BF16), imat)
    in_im = nt_dot(down_im_ref[...].astype(BF16), imat)
    incoming = jnp.concatenate([in_re, in_im], axis=1).astype(BF16)
    far = nt_dot(incoming, rad_ref[...])
    near_sum(
        entries,
        list_ref[0, length - 1],
        lambda k: list_ref[0, length - 4 - k],
        2 * boxes,
        src_ref,
        win_ref,
        obs_ref,
        sum_ref,
        (u0_ref, u1_ref, t0_ref, t1_ref),
    )
    factor = TURN * LEAD / math.sqrt(entries * width)
    out_ref[...] = sum_ref[...] * factor + far.reshape(near_ref.shape)


def per_device(
    currents, positions, radiation, interp_index, interp_weight, child_phase, near_src, trans_src, trans_id,
    trans_count, trans_table
):
    boxes, waves, width = currents.shape
    entries = near_src.shape[1]
    leaf_dirs = radiation.shape[1] // 2
    parent_dirs = child_phase.shape[1]
    parents = boxes // 8
    spectra_rows = parents * parent_dirs // 128
    size = lax.axis_size("dir")
    vmem = pl.BlockSpec(memory_space=pltpu.VMEM)
    hbm = pl.BlockSpec(memory_space=pltpu.HBM)
    params = pltpu.CompilerParams(vmem_limit_bytes=32 * 1024 * 1024)

    def in_hbm(x):
        return pltpu.with_memory_space_constraint(x, pltpu.HBM)

    def shaped(shape, dtype):
        return jax.ShapeDtypeStruct(shape, dtype)

    x_rows = boxes // 2
    own_rows = x_rows + 3 * boxes // 16
    operands = (currents.reshape(x_rows, 2 * waves, width), positions.transpose(1, 0, 2), radiation, interp_index.T, interp_weight.T, child_phase)
    packet, spectra, imat, cos_phase, sin_phase, rad = pl.pallas_call(
        outgoing_kernel,
        out_shape=(
            shaped((own_rows + spectra_rows, 16, width), BF16),
            shaped((spectra_rows, 2 * waves, 128), BF16),
            shaped((leaf_dirs, parent_dirs), BF16),
            shaped((8, parent_dirs), F32),
            shaped((8, parent_dirs), F32),
            shaped(radiation.shape, BF16),
        ),
        in_specs=[hbm] * len(operands),
        out_specs=(vmem,) * 6,
        scratch_shapes=[pltpu.VMEM(x.shape, x.dtype) for x in operands if x is not radiation]
        + [pltpu.SemaphoreType.DMA((len(operands),))],
        compiler_params=params,
        name="outgoing",
    )(*[in_hbm(x) for x in operands])

    steps = []
    for step in range(1, size):
        pairs = [(i, i ^ step) for i in range(size) if i < i ^ step]
        steps.append(swapped(packet if carries_packet(step) else spectra, "dir", pairs))

    length = list_places(boxes, entries)[2]
    window = 3 * trans_src.shape[0]
    near_scratch = [
        pltpu.VMEM((ITEMS, width, 2 * width), F32),
        pltpu.VMEM((ITEMS, width, 2 * width), F32),
        pltpu.VMEM((ITEMS, width, 2 * width), BF16),
        pltpu.VMEM((ITEMS, width, 2 * width), BF16),
    ]
    first_sum, items, observers, sources, gains = pl.pallas_call(
        prepare_kernel,
        out_shape=(
            shaped((boxes, waves, width), F32),
            shaped((1, length), jnp.int32),
            shaped((boxes, 16, width), BF16),
            shaped((2, boxes, width, 128), BF16),
            shaped((parents, window, 2, parent_dirs), F32),
        ),
        in_specs=[vmem] + [hbm] * 5,
        out_specs=(vmem,) * 5,
        scratch_shapes=[
            pltpu.VMEM(near_src.shape, jnp.int32),
            pltpu.SMEM(trans_src.shape, jnp.int32),
            pltpu.SMEM(trans_id.shape, jnp.int32),
            pltpu.SMEM(trans_count.shape, jnp.int32),
            pltpu.VMEM((parents * trans_src.shape[1], 2, parent_dirs), F32),
            pltpu.SMEM((1, length), jnp.int32),
            pltpu.VMEM((boxes, 16, width), BF16),
        ]
        + near_scratch
        + [pltpu.SemaphoreType.DMA((4,))],
        compiler_params=params,
        name="prepare",
    )(packet, *[in_hbm(x) for x in (near_src, trans_src, trans_id, trans_count, trans_table)])

    group = pl.pallas_call(
        group_kernel,
        out_shape=shaped((size * spectra_rows + own_rows, 2 * waves, 128), BF16),
        in_specs=[vmem] * (2 + len(steps)),
        out_specs=vmem,
        compiler_params=params,
        name="group",
    )(spectra, *steps, items)
    groups = lax.axis_size("box")
    group_odd = swapped(group, "box", [(i, i + 1) for i in range(1, groups - 1, 2)])
    group_even = swapped(group, "box", [(i, i + 1) for i in range(0, groups - 1, 2)])

    packets = [x for step, x in enumerate(steps, 1) if carries_packet(step)]
    near = pl.pallas_call(
        functools.partial(near_kernel, entries),
        out_shape=shaped((boxes, waves, width), F32),
        in_specs=[vmem] * (5 + len(packets)),
        out_specs=vmem,
        scratch_shapes=[
            pltpu.VMEM((3 * boxes, 16, width), BF16),
            pltpu.VMEM((2, 3 * boxes, width, 128), BF16),
            pltpu.SMEM((1, length), jnp.int32),
        ]
        + near_scratch
        + [pltpu.SemaphoreType.DMA],
        compiler_params=params,
        name="near",
    )(items, packet, *packets, observers, sources, first_sum)

    return pl.pallas_call(
        functools.partial(incoming_kernel, entries),
        out_shape=shaped((boxes, waves, width), F32),
        in_specs=[vmem] * 11,
        out_specs=vmem,
        scratch_shapes=[
            pltpu.VMEM((boxes, waves, width), F32),
            pltpu.VMEM((boxes, 16, width), BF16),
            pltpu.VMEM((2, boxes, width, 128), BF16),
            pltpu.VMEM((boxes * waves, parent_dirs), F32),
            pltpu.VMEM((boxes * waves, parent_dirs), F32),
            pltpu.SMEM((1, length), jnp.int32),
        ]
        + near_scratch
        + [pltpu.SemaphoreType.DMA],
        compiler_params=params,
        name="incoming",
    )(items, group_even, group, group_odd, gains, cos_phase, sin_phase, imat, rad, observers, near)


def solution(mesh):
    placed = (
        P(("box", "dir"), None, None),
        P(("box", "dir"), None, None),
        P(),
        P(),
        P(),
        P(),
        P(("box", "dir"), None),
        P("box", None),
        P("box", None),
        P("box"),
        P(),
    )
    return jax.shard_map(
        per_device,
        mesh=mesh,
        in_specs=placed,
        out_specs=P(("box", "dir"), None, None),
        check_vma=False,
    )
```

profile of v0, /device:TPU:1, one launch (start us, length us, event | category | flops | bytes accessed | tf_op | source)
XLA Modules:
  0.0 32.1 jit_solution(7626627111814393962)
XLA Ops:
  0.0 1.3 %outgoing.1 = (bf16[19,16,128]{2,1,0:T(8,128)(2,1)S(1)}, bf16[8,16,128]{2,1,0:T(8,128)(2,1)S(1)}, bf16[128,512]{1,0:T(8,128)(2,1)S(1)}, f32[8,512]{1,0:T(8,128)S...) custom-call(bf16[8,16,128]{2,1,0:T(8,128)(2,1)} %bitcast.4, bf16[3,16,128]{2,1,0:T(8,128)(2,1)} %bitcast.5, ...), custom_call_target="tpu_custom_call" | custom-call | tf_op jit(solution)/shard_map/outgoing/pallas_call | solution.py:513
  1.3 2.2 %collective-permute-start = (bf16[19,16,128]{2,1,0:T(8,128)(2,1)S(1)}, bf16[19,16,128]{2,1,0:T(8,128)(2,1)S(1)}, u32[]{:S(2)}, u32[]{:S(2)}) collective-permute-start(bf16[19,16,128]{2,1,0:T(8,128)(2,1)S(1)} %get-tuple-element.16.own_ref), channel_id=1, source_target_pairs={{0,1},{1,0},{2,3},{3,2},{4,5},{5,4},{6,7},{7,6},{8,9},{9,8},{10,11... | collective-permute-start | bytes 233480 | tf_op jit(solution)/shard_map/ppermute | solution.py:30
  3.5 2.2 %collective-permute-start.2 = (bf16[19,16,128]{2,1,0:T(8,128)(2,1)S(1)}, bf16[19,16,128]{2,1,0:T(8,128)(2,1)S(1)}, u32[]{:S(2)}, u32[]{:S(2)}) collective-permute-start(bf16[19,16,128]{2,1,0:T(8,128)(2,1)S(1)} %get-tuple-element.16.own_ref), channel_id=1, source_target_pairs={{0,3},{3,0},{1,2},{2,1},{4,7},{7,4},{5,6},{6,5},{8,11},{11,8},{9,1... | collective-permute-start | bytes 233480 | tf_op jit(solution)/shard_map/ppermute | solution.py:30
  5.7 0.1 collective-permute-start.1
  5.8 6.0 %prepare.1 = (f32[16,8,128]{2,1,0:T(8,128)S(1)}, s32[1,384]{1,0:T(1,128)S(1)}, bf16[16,16,128]{2,1,0:T(8,128)(2,1)S(1)}, bf16[2,16,128,128]{3,2,1,0:T(8,128)(2,1)S(1)}, f32[2,24,2,512]{3,2,1,0:T(2,128)S(1)}) custom-call(bf16[19,16,128]{2,1,0:T(8,128)(2,1)S(1)} %get-tuple-element.16.own_ref, s32[16,27]{1,0:T(8,128)} %near_hbm.1, s32[8,32]{1,0:T(8,128)} %src_hbm.1, ...), custom_call_target="tpu_custom_call" | custom-call | tf_op jit(solution)/shard_map/prepare/pallas_call | solution.py:544
  11.9 0.0 collective-permute-done.1.refs_1_
  11.9 0.0 collective-permute-done.refs_0_
  11.9 0.0 collective-permute-done.2.refs_2_.refs_1_
  11.9 1.3 %collective-permute-start.3 = (bf16[43,16,128]{2,1,0:T(8,128)(2,1)S(1)}, bf16[43,16,128]{2,1,0:T(8,128)(2,1)S(1)}, u32[]{:S(2)}, u32[]{:S(2)}) collective-permute-start(bf16[43,16,128]{2,1,0:T(8,128)(2,1)S(1)} %group.1.own_ref), channel_id=1, source_target_pairs={{0,4},{4,0},{8,12},{12,8},{16,20},{20,16},{24,28},{28,24},{1,5},{5... | collective-permute-start | bytes 528392 | tf_op jit(solution)/shard_map/ppermute | solution.py:30
  13.2 3.0 %collective-permute-start.4 = (bf16[43,16,128]{2,1,0:T(8,128)(2,1)S(1)}, bf16[43,16,128]{2,1,0:T(8,128)(2,1)S(1)}, u32[]{:S(2)}, u32[]{:S(2)}) collective-permute-start(bf16[43,16,128]{2,1,0:T(8,128)(2,1)S(1)} %group.1.own_ref), channel_id=1, source_target_pairs={{4,8},{8,4},{12,16},{16,12},{20,24},{24,20},{5,9},{9,5},{13,17},{1... | collective-permute-start | bytes 528392 | tf_op jit(solution)/shard_map/ppermute | solution.py:30
  16.2 8.6 %near.1.near_ref = f32[16,8,128]{2,1,0:T(8,128)S(1)} custom-call(s32[1,384]{1,0:T(1,128)S(1)} %get-tuple-element.17.refs_3_.items_ref, bf16[19,16,128]{2,1,0:T(8,128)(2,1)S(1)} %get-tuple-element.16.own_ref, bf16[19,16,128]{2,1,0:T(8,128)(2,1)S(1)} %collective-permute-done.refs_0_, bf16[19,16,128]{2,1,0:T(8,128)(2,1)S(1)} %collective-permute-done.2.refs_2_.refs_1_, ...), custom_call_target="tpu_custom_call" | custom-call | tf_op jit(solution)/shard_map/near/pallas_call | solution.py:583
  24.8 0.0 collective-permute-done.3.even_ref
  24.8 0.0 collective-permute-done.4.odd_ref
  24.9 7.2 %incoming.1 = f32[16,8,128]{2,1,0:T(8,128)} custom-call(s32[1,384]{1,0:T(1,128)S(1)} %get-tuple-element.17.refs_3_.items_ref, bf16[43,16,128]{2,1,0:T(8,128)(2,1)S(1)} %collective-permute-done.3.even_ref, bf16[43,16,128]{2,1,0:T(8,128)(2,1)S(1)} %group.1.own_ref, bf16[43,16,128]{2,1,0:T(8,128)(2,1)S(1)} %collective-permute-done.4.odd_ref, ...), custom_call_target="tpu_custom_call" | custom-call | tf_op jit(solution)/shard_map/incoming/pallas_call | solution.py:599
  (1 shorter events, 0.0 us)
Async XLA Ops:
  1.3 10.6 %collective-permute-start = (bf16[19,16,128]{2,1,0:T(8,128)(2,1)S(1)}, bf16[19,16,128]{2,1,0:T(8,128)(2,1)S(1)}, u32[]{:S(2)}, u32[]{:S(2)}) collective-permute-start(bf16[19,16,128]{2,1,0:T(8,128)(2,1)S(1)} %get-tuple-element.16.own_ref), channel_id=1, source_target_pairs={{0,1},{1,0},{2,3},{3,2},{4,5},{5,4},{6,7},{7,6},{8,9},{9,8},{10,11... | collective-permute-start | bytes 233480 | tf_op jit(solution)/shard_map/ppermute | solution.py:30
  3.5 8.4 %collective-permute-start.2 = (bf16[19,16,128]{2,1,0:T(8,128)(2,1)S(1)}, bf16[19,16,128]{2,1,0:T(8,128)(2,1)S(1)}, u32[]{:S(2)}, u32[]{:S(2)}) collective-permute-start(bf16[19,16,128]{2,1,0:T(8,128)(2,1)S(1)} %get-tuple-element.16.own_ref), channel_id=1, source_target_pairs={{0,3},{3,0},{1,2},{2,1},{4,7},{7,4},{5,6},{6,5},{8,11},{11,8},{9,1... | collective-permute-start | bytes 233480 | tf_op jit(solution)/shard_map/ppermute | solution.py:30
  5.7 6.2 %collective-permute-start.1 = (bf16[8,16,128]{2,1,0:T(8,128)(2,1)S(1)}, bf16[8,16,128]{2,1,0:T(8,128)(2,1)S(1)}, u32[]{:S(2)}, u32[]{:S(2)}) collective-permute-start(bf16[8,16,128]{2,1,0:T(8,128)(2,1)S(1)} %get-tuple-element.18.own_ref), channel_id=1, source_target_pairs={{0,2},{2,0},{1,3},{3,1},{4,6},{6,4},{5,7},{7,5},{8,10},{10,8},{9,1... | collective-permute-start | bytes 98312 | tf_op jit(solution)/shard_map/ppermute | solution.py:30
  11.9 12.9 %collective-permute-start.3 = (bf16[43,16,128]{2,1,0:T(8,128)(2,1)S(1)}, bf16[43,16,128]{2,1,0:T(8,128)(2,1)S(1)}, u32[]{:S(2)}, u32[]{:S(2)}) collective-permute-start(bf16[43,16,128]{2,1,0:T(8,128)(2,1)S(1)} %group.1.own_ref), channel_id=1, source_target_pairs={{0,4},{4,0},{8,12},{12,8},{16,20},{20,16},{24,28},{28,24},{1,5},{5... | collective-permute-start | bytes 528392 | tf_op jit(solution)/shard_map/ppermute | solution.py:30
  13.2 11.6 %collective-permute-start.4 = (bf16[43,16,128]{2,1,0:T(8,128)(2,1)S(1)}, bf16[43,16,128]{2,1,0:T(8,128)(2,1)S(1)}, u32[]{:S(2)}, u32[]{:S(2)}) collective-permute-start(bf16[43,16,128]{2,1,0:T(8,128)(2,1)S(1)} %group.1.own_ref), channel_id=1, source_target_pairs={{4,8},{8,4},{12,16},{16,12},{20,24},{24,20},{5,9},{9,5},{13,17},{1... | collective-permute-start | bytes 528392 | tf_op jit(solution)/shard_map/ppermute | solution.py:30
where the time goes:
time: 32.3 us; the launch traced here: 32.1 us
  Pallas kernels  23.2 us (72%)
  starting transfers between devices  8.82 us (27%)
    ppermute x5, starting transfers between devices, swapped(): lax.ppermute(x, axis, [way for i, j in pairs for way in ((i, j), (j, i))])  8.82 us
    pallas_call x1, Pallas kernels, per_device(): pl.pallas_call(functools.partial(near_kernel, entries), out_shape=shaped(...  8.59 us
    pallas_call x1, Pallas kernels, per_device(): pl.pallas_call(functools.partial(incoming_kernel, entries), out_shape=sha...  7.22 us
    pallas_call x1, Pallas kernels, per_device(): pl.pallas_call(prepare_kernel, out_shape=(shaped((boxes, waves, width), F...  6.03 us
    pallas_call x1, Pallas kernels, per_device(): pl.pallas_call(outgoing_kernel, out_shape=(shaped((own_rows + spectra_row...  1.31 us
  transfers between devices with their start and end apart: 5, of which 0 were waited for; matrix products, arithmetic and copies ran while one was open for 0% of the time, Pallas kernels for 46%

commit v1 on v0

--- a/solution.py
+++ b/solution.py
@@ -14,12 +14,12 @@
 WAVENUMBER = 4.0
 OFFSET = 0.5
 TURN = WAVENUMBER / (2.0 * math.pi)
-S0, S1, S2 = (-0.08849679958812066, 0.5822236432316782, -1.1456733260321648)
-LEAD = -70.99877392901621
+CHAIN = (-2.2803148655023415, -1.415255674611144, -7.327656729815578, -24.467745134801202)
+LEAD = 0.04087004462557604
 ITEMS = 4
 ROWS = 32
 STAGES = 4
-FIRST_ITEMS = 2
+FIRST_ITEMS = 5
 
 
 def round_up(value, step):
@@ -51,7 +51,7 @@
 
 def list_places(boxes, entries):
     gap = 2 * ITEMS
-    most = FIRST_ITEMS * boxes
+    most = FIRST_ITEMS * boxes // 2
     return most, most + gap, round_up(most + gap + boxes * entries // 2 + 2 * gap + 6, 128)
 
 
@@ -277,9 +277,9 @@
             v = jnp.maximum(u_ref[g, at : at + ROWS], 1e-12)
             q = v * lax.rsqrt(v)
             t = q - jnp.round(q)
-            x = 0.25 - jnp.abs(t)
-            z = x * x
-            cosine = x * (((z + S2) * z + S1) * z + S0)
+            cosine = t * t + CHAIN[0]
+            for constant in CHAIN[1:]:
+                cosine = cosine * cosine + constant
             t_ref[g, at : at + ROWS] = (cosine * pltpu.reciprocal(q + OFFSET * TURN, approx=True)).astype(BF16)
 
     def product(chunk, g, t_ref):
@@ -321,7 +321,7 @@
 
 def prepare_kernel(
     own_ref, near_hbm, src_hbm, id_hbm, count_hbm, table_hbm, out_ref, items_ref, obs_ref, src_ref, gain_ref, near_ref,
-    trans_src_ref, trans_id_ref, trans_count_ref, rows_ref, list_ref, win_ref, u0_ref, u1_ref, t0_ref, t1_ref, sems
+    trans_src_ref, trans_id_ref, trans_count_ref, table_ref, list_ref, win_ref, u0_ref, u1_ref, t0_ref, t1_ref, sems
 ):
     boxes = obs_ref.shape[0]
     entries = near_ref.shape[1]
@@ -334,9 +334,11 @@
             (src_hbm, trans_src_ref),
             (id_hbm, trans_id_ref),
             (count_hbm, trans_count_ref),
+            (table_hbm, table_ref),
         ),
         sems,
     )
+    table_copy = list_copies.pop()
     gain_ref[...] = jnp.zeros(gain_ref.shape, F32)
     plane_rows = 3 * boxes // 16
     source, observer = features(own_ref[boxes // 2 : boxes // 2 + plane_rows])
@@ -345,24 +347,19 @@
     obs_ref[...] = observer
     wait_all(list_copies)
     row0 = lax.axis_index("dir") * parents
-    for q in range(parents):
-        for e in range(listed):
-            pltpu.make_async_copy(
-                table_hbm.at[trans_id_ref[row0 + q, e]], rows_ref.at[q * listed + e], sems.at[1]
-            ).start()
     near_copy.wait()
     block = lax.axis_index(("box", "dir"))
     items_ref[...] = list_items(near_ref[...], block, lax.axis_index("dir"), lax.axis_size("dir"))
     fetch = pltpu.make_async_copy(items_ref, list_ref, sems.at[0])
     fetch.start()
     out_ref[...] = jnp.zeros(out_ref.shape, F32)
-    pltpu.make_async_copy(rows_ref, rows_ref, sems.at[1]).wait()
+    table_copy.wait()
     first = (lax.axis_index("box") - 1) * (window // 3)
     for q in range(parents):
         for e in range(listed):
             live = (e < trans_count_ref[row0 + q]).astype(F32)
             s = jnp.clip(trans_src_ref[row0 + q, e] - first, 0, window - 1)
-            gain_ref[q, s] += rows_ref[q * listed + e] * live
+            gain_ref[q, s] += table_ref[trans_id_ref[row0 + q, e]] * live
     fetch.wait()
     near_sum(
         entries,
@@ -378,10 +375,9 @@
 
 
 def near_kernel(entries, items_ref, own_ref, *refs):
-    *step_refs, obs_ref, own_src_ref, first_ref, out_ref, win_ref, src_ref, list_ref, u0_ref, u1_ref, t0_ref, t1_ref, sem = refs
+    *step_refs, obs_ref, own_src_ref, first_ref, out_ref, win_ref, src_ref, list_ref, u0_ref, u1_ref, t0_ref, t1_ref, sems = refs
     boxes, waves, width = out_ref.shape
-    fetch = pltpu.make_async_copy(items_ref, list_ref, sem)
-    fetch.start()
+    fetches = start_all(((items_ref, list_ref), (own_src_ref, src_ref.at[:, :boxes])), sems)
     length = list_ref.shape[1]
     here = lax.axis_index("dir")
     other_side = jnp.where((here & 1) == 0, here - 1, here + 1)
@@ -393,13 +389,12 @@
         turn_sources(source, src_ref, part * boxes)
 
     take_currents(own_ref[:x_rows], win_ref, 0)
-    src_ref[:, :boxes] = own_src_ref[...]
     take(step_refs[0], 1)
     for k, ref in enumerate(step_refs[1:], 2):
         pl.when((here ^ ((1 << k) - 1)) == other_side)(functools.partial(take, ref, 2))
     second_start = list_places(boxes, entries)[1]
     out_ref[...] = first_ref[...]
-    fetch.wait()
+    wait_all(fetches)
     near_sum(
         entries,
         list_ref[0, length - 2],
@@ -428,12 +423,17 @@
     sum_ref[...] = near_ref[...]
     x_rows = boxes // 2
     packet_rows = x_rows + 3 * boxes // 16
-    from_even = jnp.where(lax.axis_index("dir") == 0, 1, 0) == odd_box
-    even_packet, odd_packet = (ref[ref.shape[0] - packet_rows :] for ref in (even_ref, odd_ref))
-    packet = jnp.where(from_even, even_packet.astype(F32), odd_packet.astype(F32)).astype(BF16)
-    take_currents(packet[:x_rows], win_ref, 0)
-    source, _ = features(packet[x_rows:])
-    turn_sources(source, src_ref, 0)
+    here = lax.axis_index("dir")
+
+    @pl.when((here == 0) | (here == lax.axis_size("dir") - 1))
+    def _():
+        from_even = jnp.where(here == 0, 1, 0) == odd_box
+        even_packet, odd_packet = (ref[ref.shape[0] - packet_rows :] for ref in (even_ref, odd_ref))
+        packet = jnp.where(from_even, even_packet.astype(F32), odd_packet.astype(F32)).astype(BF16)
+        take_currents(packet[:x_rows], win_ref, 0)
+        source, _ = features(packet[x_rows:])
+        turn_sources(source, src_ref, 0)
+
     fetch.wait()
     cos_phase = cos_ref[...]
     sin_phase = sin_ref[...]
@@ -557,12 +557,12 @@
             pltpu.SMEM(trans_src.shape, jnp.int32),
             pltpu.SMEM(trans_id.shape, jnp.int32),
             pltpu.SMEM(trans_count.shape, jnp.int32),
-            pltpu.VMEM((parents * trans_src.shape[1], 2, parent_dirs), F32),
+            pltpu.VMEM(trans_table.shape, F32),
             pltpu.SMEM((1, length), jnp.int32),
             pltpu.VMEM((boxes, 16, width), BF16),
         ]
         + near_scratch
-        + [pltpu.SemaphoreType.DMA((4,))],
+        + [pltpu.SemaphoreType.DMA((5,))],
         compiler_params=params,
         name="prepare",
     )(packet, *[in_hbm(x) for x in (near_src, trans_src, trans_id, trans_count, trans_table)])
@@ -591,7 +591,7 @@
             pltpu.SMEM((1, length), jnp.int32),
         ]
         + near_scratch
-        + [pltpu.SemaphoreType.DMA],
+        + [pltpu.SemaphoreType.DMA((2,))],
         compiler_params=params,
         name="near",
     )(items, packet, *packets, observers, sources, first_sum)

time: 32.3 us -> 31.4 us (0.972)
  Pallas kernels: 23.2 us -> 22.1 us
    pallas_call x1, Pallas kernels: 8.59 us -> 7.21 us  [per_device(): pl.pallas_call(functools.partial(near_kernel, entries), out_shape=shaped(...]
    pallas_call x1, Pallas kernels: 6.03 us -> 6.56 us  [per_device(): pl.pallas_call(prepare_kernel, out_shape=(shaped((boxes, waves, width), F...]
  transfers between devices with their start and end apart: 5 -> 5, of which waited for: 0 -> 0; matrix products, arithmetic and copies ran while one was open for 0% -> 0% of each run, Pallas kernels for 46% -> 44%
where the time goes in v1:
time: 31.4 us; the launch traced here: 31 us
  Pallas kernels  22.1 us (70%)
  starting transfers between devices  8.82 us (28%)
    ppermute x5, starting transfers between devices, swapped(): lax.ppermute(x, axis, [way for i, j in pairs for way in ((i, j), (j, i))])  8.82 us
    pallas_call x1, Pallas kernels, per_device(): pl.pallas_call(functools.partial(near_kernel, entries), out_shape=shaped(...  7.21 us
    pallas_call x1, Pallas kernels, per_device(): pl.pallas_call(functools.partial(incoming_kernel, entries), out_shape=sha...  6.99 us
    pallas_call x1, Pallas kernels, per_device(): pl.pallas_call(prepare_kernel, out_shape=(shaped((boxes, waves, width), F...  6.56 us
    pallas_call x1, Pallas kernels, per_device(): pl.pallas_call(outgoing_kernel, out_shape=(shaped((own_rows + spectra_row...  1.31 us
  transfers between devices with their start and end apart: 5, of which 0 were waited for; matrix products, arithmetic and copies ran while one was open for 0% of the time, Pallas kernels for 44%

profile of v1, /device:TPU:1, one launch (start us, length us, event | category | flops | bytes accessed | tf_op | source)
XLA Modules:
  0.0 31.0 jit_solution(12466478199880556076)
XLA Ops:
  0.0 1.3 %outgoing.1 = (bf16[19,16,128]{2,1,0:T(8,128)(2,1)S(1)}, bf16[8,16,128]{2,1,0:T(8,128)(2,1)S(1)}, bf16[128,512]{1,0:T(8,128)(2,1)S(1)}, f32[8,512]{1,0:T(8,128)S...) custom-call(bf16[8,16,128]{2,1,0:T(8,128)(2,1)} %bitcast.4, bf16[3,16,128]{2,1,0:T(8,128)(2,1)} %bitcast.5, ...), custom_call_target="tpu_custom_call" | custom-call | tf_op jit(solution)/shard_map/outgoing/pallas_call | solution.py:513
  1.3 2.2 %collective-permute-start = (bf16[19,16,128]{2,1,0:T(8,128)(2,1)S(1)}, bf16[19,16,128]{2,1,0:T(8,128)(2,1)S(1)}, u32[]{:S(2)}, u32[]{:S(2)}) collective-permute-start(bf16[19,16,128]{2,1,0:T(8,128)(2,1)S(1)} %get-tuple-element.16.own_ref), channel_id=1, source_target_pairs={{0,1},{1,0},{2,3},{3,2},{4,5},{5,4},{6,7},{7,6},{8,9},{9,8},{10,11... | collective-permute-start | bytes 233480 | tf_op jit(solution)/shard_map/ppermute | solution.py:30
  3.5 2.2 %collective-permute-start.2 = (bf16[19,16,128]{2,1,0:T(8,128)(2,1)S(1)}, bf16[19,16,128]{2,1,0:T(8,128)(2,1)S(1)}, u32[]{:S(2)}, u32[]{:S(2)}) collective-permute-start(bf16[19,16,128]{2,1,0:T(8,128)(2,1)S(1)} %get-tuple-element.16.own_ref), channel_id=1, source_target_pairs={{0,3},{3,0},{1,2},{2,1},{4,7},{7,4},{5,6},{6,5},{8,11},{11,8},{9,1... | collective-permute-start | bytes 233480 | tf_op jit(solution)/shard_map/ppermute | solution.py:30
  5.7 0.1 collective-permute-start.1
  5.8 6.6 %prepare.1 = (f32[16,8,128]{2,1,0:T(8,128)S(1)}, s32[1,384]{1,0:T(1,128)S(1)}, bf16[16,16,128]{2,1,0:T(8,128)(2,1)S(1)}, bf16[2,16,128,128]{3,2,1,0:T(8,128)(2,1)S(1)}, f32[2,24,2,512]{3,2,1,0:T(2,128)S(1)}) custom-call(bf16[19,16,128]{2,1,0:T(8,128)(2,1)S(1)} %get-tuple-element.16.own_ref, s32[16,27]{1,0:T(8,128)} %near_hbm.1, s32[8,32]{1,0:T(8,128)} %src_hbm.1, ...), custom_call_target="tpu_custom_call" | custom-call | tf_op jit(solution)/shard_map/prepare/pallas_call | solution.py:544
  12.4 0.0 collective-permute-done.1.refs_1_
  12.4 0.0 collective-permute-done.refs_0_
  12.4 0.0 collective-permute-done.2.refs_2_.refs_1_
  12.5 1.3 %collective-permute-start.3 = (bf16[43,16,128]{2,1,0:T(8,128)(2,1)S(1)}, bf16[43,16,128]{2,1,0:T(8,128)(2,1)S(1)}, u32[]{:S(2)}, u32[]{:S(2)}) collective-permute-start(bf16[43,16,128]{2,1,0:T(8,128)(2,1)S(1)} %group.1.own_ref), channel_id=1, source_target_pairs={{0,4},{4,0},{8,12},{12,8},{16,20},{20,16},{24,28},{28,24},{1,5},{5... | collective-permute-start | bytes 528392 | tf_op jit(solution)/shard_map/ppermute | solution.py:30
  13.8 3.0 %collective-permute-start.4 = (bf16[43,16,128]{2,1,0:T(8,128)(2,1)S(1)}, bf16[43,16,128]{2,1,0:T(8,128)(2,1)S(1)}, u32[]{:S(2)}, u32[]{:S(2)}) collective-permute-start(bf16[43,16,128]{2,1,0:T(8,128)(2,1)S(1)} %group.1.own_ref), channel_id=1, source_target_pairs={{4,8},{8,4},{12,16},{16,12},{20,24},{24,20},{5,9},{9,5},{13,17},{1... | collective-permute-start | bytes 528392 | tf_op jit(solution)/shard_map/ppermute | solution.py:30
  16.8 7.2 %near.1.near_ref = f32[16,8,128]{2,1,0:T(8,128)S(1)} custom-call(s32[1,384]{1,0:T(1,128)S(1)} %get-tuple-element.17.refs_3_.items_ref, bf16[19,16,128]{2,1,0:T(8,128)(2,1)S(1)} %get-tuple-element.16.own_ref, bf16[19,16,128]{2,1,0:T(8,128)(2,1)S(1)} %collective-permute-done.refs_0_, bf16[19,16,128]{2,1,0:T(8,128)(2,1)S(1)} %collective-permute-done.2.refs_2_.refs_1_, ...), custom_call_target="tpu_custom_call" | custom-call | tf_op jit(solution)/shard_map/near/pallas_call | solution.py:583
  24.0 0.0 collective-permute-done.3.even_ref
  24.0 0.0 collective-permute-done.4.odd_ref
  24.0 7.0 %incoming.1 = f32[16,8,128]{2,1,0:T(8,128)} custom-call(s32[1,384]{1,0:T(1,128)S(1)} %get-tuple-element.17.refs_3_.items_ref, bf16[43,16,128]{2,1,0:T(8,128)(2,1)S(1)} %collective-permute-done.3.even_ref, bf16[43,16,128]{2,1,0:T(8,128)(2,1)S(1)} %group.1.own_ref, bf16[43,16,128]{2,1,0:T(8,128)(2,1)S(1)} %collective-permute-done.4.odd_ref, ...), custom_call_target="tpu_custom_call" | custom-call | tf_op jit(solution)/shard_map/incoming/pallas_call | solution.py:599
  (1 shorter events, 0.0 us)
Async XLA Ops:
  1.3 11.1 %collective-permute-start = (bf16[19,16,128]{2,1,0:T(8,128)(2,1)S(1)}, bf16[19,16,128]{2,1,0:T(8,128)(2,1)S(1)}, u32[]{:S(2)}, u32[]{:S(2)}) collective-permute-start(bf16[19,16,128]{2,1,0:T(8,128)(2,1)S(1)} %get-tuple-element.16.own_ref), channel_id=1, source_target_pairs={{0,1},{1,0},{2,3},{3,2},{4,5},{5,4},{6,7},{7,6},{8,9},{9,8},{10,11... | collective-permute-start | bytes 233480 | tf_op jit(solution)/shard_map/ppermute | solution.py:30
  3.5 8.9 %collective-permute-start.2 = (bf16[19,16,128]{2,1,0:T(8,128)(2,1)S(1)}, bf16[19,16,128]{2,1,0:T(8,128)(2,1)S(1)}, u32[]{:S(2)}, u32[]{:S(2)}) collective-permute-start(bf16[19,16,128]{2,1,0:T(8,128)(2,1)S(1)} %get-tuple-element.16.own_ref), channel_id=1, source_target_pairs={{0,3},{3,0},{1,2},{2,1},{4,7},{7,4},{5,6},{6,5},{8,11},{11,8},{9,1... | collective-permute-start | bytes 233480 | tf_op jit(solution)/shard_map/ppermute | solution.py:30
  5.7 6.7 %collective-permute-start.1 = (bf16[8,16,128]{2,1,0:T(8,128)(2,1)S(1)}, bf16[8,16,128]{2,1,0:T(8,128)(2,1)S(1)}, u32[]{:S(2)}, u32[]{:S(2)}) collective-permute-start(bf16[8,16,128]{2,1,0:T(8,128)(2,1)S(1)} %get-tuple-element.18.own_ref), channel_id=1, source_target_pairs={{0,2},{2,0},{1,3},{3,1},{4,6},{6,4},{5,7},{7,5},{8,10},{10,8},{9,1... | collective-permute-start | bytes 98312 | tf_op jit(solution)/shard_map/ppermute | solution.py:30
  12.5 11.5 %collective-permute-start.3 = (bf16[43,16,128]{2,1,0:T(8,128)(2,1)S(1)}, bf16[43,16,128]{2,1,0:T(8,128)(2,1)S(1)}, u32[]{:S(2)}, u32[]{:S(2)}) collective-permute-start(bf16[43,16,128]{2,1,0:T(8,128)(2,1)S(1)} %group.1.own_ref), channel_id=1, source_target_pairs={{0,4},{4,0},{8,12},{12,8},{16,20},{20,16},{24,28},{28,24},{1,5},{5... | collective-permute-start | bytes 528392 | tf_op jit(solution)/shard_map/ppermute | solution.py:30
  13.8 10.3 %collective-permute-start.4 = (bf16[43,16,128]{2,1,0:T(8,128)(2,1)S(1)}, bf16[43,16,128]{2,1,0:T(8,128)(2,1)S(1)}, u32[]{:S(2)}, u32[]{:S(2)}) collective-permute-start(bf16[43,16,128]{2,1,0:T(8,128)(2,1)S(1)} %group.1.own_ref), channel_id=1, source_target_pairs={{4,8},{8,4},{12,16},{16,12},{20,24},{24,20},{5,9},{9,5},{13,17},{1... | collective-permute-start | bytes 528392 | tf_op jit(solution)/shard_map/ppermute | solution.py:30

commit v2 on v1

--- a/solution.py
+++ b/solution.py
@@ -131,8 +131,8 @@
 
 
 def outgoing_kernel(
-    x_hbm, pos_hbm, rad_hbm, idx_hbm, wgt_hbm, phase_hbm, packet_ref, spectra_ref, imat_ref, cos_ref, sin_ref, rad_ref,
-    x_ref, pos_ref, idx_ref, wgt_ref, phase_ref, sems
+    x_hbm, pos_hbm, rad_hbm, idx_hbm, wgt_hbm, phase_hbm, near_hbm, packet_ref, spectra_ref, imat_ref, cos_ref, sin_ref,
+    rad_ref, items_ref, x_ref, pos_ref, idx_ref, wgt_ref, phase_ref, near_ref, sems
 ):
     wait_all(
         start_all(
@@ -143,10 +143,13 @@
                 (idx_hbm, idx_ref),
                 (wgt_hbm, wgt_ref),
                 (phase_hbm, phase_ref),
+                (near_hbm, near_ref),
             ),
             sems,
         )
     )
+    block = lax.axis_index(("box", "dir"))
+    items_ref[...] = list_items(near_ref[...], block, lax.axis_index("dir"), lax.axis_size("dir"))
     leaf_dirs, parent_dirs = imat_ref.shape
     x_rows, _, width = x_ref.shape
     axes, boxes, _ = pos_ref.shape
@@ -315,22 +318,21 @@
     lax.fori_loop(0, rounds, body, 0)
     for j in range(STAGES - 1):
         pl.when(rounds * STAGES + j < chunks)(functools.partial(stage, rounds * STAGES + j, j & 1))
-    pl.when((chunks & 1) == 0)(functools.partial(finish, 1))
+    pl.when((chunks > 0) & ((chunks & 1) == 0))(functools.partial(finish, 1))
     pl.when((chunks & 1) == 1)(functools.partial(finish, 0))
 
 
 def prepare_kernel(
-    own_ref, near_hbm, src_hbm, id_hbm, count_hbm, table_hbm, out_ref, items_ref, obs_ref, src_ref, gain_ref, near_ref,
-    trans_src_ref, trans_id_ref, trans_count_ref, table_ref, list_ref, win_ref, u0_ref, u1_ref, t0_ref, t1_ref, sems
+    entries, own_ref, items_ref, src_hbm, id_hbm, count_hbm, table_hbm, out_ref, obs_ref, src_ref, gain_ref, trans_src_ref,
+    trans_id_ref, trans_count_ref, table_ref, list_ref, win_ref, u0_ref, u1_ref, t0_ref, t1_ref, sems
 ):
     boxes = obs_ref.shape[0]
-    entries = near_ref.shape[1]
     length = list_ref.shape[1]
     parents, window = gain_ref.shape[:2]
     listed = src_hbm.shape[1]
-    near_copy, *list_copies = start_all(
+    fetch, *trans_copies = start_all(
         (
-            (near_hbm, near_ref),
+            (items_ref, list_ref),
             (src_hbm, trans_src_ref),
             (id_hbm, trans_id_ref),
             (count_hbm, trans_count_ref),
@@ -338,28 +340,13 @@
         ),
         sems,
     )
-    table_copy = list_copies.pop()
-    gain_ref[...] = jnp.zeros(gain_ref.shape, F32)
     plane_rows = 3 * boxes // 16
     source, observer = features(own_ref[boxes // 2 : boxes // 2 + plane_rows])
     turn_sources(source, src_ref, 0)
     take_currents(own_ref[: boxes // 2], win_ref, 0)
     obs_ref[...] = observer
-    wait_all(list_copies)
-    row0 = lax.axis_index("dir") * parents
-    near_copy.wait()
-    block = lax.axis_index(("box", "dir"))
-    items_ref[...] = list_items(near_ref[...], block, lax.axis_index("dir"), lax.axis_size("dir"))
-    fetch = pltpu.make_async_copy(items_ref, list_ref, sems.at[0])
-    fetch.start()
     out_ref[...] = jnp.zeros(out_ref.shape, F32)
-    table_copy.wait()
-    first = (lax.axis_index("box") - 1) * (window // 3)
-    for q in range(parents):
-        for e in range(listed):
-            live = (e < trans_count_ref[row0 + q]).astype(F32)
-            s = jnp.clip(trans_src_ref[row0 + q, e] - first, 0, window - 1)
-            gain_ref[q, s] += table_ref[trans_id_ref[row0 + q, e]] * live
+    gain_ref[...] = jnp.zeros(gain_ref.shape, F32)
     fetch.wait()
     near_sum(
         entries,
@@ -372,6 +359,14 @@
         out_ref,
         (u0_ref, u1_ref, t0_ref, t1_ref),
     )
+    wait_all(trans_copies)
+    row0 = lax.axis_index("dir") * parents
+    first = (lax.axis_index("box") - 1) * (window // 3)
+    for q in range(parents):
+        for e in range(listed):
+            live = (e < trans_count_ref[row0 + q]).astype(F32)
+            s = jnp.clip(trans_src_ref[row0 + q, e] - first, 0, window - 1)
+            gain_ref[q, s] += table_ref[trans_id_ref[row0 + q, e]] * live
 
 
 def near_kernel(entries, items_ref, own_ref, *refs):
@@ -510,7 +505,9 @@
     x_rows = boxes // 2
     own_rows = x_rows + 3 * boxes // 16
     operands = (currents.reshape(x_rows, 2 * waves, width), positions.transpose(1, 0, 2), radiation, interp_index.T, interp_weight.T, child_phase)
-    packet, spectra, imat, cos_phase, sin_phase, rad = pl.pallas_call(
+    operands = operands + (near_src,)
+    length = list_places(boxes, entries)[2]
+    packet, spectra, imat, cos_phase, sin_phase, rad, items = pl.pallas_call(
         outgoing_kernel,
         out_shape=(
             shaped((own_rows + spectra_rows, 16, width), BF16),
@@ -519,9 +516,10 @@
             shaped((8, parent_dirs), F32),
             shaped((8, parent_dirs), F32),
             shaped(radiation.shape, BF16),
+            shaped((1, length), jnp.int32),
         ),
         in_specs=[hbm] * len(operands),
-        out_specs=(vmem,) * 6,
+        out_specs=(vmem,) * 7,
         scratch_shapes=[pltpu.VMEM(x.shape, x.dtype) for x in operands if x is not radiation]
         + [pltpu.SemaphoreType.DMA((len(operands),))],
         compiler_params=params,
@@ -533,7 +531,6 @@
         pairs = [(i, i ^ step) for i in range(size) if i < i ^ step]
         steps.append(swapped(packet if carries_packet(step) else spectra, "dir", pairs))
 
-    length = list_places(boxes, entries)[2]
     window = 3 * trans_src.shape[0]
     near_scratch = [
         pltpu.VMEM((ITEMS, width, 2 * width), F32),
@@ -541,19 +538,17 @@
         pltpu.VMEM((ITEMS, width, 2 * width), BF16),
         pltpu.VMEM((ITEMS, width, 2 * width), BF16),
     ]
-    first_sum, items, observers, sources, gains = pl.pallas_call(
-        prepare_kernel,
+    first_sum, observers, sources, gains = pl.pallas_call(
+        functools.partial(prepare_kernel, entries),
         out_shape=(
             shaped((boxes, waves, width), F32),
-            shaped((1, length), jnp.int32),
             shaped((boxes, 16, width), BF16),
             shaped((2, boxes, width, 128), BF16),
             shaped((parents, window, 2, parent_dirs), F32),
         ),
-        in_specs=[vmem] + [hbm] * 5,
-        out_specs=(vmem,) * 5,
+        in_specs=[vmem] * 2 + [hbm] * 4,
+        out_specs=(vmem,) * 4,
         scratch_shapes=[
-            pltpu.VMEM(near_src.shape, jnp.int32),
             pltpu.SMEM(trans_src.shape, jnp.int32),
             pltpu.SMEM(trans_id.shape, jnp.int32),
             pltpu.SMEM(trans_count.shape, jnp.int32),
@@ -565,7 +560,7 @@
         + [pltpu.SemaphoreType.DMA((5,))],
         compiler_params=params,
         name="prepare",
-    )(packet, *[in_hbm(x) for x in (near_src, trans_src, trans_id, trans_count, trans_table)])
+    )(packet, items, *[in_hbm(x) for x in (trans_src, trans_id, trans_count, trans_table)])
 
     group = pl.pallas_call(
         group_kernel,
@@ -574,7 +569,7 @@
         out_specs=vmem,
         compiler_params=params,
         name="group",
-    )(spectra, *steps, items)
+    )(spectra, *steps, first_sum)
     groups = lax.axis_size("box")
     group_odd = swapped(group, "box", [(i, i + 1) for i in range(1, groups - 1, 2)])
     group_even = swapped(group, "box", [(i, i + 1) for i in range(0, groups - 1, 2)])

time: 31.4 us -> 31 us (0.987)
  waiting for transfers between devices: 0.01 us -> 0.61 us
  starting transfers between devices: 8.82 us -> 8.25 us
    pallas_call x1, Pallas kernels: 6.56 us -> 5.28 us  [per_device(): pl.pallas_call(functools.partial(prepare_kernel, entries), out_shape=(sha...]
    ppermute x5, waiting for transfers between devices: 0.01 us -> 0.61 us  [swapped(): lax.ppermute(x, axis, [way for i, j in pairs for way in ((i, j), (j, i))])]
    ppermute x5, starting transfers between devices: 8.82 us -> 8.25 us  [swapped(): lax.ppermute(x, axis, [way for i, j in pairs for way in ((i, j), (j, i))])]
    pallas_call x1, Pallas kernels: 7.21 us -> 7.78 us  [per_device(): pl.pallas_call(functools.partial(near_kernel, entries), out_shape=shaped(...]
    pallas_call x1, Pallas kernels: 1.31 us -> 1.79 us  [per_device(): pl.pallas_call(outgoing_kernel, out_shape=(shaped((own_rows + spectra_row...]
  transfers between devices with their start and end apart: 5 -> 5, of which waited for: 0 -> 1; matrix products, arithmetic and copies ran while one was open for 0% -> 0% of each run, Pallas kernels for 44% -> 42%
where the time goes in v2:
time: 31 us; the launch traced here: 30.8 us
  Pallas kernels  21.8 us (70%)
  starting transfers between devices  8.25 us (27%)
  waiting for transfers between devices  0.61 us (2%)
    ppermute x5, starting transfers between devices, swapped(): lax.ppermute(x, axis, [way for i, j in pairs for way in ((i, j), (j, i))])  8.25 us
    pallas_call x1, Pallas kernels, per_device(): pl.pallas_call(functools.partial(near_kernel, entries), out_shape=shaped(...  7.78 us
    pallas_call x1, Pallas kernels, per_device(): pl.pallas_call(functools.partial(incoming_kernel, entries), out_shape=sha...  6.98 us
    pallas_call x1, Pallas kernels, per_device(): pl.pallas_call(functools.partial(prepare_kernel, entries), out_shape=(sha...  5.28 us
    pallas_call x1, Pallas kernels, per_device(): pl.pallas_call(outgoing_kernel, out_shape=(shaped((own_rows + spectra_row...  1.79 us
  transfers between devices with their start and end apart: 5, of which 1 were waited for; matrix products, arithmetic and copies ran while one was open for 0% of the time, Pallas kernels for 42%

profile of v2, /device:TPU:1, one launch (start us, length us, event | category | flops | bytes accessed | tf_op | source)
XLA Modules:
  0.0 30.8 jit_solution(5883968003378618507)
XLA Ops:
  0.0 1.8 %outgoing.1 = (bf16[19,16,128]{2,1,0:T(8,128)(2,1)S(1)}, bf16[8,16,128]{2,1,0:T(8,128)(2,1)S(1)}, bf16[128,512]{1,0:T(8,128)(2,1)S(1)}, f32[8,512]{1,0:T(8,128)S...) custom-call(bf16[8,16,128]{2,1,0:T(8,128)(2,1)} %bitcast.4, ...), custom_call_target="tpu_custom_call" | custom-call | tf_op jit(solution)/shard_map/outgoing/pallas_call | solution.py:510
  1.8 2.2 %collective-permute-start = (bf16[19,16,128]{2,1,0:T(8,128)(2,1)S(1)}, bf16[19,16,128]{2,1,0:T(8,128)(2,1)S(1)}, u32[]{:S(2)}, u32[]{:S(2)}) collective-permute-start(bf16[19,16,128]{2,1,0:T(8,128)(2,1)S(1)} %get-tuple-element.18.own_ref), channel_id=1, source_target_pairs={{0,1},{1,0},{2,3},{3,2},{4,5},{5,4},{6,7},{7,6},{8,9},{9,8},{10,11... | collective-permute-start | bytes 233480 | tf_op jit(solution)/shard_map/ppermute | solution.py:30
  4.0 2.2 %collective-permute-start.2 = (bf16[19,16,128]{2,1,0:T(8,128)(2,1)S(1)}, bf16[19,16,128]{2,1,0:T(8,128)(2,1)S(1)}, u32[]{:S(2)}, u32[]{:S(2)}) collective-permute-start(bf16[19,16,128]{2,1,0:T(8,128)(2,1)S(1)} %get-tuple-element.18.own_ref), channel_id=1, source_target_pairs={{0,3},{3,0},{1,2},{2,1},{4,7},{7,4},{5,6},{6,5},{8,11},{11,8},{9,1... | collective-permute-start | bytes 233480 | tf_op jit(solution)/shard_map/ppermute | solution.py:30
  6.2 0.1 collective-permute-start.1
  6.3 5.3 %prepare.1 = (f32[16,8,128]{2,1,0:T(8,128)S(1)}, bf16[16,16,128]{2,1,0:T(8,128)(2,1)S(1)}, bf16[2,16,128,128]{3,2,1,0:T(8,128)(2,1)S(1)}, f32[2,24,2,512]{3,2,1,0:T(2,128)S(1)}) custom-call(bf16[19,16,128]{2,1,0:T(8,128)(2,1)S(1)} %get-tuple-element.18.own_ref, s32[1,384]{1,0:T(1,128)S(1)} %get-tuple-element.16.items_ref, s32[8,32]{1,0:T(8,128)} %src_hbm.1, ...), custom_call_target="tpu_custom_call" | custom-call | tf_op jit(solution)/shard_map/prepare/pallas_call | solution.py:541
  11.6 0.6 %collective-permute-done.1.refs_1_ = bf16[8,16,128]{2,1,0:T(8,128)(2,1)S(1)} collective-permute-done((bf16[8,16,128]{2,1,0:T(8,128)(2,1)S(1)}, bf16[8,16,128]{2,1,0:T(8,128)(2,1)S(1)}, u32[]{:S(2)}, u32[]{:S(2)}) %collective-permute-start.1) | collective-permute-done | bytes 32800 | tf_op jit(solution)/shard_map/ppermute | solution.py:30
  12.2 0.0 collective-permute-done.refs_0_
  12.2 0.0 collective-permute-done.2.refs_2_.refs_1_
  12.2 0.7 %collective-permute-start.3 = (bf16[43,16,128]{2,1,0:T(8,128)(2,1)S(1)}, bf16[43,16,128]{2,1,0:T(8,128)(2,1)S(1)}, u32[]{:S(2)}, u32[]{:S(2)}) collective-permute-start(bf16[43,16,128]{2,1,0:T(8,128)(2,1)S(1)} %group.1.own_ref), channel_id=1, source_target_pairs={{0,4},{4,0},{8,12},{12,8},{16,20},{20,16},{24,28},{28,24},{1,5},{5... | collective-permute-start | bytes 528392 | tf_op jit(solution)/shard_map/ppermute | solution.py:30
  13.0 3.0 %collective-permute-start.4 = (bf16[43,16,128]{2,1,0:T(8,128)(2,1)S(1)}, bf16[43,16,128]{2,1,0:T(8,128)(2,1)S(1)}, u32[]{:S(2)}, u32[]{:S(2)}) collective-permute-start(bf16[43,16,128]{2,1,0:T(8,128)(2,1)S(1)} %group.1.own_ref), channel_id=1, source_target_pairs={{4,8},{8,4},{12,16},{16,12},{20,24},{24,20},{5,9},{9,5},{13,17},{1... | collective-permute-start | bytes 528392 | tf_op jit(solution)/shard_map/ppermute | solution.py:30
  16.0 7.8 %near.1.near_ref = f32[16,8,128]{2,1,0:T(8,128)S(1)} custom-call(s32[1,384]{1,0:T(1,128)S(1)} %get-tuple-element.16.items_ref, bf16[19,16,128]{2,1,0:T(8,128)(2,1)S(1)} %get-tuple-element.18.own_ref, bf16[19,16,128]{2,1,0:T(8,128)(2,1)S(1)} %collective-permute-done.refs_0_, bf16[19,16,128]{2,1,0:T(8,128)(2,1)S(1)} %collective-permute-done.2.refs_2_.refs_1_, ...), custom_call_target="tpu_custom_call" | custom-call | tf_op jit(solution)/shard_map/near/pallas_call | solution.py:578
  23.8 0.0 collective-permute-done.3.even_ref
  23.8 0.0 collective-permute-done.4.odd_ref
  23.8 7.0 %incoming.1 = f32[16,8,128]{2,1,0:T(8,128)} custom-call(s32[1,384]{1,0:T(1,128)S(1)} %get-tuple-element.16.items_ref, bf16[43,16,128]{2,1,0:T(8,128)(2,1)S(1)} %collective-permute-done.3.even_ref, bf16[43,16,128]{2,1,0:T(8,128)(2,1)S(1)} %group.1.own_ref, bf16[43,16,128]{2,1,0:T(8,128)(2,1)S(1)} %collective-permute-done.4.odd_ref, ...), custom_call_target="tpu_custom_call" | custom-call | tf_op jit(solution)/shard_map/incoming/pallas_call | solution.py:594
  (1 shorter events, 0.0 us)
Async XLA Ops:
  1.8 10.4 %collective-permute-start = (bf16[19,16,128]{2,1,0:T(8,128)(2,1)S(1)}, bf16[19,16,128]{2,1,0:T(8,128)(2,1)S(1)}, u32[]{:S(2)}, u32[]{:S(2)}) collective-permute-start(bf16[19,16,128]{2,1,0:T(8,128)(2,1)S(1)} %get-tuple-element.18.own_ref), channel_id=1, source_target_pairs={{0,1},{1,0},{2,3},{3,2},{4,5},{5,4},{6,7},{7,6},{8,9},{9,8},{10,11... | collective-permute-start | bytes 233480 | tf_op jit(solution)/shard_map/ppermute | solution.py:30
  4.0 8.2 %collective-permute-start.2 = (bf16[19,16,128]{2,1,0:T(8,128)(2,1)S(1)}, bf16[19,16,128]{2,1,0:T(8,128)(2,1)S(1)}, u32[]{:S(2)}, u32[]{:S(2)}) collective-permute-start(bf16[19,16,128]{2,1,0:T(8,128)(2,1)S(1)} %get-tuple-element.18.own_ref), channel_id=1, source_target_pairs={{0,3},{3,0},{1,2},{2,1},{4,7},{7,4},{5,6},{6,5},{8,11},{11,8},{9,1... | collective-permute-start | bytes 233480 | tf_op jit(solution)/shard_map/ppermute | solution.py:30
  6.2 6.0 %collective-permute-start.1 = (bf16[8,16,128]{2,1,0:T(8,128)(2,1)S(1)}, bf16[8,16,128]{2,1,0:T(8,128)(2,1)S(1)}, u32[]{:S(2)}, u32[]{:S(2)}) collective-permute-start(bf16[8,16,128]{2,1,0:T(8,128)(2,1)S(1)} %get-tuple-element.17.own_ref), channel_id=1, source_target_pairs={{0,2},{2,0},{1,3},{3,1},{4,6},{6,4},{5,7},{7,5},{8,10},{10,8},{9,1... | collective-permute-start | bytes 98312 | tf_op jit(solution)/shard_map/ppermute | solution.py:30
  12.2 11.5 %collective-permute-start.3 = (bf16[43,16,128]{2,1,0:T(8,128)(2,1)S(1)}, bf16[43,16,128]{2,1,0:T(8,128)(2,1)S(1)}, u32[]{:S(2)}, u32[]{:S(2)}) collective-permute-start(bf16[43,16,128]{2,1,0:T(8,128)(2,1)S(1)} %group.1.own_ref), channel_id=1, source_target_pairs={{0,4},{4,0},{8,12},{12,8},{16,20},{20,16},{24,28},{28,24},{1,5},{5... | collective-permute-start | bytes 528392 | tf_op jit(solution)/shard_map/ppermute | solution.py:30
  13.0 10.8 %collective-permute-start.4 = (bf16[43,16,128]{2,1,0:T(8,128)(2,1)S(1)}, bf16[43,16,128]{2,1,0:T(8,128)(2,1)S(1)}, u32[]{:S(2)}, u32[]{:S(2)}) collective-permute-start(bf16[43,16,128]{2,1,0:T(8,128)(2,1)S(1)} %group.1.own_ref), channel_id=1, source_target_pairs={{4,8},{8,4},{12,16},{16,12},{20,24},{24,20},{5,9},{9,5},{13,17},{1... | collective-permute-start | bytes 528392 | tf_op jit(solution)/shard_map/ppermute | solution.py:30

commit v3 on v2

--- a/solution.py
+++ b/solution.py
@@ -19,7 +19,7 @@
 ITEMS = 4
 ROWS = 32
 STAGES = 4
-FIRST_ITEMS = 5
+FIRST_ITEMS = 6
 
 
 def round_up(value, step):
@@ -226,16 +226,14 @@
 def turn_sources(source, src_ref, start):
     boxes, rows, width = source.shape
     eye = lax.broadcasted_iota(jnp.int32, (width, width), 0) == lax.broadcasted_iota(jnp.int32, (width, width), 1)
-    turned = nt_dot(eye.astype(F32).astype(BF16), source.reshape(boxes * rows, width))
-    column = lax.broadcasted_iota(jnp.int32, (width, 128), 1)
+    twice = jnp.concatenate([source, source], axis=1).reshape(boxes * 2 * rows, width)
+    turned = nt_dot(eye.astype(F32).astype(BF16), twice)
     for b in range(boxes):
-        at = b * rows
+        at = b * 2 * rows
         lanes = turned[:, at // 128 * 128 : at // 128 * 128 + 128]
-        for slot in range(2):
-            shift = (slot * rows - at) % 128
-            moved = pltpu.roll(lanes, shift, 1) if shift else lanes
-            inside = (column >= slot * rows) & (column < (slot + 1) * rows)
-            src_ref[slot, start + b] = jnp.where(inside, moved, 0.0).astype(BF16)
+        if at % 128:
+            lanes = pltpu.roll(lanes, 128 - at % 128, 1)
+        src_ref[start + b] = lanes.astype(BF16)
 
 
 def take_currents(x_rows, win_ref, start):
@@ -253,6 +251,7 @@
     pair_bits = count_bits + box_bits + source_bits
     t1_ref[...] = jnp.zeros(t1_ref.shape, BF16)
     upper = lax.broadcasted_iota(jnp.int32, (2 * waves, width), 0) < waves
+    left = lax.broadcasted_iota(jnp.int32, (width, 128), 1) < 16
     empty = jnp.zeros((16, width), BF16)
 
     def pair_at(chunk, g, slot):
@@ -265,7 +264,7 @@
     def distances(chunk, g, u_ref):
         source0, box0, _ = pair_at(chunk, g, 0)
         source1, box1, _ = pair_at(chunk, g, 1)
-        sources = src_ref[0, source0] + src_ref[1, source1]
+        sources = jnp.where(left, src_ref[source0], src_ref[source1])
         observers = jnp.concatenate(
             [
                 jnp.concatenate([obs_ref[box0], empty], axis=1),
@@ -372,7 +371,7 @@
 def near_kernel(entries, items_ref, own_ref, *refs):
     *step_refs, obs_ref, own_src_ref, first_ref, out_ref, win_ref, src_ref, list_ref, u0_ref, u1_ref, t0_ref, t1_ref, sems = refs
     boxes, waves, width = out_ref.shape
-    fetches = start_all(((items_ref, list_ref), (own_src_ref, src_ref.at[:, :boxes])), sems)
+    fetches = start_all(((items_ref, list_ref), (own_src_ref, src_ref.at[:boxes])), sems)
     length = list_ref.shape[1]
     here = lax.axis_index("dir")
     other_side = jnp.where((here & 1) == 0, here - 1, here + 1)
@@ -418,17 +417,12 @@
     sum_ref[...] = near_ref[...]
     x_rows = boxes // 2
     packet_rows = x_rows + 3 * boxes // 16
-    here = lax.axis_index("dir")
-
-    @pl.when((here == 0) | (here == lax.axis_size("dir") - 1))
-    def _():
-        from_even = jnp.where(here == 0, 1, 0) == odd_box
-        even_packet, odd_packet = (ref[ref.shape[0] - packet_rows :] for ref in (even_ref, odd_ref))
-        packet = jnp.where(from_even, even_packet.astype(F32), odd_packet.astype(F32)).astype(BF16)
-        take_currents(packet[:x_rows], win_ref, 0)
-        source, _ = features(packet[x_rows:])
-        turn_sources(source, src_ref, 0)
-
+    from_even = jnp.where(lax.axis_index("dir") == 0, 1, 0) == odd_box
+    even_packet, odd_packet = (ref[ref.shape[0] - packet_rows :] for ref in (even_ref, odd_ref))
+    packet = jnp.where(from_even, even_packet.astype(F32), odd_packet.astype(F32)).astype(BF16)
+    take_currents(packet[:x_rows], win_ref, 0)
+    source, _ = features(packet[x_rows:])
+    turn_sources(source, src_ref, 0)
     fetch.wait()
     cos_phase = cos_ref[...]
     sin_phase = sin_ref[...]
@@ -543,7 +537,7 @@
         out_shape=(
             shaped((boxes, waves, width), F32),
             shaped((boxes, 16, width), BF16),
-            shaped((2, boxes, width, 128), BF16),
+            shaped((boxes, width, 128), BF16),
             shaped((parents, window, 2, parent_dirs), F32),
         ),
         in_specs=[vmem] * 2 + [hbm] * 4,
@@ -582,7 +576,7 @@
         out_specs=vmem,
         scratch_shapes=[
             pltpu.VMEM((3 * boxes, 16, width), BF16),
-            pltpu.VMEM((2, 3 * boxes, width, 128), BF16),
+            pltpu.VMEM((3 * boxes, width, 128), BF16),
             pltpu.SMEM((1, length), jnp.int32),
         ]
         + near_scratch
@@ -599,7 +593,7 @@
         scratch_shapes=[
             pltpu.VMEM((boxes, waves, width), F32),
             pltpu.VMEM((boxes, 16, width), BF16),
-            pltpu.VMEM((2, boxes, width, 128), BF16),
+            pltpu.VMEM((boxes, width, 128), BF16),
             pltpu.VMEM((boxes * waves, parent_dirs), F32),
             pltpu.VMEM((boxes * waves, parent_dirs), F32),
             pltpu.SMEM((1, length), jnp.int32),

time: 31 us -> 30.2 us (0.974)
  Pallas kernels: 21.8 us -> 21.1 us
    pallas_call x1, Pallas kernels: 7.78 us -> 6.42 us  [per_device(): pl.pallas_call(functools.partial(near_kernel, entries), out_shape=shaped(...]
    pallas_call x1, Pallas kernels: 6.98 us -> 7.33 us  [per_device(): pl.pallas_call(functools.partial(incoming_kernel, entries), out_shape=sha...]
  transfers between devices with their start and end apart: 5 -> 5, of which waited for: 1 -> 1; matrix products, arithmetic and copies ran while one was open for 0% -> 0% of each run, Pallas kernels for 42% -> 40%
where the time goes in v3:
time: 30.2 us; the launch traced here: 30 us
  Pallas kernels  21.1 us (70%)
  starting transfers between devices  8.5 us (28%)
  waiting for transfers between devices  0.35 us (1%)
    ppermute x5, starting transfers between devices, swapped(): lax.ppermute(x, axis, [way for i, j in pairs for way in ((i, j), (j, i))])  8.5 us
    pallas_call x1, Pallas kernels, per_device(): pl.pallas_call(functools.partial(incoming_kernel, entries), out_shape=sha...  7.33 us
    pallas_call x1, Pallas kernels, per_device(): pl.pallas_call(functools.partial(near_kernel, entries), out_shape=shaped(...  6.42 us
    pallas_call x1, Pallas kernels, per_device(): pl.pallas_call(functools.partial(prepare_kernel, entries), out_shape=(sha...  5.54 us
    pallas_call x1, Pallas kernels, per_device(): pl.pallas_call(outgoing_kernel, out_shape=(shaped((own_rows + spectra_row...  1.79 us
  transfers between devices with their start and end apart: 5, of which 1 were waited for; matrix products, arithmetic and copies ran while one was open for 0% of the time, Pallas kernels for 40%

profile of v3, /device:TPU:1, one launch (start us, length us, event | category | flops | bytes accessed | tf_op | source)
XLA Modules:
  0.0 30.0 jit_solution(17216588447527879000)
XLA Ops:
  0.0 1.8 %outgoing.1 = (bf16[19,16,128]{2,1,0:T(8,128)(2,1)S(1)}, bf16[8,16,128]{2,1,0:T(8,128)(2,1)S(1)}, bf16[128,512]{1,0:T(8,128)(2,1)S(1)}, f32[8,512]{1,0:T(8,128)S...) custom-call(bf16[8,16,128]{2,1,0:T(8,128)(2,1)} %bitcast.4, ...), custom_call_target="tpu_custom_call" | custom-call | tf_op jit(solution)/shard_map/outgoing/pallas_call | solution.py:504
  1.8 2.2 %collective-permute-start = (bf16[19,16,128]{2,1,0:T(8,128)(2,1)S(1)}, bf16[19,16,128]{2,1,0:T(8,128)(2,1)S(1)}, u32[]{:S(2)}, u32[]{:S(2)}) collective-permute-start(bf16[19,16,128]{2,1,0:T(8,128)(2,1)S(1)} %get-tuple-element.18.own_ref), channel_id=1, source_target_pairs={{0,1},{1,0},{2,3},{3,2},{4,5},{5,4},{6,7},{7,6},{8,9},{9,8},{10,11... | collective-permute-start | bytes 233480 | tf_op jit(solution)/shard_map/ppermute | solution.py:30
  4.0 2.2 %collective-permute-start.2 = (bf16[19,16,128]{2,1,0:T(8,128)(2,1)S(1)}, bf16[19,16,128]{2,1,0:T(8,128)(2,1)S(1)}, u32[]{:S(2)}, u32[]{:S(2)}) collective-permute-start(bf16[19,16,128]{2,1,0:T(8,128)(2,1)S(1)} %get-tuple-element.18.own_ref), channel_id=1, source_target_pairs={{0,3},{3,0},{1,2},{2,1},{4,7},{7,4},{5,6},{6,5},{8,11},{11,8},{9,1... | collective-permute-start | bytes 233480 | tf_op jit(solution)/shard_map/ppermute | solution.py:30
  6.2 0.1 collective-permute-start.1
  6.3 5.5 %prepare.1 = (f32[16,8,128]{2,1,0:T(8,128)S(1)}, bf16[16,16,128]{2,1,0:T(8,128)(2,1)S(1)}, bf16[16,128,128]{2,1,0:T(8,128)(2,1)S(1)}, f32[2,24,2,512]{3,2,1,0:T(2,128)S(1)}) custom-call(bf16[19,16,128]{2,1,0:T(8,128)(2,1)S(1)} %get-tuple-element.18.own_ref, s32[1,384]{1,0:T(1,128)S(1)} %get-tuple-element.16.items_ref, s32[8,32]{1,0:T(8,128)} %src_hbm.1, ...), custom_call_target="tpu_custom_call" | custom-call | tf_op jit(solution)/shard_map/prepare/pallas_call | solution.py:535
  11.9 0.3 %collective-permute-done.1.refs_1_ = bf16[8,16,128]{2,1,0:T(8,128)(2,1)S(1)} collective-permute-done((bf16[8,16,128]{2,1,0:T(8,128)(2,1)S(1)}, bf16[8,16,128]{2,1,0:T(8,128)(2,1)S(1)}, u32[]{:S(2)}, u32[]{:S(2)}) %collective-permute-start.1) | collective-permute-done | bytes 32800 | tf_op jit(solution)/shard_map/ppermute | solution.py:30
  12.2 0.0 collective-permute-done.refs_0_
  12.2 0.0 collective-permute-done.2.refs_2_.refs_1_
  12.2 1.0 %collective-permute-start.3 = (bf16[43,16,128]{2,1,0:T(8,128)(2,1)S(1)}, bf16[43,16,128]{2,1,0:T(8,128)(2,1)S(1)}, u32[]{:S(2)}, u32[]{:S(2)}) collective-permute-start(bf16[43,16,128]{2,1,0:T(8,128)(2,1)S(1)} %group.1.own_ref), channel_id=1, source_target_pairs={{0,4},{4,0},{8,12},{12,8},{16,20},{20,16},{24,28},{28,24},{1,5},{5... | collective-permute-start | bytes 528392 | tf_op jit(solution)/shard_map/ppermute | solution.py:30
  13.2 3.0 %collective-permute-start.4 = (bf16[43,16,128]{2,1,0:T(8,128)(2,1)S(1)}, bf16[43,16,128]{2,1,0:T(8,128)(2,1)S(1)}, u32[]{:S(2)}, u32[]{:S(2)}) collective-permute-start(bf16[43,16,128]{2,1,0:T(8,128)(2,1)S(1)} %group.1.own_ref), channel_id=1, source_target_pairs={{4,8},{8,4},{12,16},{16,12},{20,24},{24,20},{5,9},{9,5},{13,17},{1... | collective-permute-start | bytes 528392 | tf_op jit(solution)/shard_map/ppermute | solution.py:30
  16.2 6.4 %near.1.near_ref = f32[16,8,128]{2,1,0:T(8,128)S(1)} custom-call(s32[1,384]{1,0:T(1,128)S(1)} %get-tuple-element.16.items_ref, bf16[19,16,128]{2,1,0:T(8,128)(2,1)S(1)} %get-tuple-element.18.own_ref, bf16[19,16,128]{2,1,0:T(8,128)(2,1)S(1)} %collective-permute-done.refs_0_, bf16[19,16,128]{2,1,0:T(8,128)(2,1)S(1)} %collective-permute-done.2.refs_2_.refs_1_, ...), custom_call_target="tpu_custom_call" | custom-call | tf_op jit(solution)/shard_map/near/pallas_call | solution.py:572
  22.7 0.0 collective-permute-done.3.even_ref
  22.7 0.0 collective-permute-done.4.odd_ref
  22.7 7.3 %incoming.1 = f32[16,8,128]{2,1,0:T(8,128)} custom-call(s32[1,384]{1,0:T(1,128)S(1)} %get-tuple-element.16.items_ref, bf16[43,16,128]{2,1,0:T(8,128)(2,1)S(1)} %collective-permute-done.3.even_ref, bf16[43,16,128]{2,1,0:T(8,128)(2,1)S(1)} %group.1.own_ref, bf16[43,16,128]{2,1,0:T(8,128)(2,1)S(1)} %collective-permute-done.4.odd_ref, ...), custom_call_target="tpu_custom_call" | custom-call | tf_op jit(solution)/shard_map/incoming/pallas_call | solution.py:588
  (1 shorter events, 0.0 us)
Async XLA Ops:
  1.8 10.4 %collective-permute-start = (bf16[19,16,128]{2,1,0:T(8,128)(2,1)S(1)}, bf16[19,16,128]{2,1,0:T(8,128)(2,1)S(1)}, u32[]{:S(2)}, u32[]{:S(2)}) collective-permute-start(bf16[19,16,128]{2,1,0:T(8,128)(2,1)S(1)} %get-tuple-element.18.own_ref), channel_id=1, source_target_pairs={{0,1},{1,0},{2,3},{3,2},{4,5},{5,4},{6,7},{7,6},{8,9},{9,8},{10,11... | collective-permute-start | bytes 233480 | tf_op jit(solution)/shard_map/ppermute | solution.py:30
  4.0 8.2 %collective-permute-start.2 = (bf16[19,16,128]{2,1,0:T(8,128)(2,1)S(1)}, bf16[19,16,128]{2,1,0:T(8,128)(2,1)S(1)}, u32[]{:S(2)}, u32[]{:S(2)}) collective-permute-start(bf16[19,16,128]{2,1,0:T(8,128)(2,1)S(1)} %get-tuple-element.18.own_ref), channel_id=1, source_target_pairs={{0,3},{3,0},{1,2},{2,1},{4,7},{7,4},{5,6},{6,5},{8,11},{11,8},{9,1... | collective-permute-start | bytes 233480 | tf_op jit(solution)/shard_map/ppermute | solution.py:30
  6.2 6.0 %collective-permute-start.1 = (bf16[8,16,128]{2,1,0:T(8,128)(2,1)S(1)}, bf16[8,16,128]{2,1,0:T(8,128)(2,1)S(1)}, u32[]{:S(2)}, u32[]{:S(2)}) collective-permute-start(bf16[8,16,128]{2,1,0:T(8,128)(2,1)S(1)} %get-tuple-element.17.own_ref), channel_id=1, source_target_pairs={{0,2},{2,0},{1,3},{3,1},{4,6},{6,4},{5,7},{7,5},{8,10},{10,8},{9,1... | collective-permute-start | bytes 98312 | tf_op jit(solution)/shard_map/ppermute | solution.py:30
  12.2 10.4 %collective-permute-start.3 = (bf16[43,16,128]{2,1,0:T(8,128)(2,1)S(1)}, bf16[43,16,128]{2,1,0:T(8,128)(2,1)S(1)}, u32[]{:S(2)}, u32[]{:S(2)}) collective-permute-start(bf16[43,16,128]{2,1,0:T(8,128)(2,1)S(1)} %group.1.own_ref), channel_id=1, source_target_pairs={{0,4},{4,0},{8,12},{12,8},{16,20},{20,16},{24,28},{28,24},{1,5},{5... | collective-permute-start | bytes 528392 | tf_op jit(solution)/shard_map/ppermute | solution.py:30
  13.2 9.5 %collective-permute-start.4 = (bf16[43,16,128]{2,1,0:T(8,128)(2,1)S(1)}, bf16[43,16,128]{2,1,0:T(8,128)(2,1)S(1)}, u32[]{:S(2)}, u32[]{:S(2)}) collective-permute-start(bf16[43,16,128]{2,1,0:T(8,128)(2,1)S(1)} %group.1.own_ref), channel_id=1, source_target_pairs={{4,8},{8,4},{12,16},{16,12},{20,24},{24,20},{5,9},{9,5},{13,17},{1... | collective-permute-start | bytes 528392 | tf_op jit(solution)/shard_map/ppermute | solution.py:30

commit v4 on v3

--- a/solution.py
+++ b/solution.py
@@ -322,8 +322,8 @@
 
 
 def prepare_kernel(
-    entries, own_ref, items_ref, src_hbm, id_hbm, count_hbm, table_hbm, out_ref, obs_ref, src_ref, gain_ref, trans_src_ref,
-    trans_id_ref, trans_count_ref, table_ref, list_ref, win_ref, u0_ref, u1_ref, t0_ref, t1_ref, sems
+    entries, own_ref, items_ref, src_hbm, id_hbm, count_hbm, table_hbm, out_ref, obs_ref, src_ref, win_ref, gain_ref,
+    trans_src_ref, trans_id_ref, trans_count_ref, table_ref, list_ref, u0_ref, u1_ref, t0_ref, t1_ref, sems
 ):
     boxes = obs_ref.shape[0]
     length = list_ref.shape[1]
@@ -368,27 +368,35 @@
             gain_ref[q, s] += table_ref[trans_id_ref[row0 + q, e]] * live
 
 
-def near_kernel(entries, items_ref, own_ref, *refs):
-    *step_refs, obs_ref, own_src_ref, first_ref, out_ref, win_ref, src_ref, list_ref, u0_ref, u1_ref, t0_ref, t1_ref, sems = refs
+def near_kernel(entries, items_ref, *refs):
+    *refs, sem = refs
+    (
+        *step_refs, obs_ref, first_ref, _, _, out_ref, src_ref, win_ref, list_ref, u0_ref, u1_ref, t0_ref, t1_ref
+    ) = refs
     boxes, waves, width = out_ref.shape
-    fetches = start_all(((items_ref, list_ref), (own_src_ref, src_ref.at[:boxes])), sems)
+    fetch = pltpu.make_async_copy(items_ref, list_ref, sem)
+    fetch.start()
     length = list_ref.shape[1]
     here = lax.axis_index("dir")
     other_side = jnp.where((here & 1) == 0, here - 1, here + 1)
     x_rows = boxes // 2
-
-    def take(ref, part):
-        take_currents(ref[:x_rows], win_ref, part * boxes)
-        source, _ = features(ref[x_rows : x_rows + 3 * boxes // 16])
+    own_rows = x_rows + 3 * boxes // 16
+
+    def take(packet, part):
+        take_currents(packet[:x_rows], win_ref, part * boxes)
+        source, _ = features(packet[x_rows:])
         turn_sources(source, src_ref, part * boxes)
 
-    take_currents(own_ref[:x_rows], win_ref, 0)
-    take(step_refs[0], 1)
-    for k, ref in enumerate(step_refs[1:], 2):
-        pl.when((here ^ ((1 << k) - 1)) == other_side)(functools.partial(take, ref, 2))
+    take(step_refs[0][:own_rows], 1)
+    if len(step_refs) > 1:
+        packet = step_refs[1][:own_rows]
+        for k, ref in enumerate(step_refs[2:], 3):
+            from_here = (here ^ ((1 << k) - 1)) == other_side
+            packet = jnp.where(from_here, ref[:own_rows].astype(F32), packet.astype(F32)).astype(BF16)
+        take(packet, 2)
     second_start = list_places(boxes, entries)[1]
     out_ref[...] = first_ref[...]
-    wait_all(fetches)
+    fetch.wait()
     near_sum(
         entries,
         list_ref[0, length - 2],
@@ -403,7 +411,7 @@
 
 
 def incoming_kernel(
-    entries, items_ref, even_ref, own_ref, odd_ref, gain_ref, cos_ref, sin_ref, imat_ref, rad_ref, obs_ref, near_ref, out_ref,
+    entries, items_ref, odd_ref, own_ref, even_ref, gain_ref, cos_ref, sin_ref, imat_ref, rad_ref, obs_ref, near_ref, out_ref,
     sum_ref, win_ref, src_ref, down_re_ref, down_im_ref, list_ref, u0_ref, u1_ref, t0_ref, t1_ref, sem
 ):
     parents, window, _, parent_dirs = gain_ref.shape
@@ -532,23 +540,23 @@
         pltpu.VMEM((ITEMS, width, 2 * width), BF16),
         pltpu.VMEM((ITEMS, width, 2 * width), BF16),
     ]
-    first_sum, observers, sources, gains = pl.pallas_call(
+    first_sum, observers, sources, ordered, gains = pl.pallas_call(
         functools.partial(prepare_kernel, entries),
         out_shape=(
             shaped((boxes, waves, width), F32),
             shaped((boxes, 16, width), BF16),
-            shaped((boxes, width, 128), BF16),
+            shaped((3 * boxes, width, 128), BF16),
+            shaped((3 * boxes, 16, width), BF16),
             shaped((parents, window, 2, parent_dirs), F32),
         ),
         in_specs=[vmem] * 2 + [hbm] * 4,
-        out_specs=(vmem,) * 4,
+        out_specs=(vmem,) * 5,
         scratch_shapes=[
             pltpu.SMEM(trans_src.shape, jnp.int32),
             pltpu.SMEM(trans_id.shape, jnp.int32),
             pltpu.SMEM(trans_count.shape, jnp.int32),
             pltpu.VMEM(trans_table.shape, F32),
             pltpu.SMEM((1, length), jnp.int32),
-            pltpu.VMEM((boxes, 16, width), BF16),
         ]
         + near_scratch
         + [pltpu.SemaphoreType.DMA((5,))],
@@ -569,21 +577,20 @@
     group_even = swapped(group, "box", [(i, i + 1) for i in range(0, groups - 1, 2)])
 
     packets = [x for step, x in enumerate(steps, 1) if carries_packet(step)]
-    near = pl.pallas_call(
+    near, _, _ = pl.pallas_call(
         functools.partial(near_kernel, entries),
-        out_shape=shaped((boxes, waves, width), F32),
+        out_shape=(
+            shaped((boxes, waves, width), F32),
+            shaped(sources.shape, BF16),
+            shaped(ordered.shape, BF16),
+        ),
         in_specs=[vmem] * (5 + len(packets)),
-        out_specs=vmem,
-        scratch_shapes=[
-            pltpu.VMEM((3 * boxes, 16, width), BF16),
-            pltpu.VMEM((3 * boxes, width, 128), BF16),
-            pltpu.SMEM((1, length), jnp.int32),
-        ]
-        + near_scratch
-        + [pltpu.SemaphoreType.DMA((2,))],
+        out_specs=(vmem,) * 3,
+        input_output_aliases={3 + len(packets): 1, 4 + len(packets): 2},
+        scratch_shapes=[pltpu.SMEM((1, length), jnp.int32)] + near_scratch + [pltpu.SemaphoreType.DMA],
         compiler_params=params,
         name="near",
-    )(items, packet, *packets, observers, sources, first_sum)
+    )(items, *packets, observers, first_sum, sources, ordered)
 
     return pl.pallas_call(
         functools.partial(incoming_kernel, entries),
@@ -602,7 +609,7 @@
         + [pltpu.SemaphoreType.DMA],
         compiler_params=params,
         name="incoming",
-    )(items, group_even, group, group_odd, gains, cos_phase, sin_phase, imat, rad, observers, near)
+    )(items, group_odd, group, group_even, gains, cos_phase, sin_phase, imat, rad, observers, near)
 
 
 def solution(mesh):

time: 30.2 us -> 29.8 us (0.987)
  Pallas kernels: 21.1 us -> 20.7 us
    pallas_call x1, Pallas kernels: 7.33 us -> 6.93 us  [per_device(): pl.pallas_call(functools.partial(incoming_kernel, entries), out_shape=sha...]
where the time goes in v4:
time: 29.8 us; the launch traced here: 29.6 us
  Pallas kernels  20.7 us (69%)
  starting transfers between devices  8.47 us (28%)
  waiting for transfers between devices  0.4 us (1%)
    ppermute x5, starting transfers between devices, swapped(): lax.ppermute(x, axis, [way for i, j in pairs for way in ((i, j), (j, i))])  8.47 us
    pallas_call x1, Pallas kernels, per_device(): pl.pallas_call(functools.partial(incoming_kernel, entries), out_shape=sha...  6.93 us
    pallas_call x1, Pallas kernels, per_device(): pl.pallas_call(functools.partial(near_kernel, entries), out_shape=(shaped...  6.46 us
    pallas_call x1, Pallas kernels, per_device(): pl.pallas_call(functools.partial(prepare_kernel, entries), out_shape=(sha...  5.5 us
    pallas_call x1, Pallas kernels, per_device(): pl.pallas_call(outgoing_kernel, out_shape=(shaped((own_rows + spectra_row...  1.79 us
  transfers between devices with their start and end apart: 5, of which 1 were waited for; matrix products, arithmetic and copies ran while one was open for 0% of the time, Pallas kernels for 40%

profile of v4, /device:TPU:1, one launch (start us, length us, event | category | flops | bytes accessed | tf_op | source)
XLA Modules:
  0.0 29.6 jit_solution(8177557000742576425)
XLA Ops:
  0.0 1.8 %outgoing.1 = (bf16[19,16,128]{2,1,0:T(8,128)(2,1)S(1)}, bf16[8,16,128]{2,1,0:T(8,128)(2,1)S(1)}, bf16[128,512]{1,0:T(8,128)(2,1)S(1)}, f32[8,512]{1,0:T(8,128)S...) custom-call(bf16[8,16,128]{2,1,0:T(8,128)(2,1)} %bitcast.4, ...), custom_call_target="tpu_custom_call" | custom-call | tf_op jit(solution)/shard_map/outgoing/pallas_call | solution.py:512
  1.8 2.2 %collective-permute-start = (bf16[19,16,128]{2,1,0:T(8,128)(2,1)S(1)}, bf16[19,16,128]{2,1,0:T(8,128)(2,1)S(1)}, u32[]{:S(2)}, u32[]{:S(2)}) collective-permute-start(bf16[19,16,128]{2,1,0:T(8,128)(2,1)S(1)} %get-tuple-element.20.own_ref), channel_id=1, source_target_pairs={{0,1},{1,0},{2,3},{3,2},{4,5},{5,4},{6,7},{7,6},{8,9},{9,8},{10,11... | collective-permute-start | bytes 233480 | tf_op jit(solution)/shard_map/ppermute | solution.py:30
  4.0 2.2 %collective-permute-start.2 = (bf16[19,16,128]{2,1,0:T(8,128)(2,1)S(1)}, bf16[19,16,128]{2,1,0:T(8,128)(2,1)S(1)}, u32[]{:S(2)}, u32[]{:S(2)}) collective-permute-start(bf16[19,16,128]{2,1,0:T(8,128)(2,1)S(1)} %get-tuple-element.20.own_ref), channel_id=1, source_target_pairs={{0,3},{3,0},{1,2},{2,1},{4,7},{7,4},{5,6},{6,5},{8,11},{11,8},{9,1... | collective-permute-start | bytes 233480 | tf_op jit(solution)/shard_map/ppermute | solution.py:30
  6.2 0.1 collective-permute-start.1
  6.3 5.5 %prepare.1 = (f32[16,8,128]{2,1,0:T(8,128)S(1)}, bf16[16,16,128]{2,1,0:T(8,128)(2,1)S(1)}, bf16[48,128,128]{2,1,0:T(8,128)(2,1)S(1)}, bf16[48,16,128]{2,1,0:T(8,128)(2,1)S(1)}, f32[2,24,2,512]{3,2,1,0:T(2,128)S(1)}) custom-call(bf16[19,16,128]{2,1,0:T(8,128)(2,1)S(1)} %get-tuple-element.20.own_ref, s32[1,384]{1,0:T(1,128)S(1)} %get-tuple-element.18.items_ref, ...), custom_call_target="tpu_custom_call" | custom-call | tf_op jit(solution)/shard_map/prepare/pallas_call | solution.py:543
  11.8 0.4 %collective-permute-done.1.refs_1_ = bf16[8,16,128]{2,1,0:T(8,128)(2,1)S(1)} collective-permute-done((bf16[8,16,128]{2,1,0:T(8,128)(2,1)S(1)}, bf16[8,16,128]{2,1,0:T(8,128)(2,1)S(1)}, u32[]{:S(2)}, u32[]{:S(2)}) %collective-permute-start.1) | collective-permute-done | bytes 32800 | tf_op jit(solution)/shard_map/ppermute | solution.py:30
  12.2 0.0 collective-permute-done.refs_0_
  12.2 0.0 collective-permute-done.2.refs_2_.refs_1_
  12.2 3.9 %collective-permute-start.3 = (bf16[43,16,128]{2,1,0:T(8,128)(2,1)S(1)}, bf16[43,16,128]{2,1,0:T(8,128)(2,1)S(1)}, u32[]{:S(2)}, u32[]{:S(2)}) collective-permute-start(bf16[43,16,128]{2,1,0:T(8,128)(2,1)S(1)} %group.1.own_ref), channel_id=1, source_target_pairs={{4,8},{8,4},{12,16},{16,12},{20,24},{24,20},{5,9},{9,5},{13,17},{1... | collective-permute-start | bytes 528392 | tf_op jit(solution)/shard_map/ppermute | solution.py:30
  16.1 0.1 collective-permute-start.4
  16.2 6.5 %near.1 = (f32[16,8,128]{2,1,0:T(8,128)S(1)}, bf16[48,128,128]{2,1,0:T(8,128)(2,1)S(1)}, bf16[48,16,128]{2,1,0:T(8,128)(2,1)S(1)}) custom-call(s32[1,384]{1,0:T(1,128)S(1)} %get-tuple-element.18.items_ref, bf16[19,16,128]{2,1,0:T(8,128)(2,1)S(1)} %collective-permute-done.refs_0_, ...), custom_call_target="tpu_custom_call", output_to_operand_aliasing={{1}: (5, {}), {2}: (6, {})} | custom-call | tf_op jit(solution)/shard_map/near/pallas_call | solution.py:580
  22.7 0.0 collective-permute-done.3.odd_ref
  22.7 0.0 collective-permute-done.4.even_ref
  22.7 6.9 %incoming.1 = f32[16,8,128]{2,1,0:T(8,128)} custom-call(s32[1,384]{1,0:T(1,128)S(1)} %get-tuple-element.18.items_ref, bf16[43,16,128]{2,1,0:T(8,128)(2,1)S(1)} %collective-permute-done.3.odd_ref, bf16[43,16,128]{2,1,0:T(8,128)(2,1)S(1)} %group.1.own_ref, bf16[43,16,128]{2,1,0:T(8,128)(2,1)S(1)} %collective-permute-done.4.even_ref, ...), custom_call_target="tpu_custom_call" | custom-call | tf_op jit(solution)/shard_map/incoming/pallas_call | solution.py:595
  (1 shorter events, 0.0 us)
Async XLA Ops:
  1.8 10.4 %collective-permute-start = (bf16[19,16,128]{2,1,0:T(8,128)(2,1)S(1)}, bf16[19,16,128]{2,1,0:T(8,128)(2,1)S(1)}, u32[]{:S(2)}, u32[]{:S(2)}) collective-permute-start(bf16[19,16,128]{2,1,0:T(8,128)(2,1)S(1)} %get-tuple-element.20.own_ref), channel_id=1, source_target_pairs={{0,1},{1,0},{2,3},{3,2},{4,5},{5,4},{6,7},{7,6},{8,9},{9,8},{10,11... | collective-permute-start | bytes 233480 | tf_op jit(solution)/shard_map/ppermute | solution.py:30
  4.0 8.2 %collective-permute-start.2 = (bf16[19,16,128]{2,1,0:T(8,128)(2,1)S(1)}, bf16[19,16,128]{2,1,0:T(8,128)(2,1)S(1)}, u32[]{:S(2)}, u32[]{:S(2)}) collective-permute-start(bf16[19,16,128]{2,1,0:T(8,128)(2,1)S(1)} %get-tuple-element.20.own_ref), channel_id=1, source_target_pairs={{0,3},{3,0},{1,2},{2,1},{4,7},{7,4},{5,6},{6,5},{8,11},{11,8},{9,1... | collective-permute-start | bytes 233480 | tf_op jit(solution)/shard_map/ppermute | solution.py:30
  6.2 6.0 %collective-permute-start.1 = (bf16[8,16,128]{2,1,0:T(8,128)(2,1)S(1)}, bf16[8,16,128]{2,1,0:T(8,128)(2,1)S(1)}, u32[]{:S(2)}, u32[]{:S(2)}) collective-permute-start(bf16[8,16,128]{2,1,0:T(8,128)(2,1)S(1)} %get-tuple-element.19.own_ref), channel_id=1, source_target_pairs={{0,2},{2,0},{1,3},{3,1},{4,6},{6,4},{5,7},{7,5},{8,10},{10,8},{9,1... | collective-permute-start | bytes 98312 | tf_op jit(solution)/shard_map/ppermute | solution.py:30
  12.2 10.5 %collective-permute-start.3 = (bf16[43,16,128]{2,1,0:T(8,128)(2,1)S(1)}, bf16[43,16,128]{2,1,0:T(8,128)(2,1)S(1)}, u32[]{:S(2)}, u32[]{:S(2)}) collective-permute-start(bf16[43,16,128]{2,1,0:T(8,128)(2,1)S(1)} %group.1.own_ref), channel_id=1, source_target_pairs={{4,8},{8,4},{12,16},{16,12},{20,24},{24,20},{5,9},{9,5},{13,17},{1... | collective-permute-start | bytes 528392 | tf_op jit(solution)/shard_map/ppermute | solution.py:30
  16.1 6.6 %collective-permute-start.4 = (bf16[43,16,128]{2,1,0:T(8,128)(2,1)S(1)}, bf16[43,16,128]{2,1,0:T(8,128)(2,1)S(1)}, u32[]{:S(2)}, u32[]{:S(2)}) collective-permute-start(bf16[43,16,128]{2,1,0:T(8,128)(2,1)S(1)} %group.1.own_ref), channel_id=1, source_target_pairs={{0,4},{4,0},{8,12},{12,8},{16,20},{20,16},{24,28},{28,24},{1,5},{5... | collective-permute-start | bytes 528392 | tf_op jit(solution)/shard_map/ppermute | solution.py:30

commit v5 on v4

--- a/solution.py
+++ b/solution.py
@@ -20,6 +20,8 @@
 ROWS = 32
 STAGES = 4
 FIRST_ITEMS = 6
+AHEAD = 2
+LEFT_OVER = 2
 
 
 def round_up(value, step):
@@ -78,7 +80,7 @@
     box_col = lax.broadcasted_iota(jnp.int32, (boxes, boxes), 1)
     rank = nn_dot((box_col < box_row).astype(F32).astype(BF16), flags.astype(BF16)).astype(jnp.int32)
     pairs = jnp.sum(flags, axis=0, keepdims=True)
-    from_cross = (lane >= 2 * boxes) & edge
+    from_cross = lane >= jnp.where(edge, 2 * boxes, 3 * boxes - LEFT_OVER)
     cross_pairs = jnp.where(from_cross[:1], pairs, 0.0)
     group_pairs = jnp.where(from_cross[:1], 0.0, pairs)
     row = lax.broadcasted_iota(jnp.int32, (lanes, lanes), 0)
@@ -244,7 +246,7 @@
         win_ref[start + 2 * k + 1] = jnp.concatenate([wide[8:], wide[:8]], axis=0).astype(BF16)
 
 
-def near_sum(entries, total, item_at, first_source, src_ref, win_ref, obs_ref, out_ref, scratch):
+def near_sum(entries, total, item_at, first_source, src_ref, win_ref, obs_ref, out_ref, scratch, ahead=0):
     u0_ref, u1_ref, t0_ref, t1_ref = scratch
     boxes, waves, width = out_ref.shape
     count_bits, box_bits, source_bits = code_bits(boxes, entries)
@@ -303,20 +305,23 @@
 
     def body(k, carry):
         for j in range(STAGES):
-            stage(k * STAGES + j, j & 1)
+            stage(ahead + k * STAGES + j, j & 1)
         return carry
 
     def finish(turn):
         for g in range(ITEMS):
             product(jnp.maximum(chunks - 1, 0), g, t_refs[turn])
 
-    chunks = (total + (ITEMS - 1)) // ITEMS
-    rounds = chunks // STAGES
+    chunks = jnp.maximum((total + (ITEMS - 1)) // ITEMS, ahead)
+    rounds = (chunks - ahead) // STAGES
     for g in range(ITEMS):
         distances(0, g, u0_ref)
+    for j in range(ahead):
+        stage(j, j & 1)
     lax.fori_loop(0, rounds, body, 0)
+    last = ahead + rounds * STAGES
     for j in range(STAGES - 1):
-        pl.when(rounds * STAGES + j < chunks)(functools.partial(stage, rounds * STAGES + j, j & 1))
+        pl.when(last + j < chunks)(functools.partial(stage, last + j, j & 1))
     pl.when((chunks > 0) & ((chunks & 1) == 0))(functools.partial(finish, 1))
     pl.when((chunks & 1) == 1)(functools.partial(finish, 0))
 
@@ -410,9 +415,13 @@
     )
 
 
-def incoming_kernel(
-    entries, items_ref, odd_ref, own_ref, even_ref, gain_ref, cos_ref, sin_ref, imat_ref, rad_ref, obs_ref, near_ref, out_ref,
-    sum_ref, win_ref, src_ref, down_re_ref, down_im_ref, list_ref, u0_ref, u1_ref, t0_ref, t1_ref, sem
+def incoming_kernel(entries, others, *refs):
+    incoming(entries, *refs[others:], other_refs=refs[:others])
+
+
+def incoming(
+    entries, items_ref, even_ref, own_ref, odd_ref, gain_ref, cos_ref, sin_ref, imat_ref, rad_ref, obs_ref, near_ref, out_ref,
+    sum_ref, win_ref, src_ref, down_re_ref, down_im_ref, list_ref, u0_ref, u1_ref, t0_ref, t1_ref, sem, other_refs=()
 ):
     parents, window, _, parent_dirs = gain_ref.shape
     boxes, waves, width = near_ref.shape
@@ -425,9 +434,15 @@
     sum_ref[...] = near_ref[...]
     x_rows = boxes // 2
     packet_rows = x_rows + 3 * boxes // 16
-    from_even = jnp.where(lax.axis_index("dir") == 0, 1, 0) == odd_box
+    here = lax.axis_index("dir")
+    from_even = jnp.where(here == 0, 1, 0) == odd_box
     even_packet, odd_packet = (ref[ref.shape[0] - packet_rows :] for ref in (even_ref, odd_ref))
-    packet = jnp.where(from_even, even_packet.astype(F32), odd_packet.astype(F32)).astype(BF16)
+    packet = jnp.where(from_even, even_packet.astype(F32), odd_packet.astype(F32))
+    other_side = jnp.where((here & 1) == 0, here - 1, here + 1)
+    for k, ref in enumerate(other_refs, 2):
+        from_group = (here ^ ((1 << k) - 1)) == other_side
+        packet = jnp.where(from_group, ref[:packet_rows].astype(F32), packet)
+    packet = packet.astype(BF16)
     take_currents(packet[:x_rows], win_ref, 0)
     source, _ = features(packet[x_rows:])
     turn_sources(source, src_ref, 0)
@@ -478,6 +493,7 @@
         obs_ref,
         sum_ref,
         (u0_ref, u1_ref, t0_ref, t1_ref),
+        AHEAD,
     )
     factor = TURN * LEAD / math.sqrt(entries * width)
     out_ref[...] = sum_ref[...] * factor + far.reshape(near_ref.shape)
@@ -593,9 +609,9 @@
     )(items, *packets, observers, first_sum, sources, ordered)
 
     return pl.pallas_call(
-        functools.partial(incoming_kernel, entries),
+        functools.partial(incoming_kernel, entries, len(packets) - 1),
         out_shape=shaped((boxes, waves, width), F32),
-        in_specs=[vmem] * 11,
+        in_specs=[vmem] * (10 + len(packets)),
         out_specs=vmem,
         scratch_shapes=[
             pltpu.VMEM((boxes, waves, width), F32),
@@ -609,7 +625,7 @@
         + [pltpu.SemaphoreType.DMA],
         compiler_params=params,
         name="incoming",
-    )(items, group_odd, group, group_even, gains, cos_phase, sin_phase, imat, rad, observers, near)
+    )(*packets[1:], items, group_even, group, group_odd, gains, cos_phase, sin_phase, imat, rad, observers, near)
 
 
 def solution(mesh):

time: 29.8 us -> 30.1 us (1.010)
  starting transfers between devices: 8.47 us -> 9.04 us
  waiting for transfers between devices: 0.4 us -> 0.01 us
    ppermute x5, starting transfers between devices: 8.47 us -> 9.04 us  [swapped(): lax.ppermute(x, axis, [way for i, j in pairs for way in ((i, j), (j, i))])]
    ppermute x5, waiting for transfers between devices: 0.4 us -> 0.01 us  [swapped(): lax.ppermute(x, axis, [way for i, j in pairs for way in ((i, j), (j, i))])]
  transfers between devices with their start and end apart: 5 -> 5, of which waited for: 1 -> 0; matrix products, arithmetic and copies ran while one was open for 0% -> 0% of each run, Pallas kernels for 40% -> 40%
where the time goes in v5:
time: 30.1 us; the launch traced here: 30 us
  Pallas kernels  20.9 us (69%)
  starting transfers between devices  9.04 us (30%)
    ppermute x5, starting transfers between devices, swapped(): lax.ppermute(x, axis, [way for i, j in pairs for way in ((i, j), (j, i))])  9.04 us
    pallas_call x1, Pallas kernels, per_device(): pl.pallas_call(functools.partial(incoming_kernel, entries, len(packets) -...  7.11 us
    pallas_call x1, Pallas kernels, per_device(): pl.pallas_call(functools.partial(near_kernel, entries), out_shape=(shaped...  6.46 us
    pallas_call x1, Pallas kernels, per_device(): pl.pallas_call(functools.partial(prepare_kernel, entries), out_shape=(sha...  5.5 us
    pallas_call x1, Pallas kernels, per_device(): pl.pallas_call(outgoing_kernel, out_shape=(shaped((own_rows + spectra_row...  1.79 us
  transfers between devices with their start and end apart: 5, of which 0 were waited for; matrix products, arithmetic and copies ran while one was open for 0% of the time, Pallas kernels for 40%

profile of v5, /device:TPU:1, one launch (start us, length us, event | category | flops | bytes accessed | tf_op | source)
XLA Modules:
  0.0 30.0 jit_solution(2414534597297699894)
XLA Ops:
  0.0 1.8 %outgoing.1 = (bf16[19,16,128]{2,1,0:T(8,128)(2,1)S(1)}, bf16[8,16,128]{2,1,0:T(8,128)(2,1)S(1)}, bf16[128,512]{1,0:T(8,128)(2,1)S(1)}, f32[8,512]{1,0:T(8,128)S...) custom-call(bf16[8,16,128]{2,1,0:T(8,128)(2,1)} %bitcast.4, ...), custom_call_target="tpu_custom_call" | custom-call | tf_op jit(solution)/shard_map/outgoing/pallas_call | solution.py:528
  1.8 4.2 %collective-permute-start = (bf16[19,16,128]{2,1,0:T(8,128)(2,1)S(1)}, bf16[19,16,128]{2,1,0:T(8,128)(2,1)S(1)}, u32[]{:S(2)}, u32[]{:S(2)}) collective-permute-start(bf16[19,16,128]{2,1,0:T(8,128)(2,1)S(1)} %get-tuple-element.18.own_ref), channel_id=1, source_target_pairs={{0,3},{3,0},{1,2},{2,1},{4,7},{7,4},{5,6},{6,5},{8,11},{11,8},{9,1... | collective-permute-start | bytes 233480 | tf_op jit(solution)/shard_map/ppermute | solution.py:32
  6.0 0.0 collective-permute-start.1
  6.0 0.4 %collective-permute-start.2 = (bf16[8,16,128]{2,1,0:T(8,128)(2,1)S(1)}, bf16[8,16,128]{2,1,0:T(8,128)(2,1)S(1)}, u32[]{:S(2)}, u32[]{:S(2)}) collective-permute-start(bf16[8,16,128]{2,1,0:T(8,128)(2,1)S(1)} %get-tuple-element.20.own_ref), channel_id=1, source_target_pairs={{0,2},{2,0},{1,3},{3,1},{4,6},{6,4},{5,7},{7,5},{8,10},{10,8},{9,1... | collective-permute-start | bytes 98312 | tf_op jit(solution)/shard_map/ppermute | solution.py:32
  6.4 5.5 %prepare.1 = (f32[16,8,128]{2,1,0:T(8,128)S(1)}, bf16[16,16,128]{2,1,0:T(8,128)(2,1)S(1)}, bf16[48,128,128]{2,1,0:T(8,128)(2,1)S(1)}, bf16[48,16,128]{2,1,0:T(8,128)(2,1)S(1)}, f32[2,24,2,512]{3,2,1,0:T(2,128)S(1)}) custom-call(bf16[19,16,128]{2,1,0:T(8,128)(2,1)S(1)} %get-tuple-element.18.own_ref, s32[1,384]{1,0:T(1,128)S(1)} %get-tuple-element.19.items_ref.refs_1_, ...), custom_call_target="tpu_custom_call" | custom-call | tf_op jit(solution)/shard_map/prepare/pallas_call | solution.py:559
  11.9 0.0 collective-permute-done.2.refs_1_
  11.9 0.0 collective-permute-done.refs_2_.refs_1_.refs_0_
  11.9 0.0 collective-permute-done.1.refs_0_
  12.0 1.3 %collective-permute-start.3 = (bf16[43,16,128]{2,1,0:T(8,128)(2,1)S(1)}, bf16[43,16,128]{2,1,0:T(8,128)(2,1)S(1)}, u32[]{:S(2)}, u32[]{:S(2)}) collective-permute-start(bf16[43,16,128]{2,1,0:T(8,128)(2,1)S(1)} %group.1.refs_3_), channel_id=1, source_target_pairs={{0,4},{4,0},{8,12},{12,8},{16,20},{20,16},{24,28},{28,24},{1,5},{5... | collective-permute-start | bytes 528392 | tf_op jit(solution)/shard_map/ppermute | solution.py:32
  13.2 3.2 %collective-permute-start.4 = (bf16[43,16,128]{2,1,0:T(8,128)(2,1)S(1)}, bf16[43,16,128]{2,1,0:T(8,128)(2,1)S(1)}, u32[]{:S(2)}, u32[]{:S(2)}) collective-permute-start(bf16[43,16,128]{2,1,0:T(8,128)(2,1)S(1)} %group.1.refs_3_), channel_id=1, source_target_pairs={{4,8},{8,4},{12,16},{16,12},{20,24},{24,20},{5,9},{9,5},{13,17},{1... | collective-permute-start | bytes 528392 | tf_op jit(solution)/shard_map/ppermute | solution.py:32
  16.4 6.5 %near.1 = (f32[16,8,128]{2,1,0:T(8,128)S(1)}, bf16[48,128,128]{2,1,0:T(8,128)(2,1)S(1)}, bf16[48,16,128]{2,1,0:T(8,128)(2,1)S(1)}) custom-call(s32[1,384]{1,0:T(1,128)S(1)} %get-tuple-element.19.items_ref.refs_1_, bf16[19,16,128]{2,1,0:T(8,128)(2,1)S(1)} %collective-permute-done.1.refs_0_, ...), custom_call_target="tpu_custom_call", output_to_operand_aliasing={{1}: (5, {}), {2}: (6, {})} | custom-call | tf_op jit(solution)/shard_map/near/pallas_call | solution.py:596
  22.9 0.0 collective-permute-done.3.refs_2_
  22.9 0.0 collective-permute-done.4.refs_4_
  22.9 7.1 %incoming.1 = f32[16,8,128]{2,1,0:T(8,128)} custom-call(bf16[19,16,128]{2,1,0:T(8,128)(2,1)S(1)} %collective-permute-done.refs_2_.refs_1_.refs_0_, s32[1,384]{1,0:T(1,128)S(1)} %get-tuple-element.19.items_ref.refs_1_, bf16[43,16,128]{2,1,0:T(8,128)(2,1)S(1)} %collective-permute-done.3.refs_2_, bf16[43,16,128]{2,1,0:T(8,128)(2,1)S(1)} %group.1.refs_3_, ...), custom_call_target="tpu_custom_call" | custom-call | tf_op jit(solution)/shard_map/incoming/pallas_call | solution.py:611
  (1 shorter events, 0.0 us)
Async XLA Ops:
  1.8 10.1 %collective-permute-start = (bf16[19,16,128]{2,1,0:T(8,128)(2,1)S(1)}, bf16[19,16,128]{2,1,0:T(8,128)(2,1)S(1)}, u32[]{:S(2)}, u32[]{:S(2)}) collective-permute-start(bf16[19,16,128]{2,1,0:T(8,128)(2,1)S(1)} %get-tuple-element.18.own_ref), channel_id=1, source_target_pairs={{0,3},{3,0},{1,2},{2,1},{4,7},{7,4},{5,6},{6,5},{8,11},{11,8},{9,1... | collective-permute-start | bytes 233480 | tf_op jit(solution)/shard_map/ppermute | solution.py:32
  6.0 5.9 %collective-permute-start.1 = (bf16[19,16,128]{2,1,0:T(8,128)(2,1)S(1)}, bf16[19,16,128]{2,1,0:T(8,128)(2,1)S(1)}, u32[]{:S(2)}, u32[]{:S(2)}) collective-permute-start(bf16[19,16,128]{2,1,0:T(8,128)(2,1)S(1)} %get-tuple-element.18.own_ref), channel_id=1, source_target_pairs={{0,1},{1,0},{2,3},{3,2},{4,5},{5,4},{6,7},{7,6},{8,9},{9,8},{10,11... | collective-permute-start | bytes 233480 | tf_op jit(solution)/shard_map/ppermute | solution.py:32
  6.0 5.9 %collective-permute-start.2 = (bf16[8,16,128]{2,1,0:T(8,128)(2,1)S(1)}, bf16[8,16,128]{2,1,0:T(8,128)(2,1)S(1)}, u32[]{:S(2)}, u32[]{:S(2)}) collective-permute-start(bf16[8,16,128]{2,1,0:T(8,128)(2,1)S(1)} %get-tuple-element.20.own_ref), channel_id=1, source_target_pairs={{0,2},{2,0},{1,3},{3,1},{4,6},{6,4},{5,7},{7,5},{8,10},{10,8},{9,1... | collective-permute-start | bytes 98312 | tf_op jit(solution)/shard_map/ppermute | solution.py:32
  12.0 10.9 %collective-permute-start.3 = (bf16[43,16,128]{2,1,0:T(8,128)(2,1)S(1)}, bf16[43,16,128]{2,1,0:T(8,128)(2,1)S(1)}, u32[]{:S(2)}, u32[]{:S(2)}) collective-permute-start(bf16[43,16,128]{2,1,0:T(8,128)(2,1)S(1)} %group.1.refs_3_), channel_id=1, source_target_pairs={{0,4},{4,0},{8,12},{12,8},{16,20},{20,16},{24,28},{28,24},{1,5},{5... | collective-permute-start | bytes 528392 | tf_op jit(solution)/shard_map/ppermute | solution.py:32
  13.2 9.7 %collective-permute-start.4 = (bf16[43,16,128]{2,1,0:T(8,128)(2,1)S(1)}, bf16[43,16,128]{2,1,0:T(8,128)(2,1)S(1)}, u32[]{:S(2)}, u32[]{:S(2)}) collective-permute-start(bf16[43,16,128]{2,1,0:T(8,128)(2,1)S(1)} %group.1.refs_3_), channel_id=1, source_target_pairs={{4,8},{8,4},{12,16},{16,12},{20,24},{24,20},{5,9},{9,5},{13,17},{1... | collective-permute-start | bytes 528392 | tf_op jit(solution)/shard_map/ppermute | solution.py:32

commit v6 on v5

--- a/solution.py
+++ b/solution.py
@@ -19,7 +19,6 @@
 ITEMS = 4
 ROWS = 32
 STAGES = 4
-FIRST_ITEMS = 6
 AHEAD = 2
 LEFT_OVER = 2
 
@@ -48,20 +47,19 @@
 
 
 def code_bits(boxes, entries):
-    return entries.bit_length(), (boxes - 1).bit_length(), (3 * boxes - 1).bit_length()
+    return entries.bit_length(), (boxes - 1).bit_length()
 
 
 def list_places(boxes, entries):
     gap = 2 * ITEMS
-    most = FIRST_ITEMS * boxes // 2
-    return most, most + gap, round_up(most + gap + boxes * entries // 2 + 2 * gap + 6, 128)
+    second_start = (boxes * (boxes + 1) // 2 + 1) // 2 + gap
+    return second_start, round_up(second_start + boxes * entries // 2 + 2 * gap + 6, 128)
 
 
 def list_items(near_src, block, here, size):
     boxes, entries = near_src.shape
-    most, second_start, length = list_places(boxes, entries)
-    count_bits, box_bits, source_bits = code_bits(boxes, entries)
-    pair_bits = count_bits + box_bits + source_bits
+    second_start, length = list_places(boxes, entries)
+    count_bits, box_bits = code_bits(boxes, entries)
     lanes = round_up(3 * boxes, 128)
     odd = (here & 1) == 1
     edge = (here == 0) | (here == size - 1)
@@ -74,49 +72,45 @@
     count = jnp.zeros((boxes, lanes), jnp.int32)
     for e in range(entries):
         count = count + (local[:, e : e + 1] == lane).astype(jnp.int32)
-    present = count > 0
+    from_own = lane < boxes
+    mirrored = count.astype(F32).T[:boxes]
+    mirrored = jnp.concatenate([mirrored, jnp.zeros((boxes, lanes - boxes), F32)], axis=1).astype(jnp.int32)
+    back = jnp.where(from_own & (lane != box), mirrored, 0)
+    present = (count + back > 0) & ((lane >= box) | (lane >= boxes))
     flags = present.astype(F32)
     box_row = lax.broadcasted_iota(jnp.int32, (boxes, boxes), 0)
     box_col = lax.broadcasted_iota(jnp.int32, (boxes, boxes), 1)
     rank = nn_dot((box_col < box_row).astype(F32).astype(BF16), flags.astype(BF16)).astype(jnp.int32)
     pairs = jnp.sum(flags, axis=0, keepdims=True)
     from_cross = lane >= jnp.where(edge, 2 * boxes, 3 * boxes - LEFT_OVER)
+    own_pairs = jnp.where(from_own[:1], pairs, 0.0)
     cross_pairs = jnp.where(from_cross[:1], pairs, 0.0)
-    group_pairs = jnp.where(from_cross[:1], 0.0, pairs)
+    group_pairs = jnp.where(from_own[:1] | from_cross[:1], 0.0, pairs)
     row = lax.broadcasted_iota(jnp.int32, (lanes, lanes), 0)
     col = lax.broadcasted_iota(jnp.int32, (lanes, lanes), 1)
     ahead = (row < col).astype(F32).astype(BF16)
-    lists = jnp.concatenate([group_pairs, cross_pairs, jnp.zeros((6, lanes), F32)], axis=0)
+    lists = jnp.concatenate([own_pairs, group_pairs, cross_pairs, jnp.zeros((5, lanes), F32)], axis=0)
     offset = nn_dot(lists.astype(BF16), ahead).astype(jnp.int32)
-    own_pairs = jnp.where(lane[:1] < boxes, group_pairs, 0.0)
-
-    def total(pairs):
-        return jnp.sum(pairs, axis=1, keepdims=True).astype(jnp.int32)
-
-    first_total = jnp.minimum(total(own_pairs), 2 * most)
-    second_total = total(group_pairs) - first_total
-    cross_total = total(cross_pairs)
-    order = offset[0:1] + rank
-    in_second = order >= first_total
-    order = jnp.where(in_second, order - first_total, order)
-    order = jnp.where(from_cross, offset[1:2] + rank, order)
+    order = jnp.where(from_own, offset[0:1], jnp.where(from_cross, offset[2:3], offset[1:2])) + rank
     half = order >> 1
-    place = jnp.where(from_cross, (length - 4) - half, jnp.where(in_second, second_start + half, half))
+    place = jnp.where(from_own, half, jnp.where(from_cross, (length - 4) - half, second_start + half))
     place = jnp.where(present, place, -1)
-    code = (lane << (count_bits + box_bits)) | (box << count_bits) | count
-    code = jnp.where((order & 1) == 1, code << pair_bits, code)
+    code = (((lane << box_bits) | box) << (2 * count_bits)) | (back << count_bits) | count
+    odd_place = (order & 1) == 1
     place_t = place.T
-    code_t = code.T
+    codes_t = (jnp.where(odd_place, 0, code).T, jnp.where(odd_place, code, 0).T)
     rows = 3 * boxes
     slot = lax.broadcasted_iota(jnp.int32, (rows, length), 1)
-    found = jnp.zeros((rows, length), jnp.int32)
+    found = [jnp.zeros((rows, length), jnp.int32) for _ in range(2)]
     for i in range(boxes):
         hit = place_t[:rows, i : i + 1] == slot
-        found = found + jnp.where(hit, code_t[:rows, i : i + 1], 0)
-    listed = jnp.sum(found, axis=0, keepdims=True)
-    at = lax.broadcasted_iota(jnp.int32, (1, length), 1)
-    for back, pairs in ((3, first_total), (2, second_total), (1, cross_total)):
-        listed = jnp.where(at == length - back, (pairs + 1) >> 1, listed)
+        for k in range(2):
+            found[k] = found[k] + jnp.where(hit, codes_t[k][:rows, i : i + 1], 0)
+    listed = jnp.concatenate([jnp.sum(x, axis=0, keepdims=True) for x in found], axis=0)
+    at = lax.broadcasted_iota(jnp.int32, (2, length), 1)
+    for ahead_of_end, pairs in ((3, own_pairs), (2, group_pairs), (1, cross_pairs)):
+        total = jnp.sum(pairs, axis=1, keepdims=True).astype(jnp.int32)
+        listed = jnp.where(at == length - ahead_of_end, (total + 1) >> 1, listed)
     return listed
 
 
@@ -246,22 +240,25 @@
         win_ref[start + 2 * k + 1] = jnp.concatenate([wide[8:], wide[:8]], axis=0).astype(BF16)
 
 
-def near_sum(entries, total, item_at, first_source, src_ref, win_ref, obs_ref, out_ref, scratch, ahead=0):
+def near_sum(
+    entries, total, item_at, first_source, src_ref, win_ref, obs_ref, out_ref, scratch, ahead=0, mutual=False
+):
     u0_ref, u1_ref, t0_ref, t1_ref = scratch
     boxes, waves, width = out_ref.shape
-    count_bits, box_bits, source_bits = code_bits(boxes, entries)
-    pair_bits = count_bits + box_bits + source_bits
+    count_bits, box_bits = code_bits(boxes, entries)
     t1_ref[...] = jnp.zeros(t1_ref.shape, BF16)
     upper = lax.broadcasted_iota(jnp.int32, (2 * waves, width), 0) < waves
     left = lax.broadcasted_iota(jnp.int32, (width, 128), 1) < 16
     empty = jnp.zeros((16, width), BF16)
 
     def pair_at(chunk, g, slot):
-        code = item_at(chunk * ITEMS + g) >> (slot * pair_bits)
-        source = (code >> (count_bits + box_bits)) & ((1 << source_bits) - 1)
+        code = item_at(slot, chunk * ITEMS + g)
+        source = code >> (2 * count_bits + box_bits)
         if first_source:
             source = jnp.maximum(source - first_source, 0)
-        return source, (code >> count_bits) & ((1 << box_bits) - 1), code & ((1 << count_bits) - 1)
+        box = (code >> (2 * count_bits)) & ((1 << box_bits) - 1)
+        counts = [(code >> (way * count_bits)) & ((1 << count_bits) - 1) for way in range(2)]
+        return source, box, [count.astype(F32) for count in counts]
 
     def distances(chunk, g, u_ref):
         source0, box0, _ = pair_at(chunk, g, 0)
@@ -287,12 +284,18 @@
             t_ref[g, at : at + ROWS] = (cosine * pltpu.reciprocal(q + OFFSET * TURN, approx=True)).astype(BF16)
 
     def product(chunk, g, t_ref):
-        source0, box0, count0 = pair_at(chunk, g, 0)
-        source1, box1, count1 = pair_at(chunk, g, 1)
+        source0, box0, counts0 = pair_at(chunk, g, 0)
+        source1, box1, counts1 = pair_at(chunk, g, 1)
         currents = jnp.where(upper, win_ref[source0].astype(F32), win_ref[source1 ^ 1].astype(F32)).astype(BF16)
         got = nn_dot(currents, t_ref[g])
-        out_ref[box0] += count0.astype(F32) * got[:waves, :width]
-        out_ref[box1] += count1.astype(F32) * got[waves:, width:]
+        out_ref[box0] += counts0[0] * got[:waves, :width]
+        out_ref[box1] += counts1[0] * got[waves:, width:]
+        if mutual:
+            first = jnp.where(upper, win_ref[box0].astype(F32), 0.0).astype(BF16)
+            second = jnp.where(upper, 0.0, win_ref[box1 ^ 1].astype(F32)).astype(BF16)
+            got = nt_dot(jnp.concatenate([first, second], axis=1), t_ref[g])
+            out_ref[source0] += counts0[1] * got[:waves]
+            out_ref[source1] += counts1[1] * got[waves:]
 
     u_refs = (u0_ref, u1_ref)
     t_refs = (t0_ref, t1_ref)
@@ -355,13 +358,14 @@
     near_sum(
         entries,
         list_ref[0, length - 3],
-        lambda k: list_ref[0, k],
+        lambda slot, k: list_ref[slot, k],
         0,
         src_ref,
         win_ref,
         obs_ref,
         out_ref,
         (u0_ref, u1_ref, t0_ref, t1_ref),
+        mutual=True,
     )
     wait_all(trans_copies)
     row0 = lax.axis_index("dir") * parents
@@ -399,13 +403,13 @@
             from_here = (here ^ ((1 << k) - 1)) == other_side
             packet = jnp.where(from_here, ref[:own_rows].astype(F32), packet.astype(F32)).astype(BF16)
         take(packet, 2)
-    second_start = list_places(boxes, entries)[1]
+    second_start, _ = list_places(boxes, entries)
     out_ref[...] = first_ref[...]
     fetch.wait()
     near_sum(
         entries,
         list_ref[0, length - 2],
-        lambda k: list_ref[0, second_start + k],
+        lambda slot, k: list_ref[slot, second_start + k],
         0,
         src_ref,
         win_ref,
@@ -486,7 +490,7 @@
     near_sum(
         entries,
         list_ref[0, length - 1],
-        lambda k: list_ref[0, length - 4 - k],
+        lambda slot, k: list_ref[slot, length - 4 - k],
         2 * boxes,
         src_ref,
         win_ref,
@@ -524,7 +528,7 @@
     own_rows = x_rows + 3 * boxes // 16
     operands = (currents.reshape(x_rows, 2 * waves, width), positions.transpose(1, 0, 2), radiation, interp_index.T, interp_weight.T, child_phase)
     operands = operands + (near_src,)
-    length = list_places(boxes, entries)[2]
+    _, length = list_places(boxes, entries)
     packet, spectra, imat, cos_phase, sin_phase, rad, items = pl.pallas_call(
         outgoing_kernel,
         out_shape=(
@@ -534,7 +538,7 @@
             shaped((8, parent_dirs), F32),
             shaped((8, parent_dirs), F32),
             shaped(radiation.shape, BF16),
-            shaped((1, length), jnp.int32),
+            shaped((2, length), jnp.int32),
         ),
         in_specs=[hbm] * len(operands),
         out_specs=(vmem,) * 7,
@@ -572,7 +576,7 @@
             pltpu.SMEM(trans_id.shape, jnp.int32),
             pltpu.SMEM(trans_count.shape, jnp.int32),
             pltpu.VMEM(trans_table.shape, F32),
-            pltpu.SMEM((1, length), jnp.int32),
+            pltpu.SMEM((2, length), jnp.int32),
         ]
         + near_scratch
         + [pltpu.SemaphoreType.DMA((5,))],
@@ -603,7 +607,7 @@
         in_specs=[vmem] * (5 + len(packets)),
         out_specs=(vmem,) * 3,
         input_output_aliases={3 + len(packets): 1, 4 + len(packets): 2},
-        scratch_shapes=[pltpu.SMEM((1, length), jnp.int32)] + near_scratch + [pltpu.SemaphoreType.DMA],
+        scratch_shapes=[pltpu.SMEM((2, length), jnp.int32)] + near_scratch + [pltpu.SemaphoreType.DMA],
         compiler_params=params,
         name="near",
     )(items, *packets, observers, first_sum, sources, ordered)
@@ -619,7 +623,7 @@
             pltpu.VMEM((boxes, width, 128), BF16),
             pltpu.VMEM((boxes * waves, parent_dirs), F32),
             pltpu.VMEM((boxes * waves, parent_dirs), F32),
-            pltpu.SMEM((1, length), jnp.int32),
+            pltpu.SMEM((2, length), jnp.int32),
         ]
         + near_scratch
         + [pltpu.SemaphoreType.DMA],

time: 30.1 us -> 30.2 us (level); the launches traced: 30 us -> 29.8 us
  starting transfers between devices: 9.04 us -> 8.63 us
  waiting for transfers between devices: 0.01 us -> 0.38 us
    pallas_call x1, Pallas kernels: 6.46 us -> 5.52 us  [per_device(): pl.pallas_call(functools.partial(near_kernel, entries), out_shape=(shaped...]
    pallas_call x1, Pallas kernels: 5.5 us -> 6.4 us  [per_device(): pl.pallas_call(functools.partial(prepare_kernel, entries), out_shape=(sha...]
    ppermute x5, starting transfers between devices: 9.04 us -> 8.63 us  [swapped(): lax.ppermute(x, axis, [way for i, j in pairs for way in ((i, j), (j, i))])]
    pallas_call x1, Pallas kernels: 7.11 us -> 6.72 us  [per_device(): pl.pallas_call(functools.partial(incoming_kernel, entries, len(packets) -...]
    ppermute x5, waiting for transfers between devices: 0.01 us -> 0.38 us  [swapped(): lax.ppermute(x, axis, [way for i, j in pairs for way in ((i, j), (j, i))])]
  transfers between devices with their start and end apart: 5 -> 5, of which waited for: 0 -> 1; matrix products, arithmetic and copies ran while one was open for 0% -> 0% of each run, Pallas kernels for 40% -> 40%
where the time goes in v6:
time: 30.2 us; the launch traced here: 29.8 us
  Pallas kernels  20.7 us (69%)
  starting transfers between devices  8.63 us (29%)
  waiting for transfers between devices  0.38 us (1%)
    ppermute x5, starting transfers between devices, swapped(): lax.ppermute(x, axis, [way for i, j in pairs for way in ((i, j), (j, i))])  8.63 us
    pallas_call x1, Pallas kernels, per_device(): pl.pallas_call(functools.partial(incoming_kernel, entries, len(packets) -...  6.72 us
    pallas_call x1, Pallas kernels, per_device(): pl.pallas_call(functools.partial(prepare_kernel, entries), out_shape=(sha...  6.4 us
    pallas_call x1, Pallas kernels, per_device(): pl.pallas_call(functools.partial(near_kernel, entries), out_shape=(shaped...  5.52 us
    pallas_call x1, Pallas kernels, per_device(): pl.pallas_call(outgoing_kernel, out_shape=(shaped((own_rows + spectra_row...  2.04 us
  transfers between devices with their start and end apart: 5, of which 1 were waited for; matrix products, arithmetic and copies ran while one was open for 0% of the time, Pallas kernels for 40%

profile of v6, /device:TPU:1, one launch (start us, length us, event | category | flops | bytes accessed | tf_op | source)
XLA Modules:
  0.0 29.8 jit_solution(1661893628595744941)
XLA Ops:
  0.0 2.0 %outgoing.1 = (bf16[19,16,128]{2,1,0:T(8,128)(2,1)S(1)}, bf16[8,16,128]{2,1,0:T(8,128)(2,1)S(1)}, bf16[128,512]{1,0:T(8,128)(2,1)S(1)}, f32[8,512]{1,0:T(8,128)S...) custom-call(bf16[8,16,128]{2,1,0:T(8,128)(2,1)} %bitcast.4, ...), custom_call_target="tpu_custom_call" | custom-call | tf_op jit(solution)/shard_map/outgoing/pallas_call | solution.py:532
  2.0 4.2 %collective-permute-start = (bf16[19,16,128]{2,1,0:T(8,128)(2,1)S(1)}, bf16[19,16,128]{2,1,0:T(8,128)(2,1)S(1)}, u32[]{:S(2)}, u32[]{:S(2)}) collective-permute-start(bf16[19,16,128]{2,1,0:T(8,128)(2,1)S(1)} %get-tuple-element.18.own_ref), channel_id=1, source_target_pairs={{0,3},{3,0},{1,2},{2,1},{4,7},{7,4},{5,6},{6,5},{8,11},{11,8},{9,1... | collective-permute-start | bytes 233480 | tf_op jit(solution)/shard_map/ppermute | solution.py:31
  6.3 0.0 collective-permute-start.1
  6.3 0.4 %collective-permute-start.2 = (bf16[8,16,128]{2,1,0:T(8,128)(2,1)S(1)}, bf16[8,16,128]{2,1,0:T(8,128)(2,1)S(1)}, u32[]{:S(2)}, u32[]{:S(2)}) collective-permute-start(bf16[8,16,128]{2,1,0:T(8,128)(2,1)S(1)} %get-tuple-element.20.own_ref), channel_id=1, source_target_pairs={{0,2},{2,0},{1,3},{3,1},{4,6},{6,4},{5,7},{7,5},{8,10},{10,8},{9,1... | collective-permute-start | bytes 98312 | tf_op jit(solution)/shard_map/ppermute | solution.py:31
  6.6 6.4 %prepare.1 = (f32[16,8,128]{2,1,0:T(8,128)S(1)}, bf16[16,16,128]{2,1,0:T(8,128)(2,1)S(1)}, bf16[48,128,128]{2,1,0:T(8,128)(2,1)S(1)}, bf16[48,16,128]{2,1,0:T(8,128)(2,1)S(1)}, f32[2,24,2,512]{3,2,1,0:T(2,128)S(1)}) custom-call(bf16[19,16,128]{2,1,0:T(8,128)(2,1)S(1)} %get-tuple-element.18.own_ref, s32[2,384]{1,0:T(2,128)S(1)} %get-tuple-element.19.items_ref.refs_1_, ...), custom_call_target="tpu_custom_call" | custom-call | tf_op jit(solution)/shard_map/prepare/pallas_call | solution.py:563
  13.0 0.0 collective-permute-done.2.refs_1_
  13.0 0.0 collective-permute-done.refs_2_.refs_1_.refs_0_
  13.1 0.0 collective-permute-done.1.refs_0_
  13.1 1.7 %collective-permute-start.3 = (bf16[43,16,128]{2,1,0:T(8,128)(2,1)S(1)}, bf16[43,16,128]{2,1,0:T(8,128)(2,1)S(1)}, u32[]{:S(2)}, u32[]{:S(2)}) collective-permute-start(bf16[43,16,128]{2,1,0:T(8,128)(2,1)S(1)} %group.1.refs_3_), channel_id=1, source_target_pairs={{0,4},{4,0},{8,12},{12,8},{16,20},{20,16},{24,28},{28,24},{1,5},{5... | collective-permute-start | bytes 528392 | tf_op jit(solution)/shard_map/ppermute | solution.py:31
  14.8 2.4 %collective-permute-start.4 = (bf16[43,16,128]{2,1,0:T(8,128)(2,1)S(1)}, bf16[43,16,128]{2,1,0:T(8,128)(2,1)S(1)}, u32[]{:S(2)}, u32[]{:S(2)}) collective-permute-start(bf16[43,16,128]{2,1,0:T(8,128)(2,1)S(1)} %group.1.refs_3_), channel_id=1, source_target_pairs={{4,8},{8,4},{12,16},{16,12},{20,24},{24,20},{5,9},{9,5},{13,17},{1... | collective-permute-start | bytes 528392 | tf_op jit(solution)/shard_map/ppermute | solution.py:31
  17.2 5.5 %near.1 = (f32[16,8,128]{2,1,0:T(8,128)S(1)}, bf16[48,128,128]{2,1,0:T(8,128)(2,1)S(1)}, bf16[48,16,128]{2,1,0:T(8,128)(2,1)S(1)}) custom-call(s32[2,384]{1,0:T(2,128)S(1)} %get-tuple-element.19.items_ref.refs_1_, bf16[19,16,128]{2,1,0:T(8,128)(2,1)S(1)} %collective-permute-done.1.refs_0_, ...), custom_call_target="tpu_custom_call", output_to_operand_aliasing={{1}: (5, {}), {2}: (6, {})} | custom-call | tf_op jit(solution)/shard_map/near/pallas_call | solution.py:600
  22.7 0.0 collective-permute-done.3.refs_2_
  22.7 0.4 %collective-permute-done.4.refs_4_ = bf16[43,16,128]{2,1,0:T(8,128)(2,1)S(1)} collective-permute-done((bf16[43,16,128]{2,1,0:T(8,128)(2,1)S(1)}, bf16[43,16,128]{2,1,0:T(8,128)(2,1)S(1)}, u32[]{:S(2)}, u32[]{:S(2)}) %collective-permute-start.4) | collective-permute-done | bytes 176160 | tf_op jit(solution)/shard_map/ppermute | solution.py:31
  23.1 6.7 %incoming.1 = f32[16,8,128]{2,1,0:T(8,128)} custom-call(bf16[19,16,128]{2,1,0:T(8,128)(2,1)S(1)} %collective-permute-done.refs_2_.refs_1_.refs_0_, s32[2,384]{1,0:T(2,128)S(1)} %get-tuple-element.19.items_ref.refs_1_, bf16[43,16,128]{2,1,0:T(8,128)(2,1)S(1)} %collective-permute-done.3.refs_2_, bf16[43,16,128]{2,1,0:T(8,128)(2,1)S(1)} %group.1.refs_3_, ...), custom_call_target="tpu_custom_call" | custom-call | tf_op jit(solution)/shard_map/incoming/pallas_call | solution.py:615
  (1 shorter events, 0.0 us)
Async XLA Ops:
  2.0 11.0 %collective-permute-start = (bf16[19,16,128]{2,1,0:T(8,128)(2,1)S(1)}, bf16[19,16,128]{2,1,0:T(8,128)(2,1)S(1)}, u32[]{:S(2)}, u32[]{:S(2)}) collective-permute-start(bf16[19,16,128]{2,1,0:T(8,128)(2,1)S(1)} %get-tuple-element.18.own_ref), channel_id=1, source_target_pairs={{0,3},{3,0},{1,2},{2,1},{4,7},{7,4},{5,6},{6,5},{8,11},{11,8},{9,1... | collective-permute-start | bytes 233480 | tf_op jit(solution)/shard_map/ppermute | solution.py:31
  6.3 6.8 %collective-permute-start.1 = (bf16[19,16,128]{2,1,0:T(8,128)(2,1)S(1)}, bf16[19,16,128]{2,1,0:T(8,128)(2,1)S(1)}, u32[]{:S(2)}, u32[]{:S(2)}) collective-permute-start(bf16[19,16,128]{2,1,0:T(8,128)(2,1)S(1)} %get-tuple-element.18.own_ref), channel_id=1, source_target_pairs={{0,1},{1,0},{2,3},{3,2},{4,5},{5,4},{6,7},{7,6},{8,9},{9,8},{10,11... | collective-permute-start | bytes 233480 | tf_op jit(solution)/shard_map/ppermute | solution.py:31
  6.3 6.8 %collective-permute-start.2 = (bf16[8,16,128]{2,1,0:T(8,128)(2,1)S(1)}, bf16[8,16,128]{2,1,0:T(8,128)(2,1)S(1)}, u32[]{:S(2)}, u32[]{:S(2)}) collective-permute-start(bf16[8,16,128]{2,1,0:T(8,128)(2,1)S(1)} %get-tuple-element.20.own_ref), channel_id=1, source_target_pairs={{0,2},{2,0},{1,3},{3,1},{4,6},{6,4},{5,7},{7,5},{8,10},{10,8},{9,1... | collective-permute-start | bytes 98312 | tf_op jit(solution)/shard_map/ppermute | solution.py:31
  13.1 9.6 %collective-permute-start.3 = (bf16[43,16,128]{2,1,0:T(8,128)(2,1)S(1)}, bf16[43,16,128]{2,1,0:T(8,128)(2,1)S(1)}, u32[]{:S(2)}, u32[]{:S(2)}) collective-permute-start(bf16[43,16,128]{2,1,0:T(8,128)(2,1)S(1)} %group.1.refs_3_), channel_id=1, source_target_pairs={{0,4},{4,0},{8,12},{12,8},{16,20},{20,16},{24,28},{28,24},{1,5},{5... | collective-permute-start | bytes 528392 | tf_op jit(solution)/shard_map/ppermute | solution.py:31
  14.8 8.3 %collective-permute-start.4 = (bf16[43,16,128]{2,1,0:T(8,128)(2,1)S(1)}, bf16[43,16,128]{2,1,0:T(8,128)(2,1)S(1)}, u32[]{:S(2)}, u32[]{:S(2)}) collective-permute-start(bf16[43,16,128]{2,1,0:T(8,128)(2,1)S(1)} %group.1.refs_3_), channel_id=1, source_target_pairs={{4,8},{8,4},{12,16},{16,12},{20,24},{24,20},{5,9},{9,5},{13,17},{1... | collective-permute-start | bytes 528392 | tf_op jit(solution)/shard_map/ppermute | solution.py:31

commit v7 on v5

--- a/solution.py
+++ b/solution.py
@@ -18,7 +18,7 @@
 LEAD = 0.04087004462557604
 ITEMS = 4
 ROWS = 32
-STAGES = 4
+STAGES = 2
 FIRST_ITEMS = 6
 AHEAD = 2
 LEFT_OVER = 2

time: 30.1 us -> 30.1 us (level)
  transfers between devices with their start and end apart: 5 -> 5, of which waited for: 0 -> 0; matrix products, arithmetic and copies ran while one was open for 0% -> 0% of each run, Pallas kernels for 40% -> 39%
where the time goes in v7:
time: 30.1 us; the launch traced here: 30 us
  Pallas kernels  20.8 us (69%)
  starting transfers between devices  9.04 us (30%)
    ppermute x5, starting transfers between devices, swapped(): lax.ppermute(x, axis, [way for i, j in pairs for way in ((i, j), (j, i))])  9.04 us
    pallas_call x1, Pallas kernels, per_device(): pl.pallas_call(functools.partial(incoming_kernel, entries, len(packets) -...  7.21 us
    pallas_call x1, Pallas kernels, per_device(): pl.pallas_call(functools.partial(near_kernel, entries), out_shape=(shaped...  6.24 us
    pallas_call x1, Pallas kernels, per_device(): pl.pallas_call(functools.partial(prepare_kernel, entries), out_shape=(sha...  5.56 us
    pallas_call x1, Pallas kernels, per_device(): pl.pallas_call(outgoing_kernel, out_shape=(shaped((own_rows + spectra_row...  1.79 us
  transfers between devices with their start and end apart: 5, of which 0 were waited for; matrix products, arithmetic and copies ran while one was open for 0% of the time, Pallas kernels for 39%

profile of v7, /device:TPU:1, one launch (start us, length us, event | category | flops | bytes accessed | tf_op | source)
XLA Modules:
  0.0 30.0 jit_solution(15386145061475300367)
XLA Ops:
  0.0 1.8 %outgoing.1 = (bf16[19,16,128]{2,1,0:T(8,128)(2,1)S(1)}, bf16[8,16,128]{2,1,0:T(8,128)(2,1)S(1)}, bf16[128,512]{1,0:T(8,128)(2,1)S(1)}, f32[8,512]{1,0:T(8,128)S...) custom-call(bf16[8,16,128]{2,1,0:T(8,128)(2,1)} %bitcast.4, ...), custom_call_target="tpu_custom_call" | custom-call | tf_op jit(solution)/shard_map/outgoing/pallas_call | solution.py:528
  1.8 4.2 %collective-permute-start = (bf16[19,16,128]{2,1,0:T(8,128)(2,1)S(1)}, bf16[19,16,128]{2,1,0:T(8,128)(2,1)S(1)}, u32[]{:S(2)}, u32[]{:S(2)}) collective-permute-start(bf16[19,16,128]{2,1,0:T(8,128)(2,1)S(1)} %get-tuple-element.18.own_ref), channel_id=1, source_target_pairs={{0,3},{3,0},{1,2},{2,1},{4,7},{7,4},{5,6},{6,5},{8,11},{11,8},{9,1... | collective-permute-start | bytes 233480 | tf_op jit(solution)/shard_map/ppermute | solution.py:32
  6.0 0.0 collective-permute-start.1
  6.0 0.4 %collective-permute-start.2 = (bf16[8,16,128]{2,1,0:T(8,128)(2,1)S(1)}, bf16[8,16,128]{2,1,0:T(8,128)(2,1)S(1)}, u32[]{:S(2)}, u32[]{:S(2)}) collective-permute-start(bf16[8,16,128]{2,1,0:T(8,128)(2,1)S(1)} %get-tuple-element.20.own_ref), channel_id=1, source_target_pairs={{0,2},{2,0},{1,3},{3,1},{4,6},{6,4},{5,7},{7,5},{8,10},{10,8},{9,1... | collective-permute-start | bytes 98312 | tf_op jit(solution)/shard_map/ppermute | solution.py:32
  6.4 5.6 %prepare.1 = (f32[16,8,128]{2,1,0:T(8,128)S(1)}, bf16[16,16,128]{2,1,0:T(8,128)(2,1)S(1)}, bf16[48,128,128]{2,1,0:T(8,128)(2,1)S(1)}, bf16[48,16,128]{2,1,0:T(8,128)(2,1)S(1)}, f32[2,24,2,512]{3,2,1,0:T(2,128)S(1)}) custom-call(bf16[19,16,128]{2,1,0:T(8,128)(2,1)S(1)} %get-tuple-element.18.own_ref, s32[1,384]{1,0:T(1,128)S(1)} %get-tuple-element.19.items_ref.refs_1_, ...), custom_call_target="tpu_custom_call" | custom-call | tf_op jit(solution)/shard_map/prepare/pallas_call | solution.py:559
  12.0 0.0 collective-permute-done.2.refs_1_
  12.0 0.0 collective-permute-done.refs_2_.refs_1_.refs_0_
  12.0 0.0 collective-permute-done.1.refs_0_
  12.0 1.3 %collective-permute-start.3 = (bf16[43,16,128]{2,1,0:T(8,128)(2,1)S(1)}, bf16[43,16,128]{2,1,0:T(8,128)(2,1)S(1)}, u32[]{:S(2)}, u32[]{:S(2)}) collective-permute-start(bf16[43,16,128]{2,1,0:T(8,128)(2,1)S(1)} %group.1.refs_3_), channel_id=1, source_target_pairs={{0,4},{4,0},{8,12},{12,8},{16,20},{20,16},{24,28},{28,24},{1,5},{5... | collective-permute-start | bytes 528392 | tf_op jit(solution)/shard_map/ppermute | solution.py:32
  13.3 3.2 %collective-permute-start.4 = (bf16[43,16,128]{2,1,0:T(8,128)(2,1)S(1)}, bf16[43,16,128]{2,1,0:T(8,128)(2,1)S(1)}, u32[]{:S(2)}, u32[]{:S(2)}) collective-permute-start(bf16[43,16,128]{2,1,0:T(8,128)(2,1)S(1)} %group.1.refs_3_), channel_id=1, source_target_pairs={{4,8},{8,4},{12,16},{16,12},{20,24},{24,20},{5,9},{9,5},{13,17},{1... | collective-permute-start | bytes 528392 | tf_op jit(solution)/shard_map/ppermute | solution.py:32
  16.5 6.2 %near.1 = (f32[16,8,128]{2,1,0:T(8,128)S(1)}, bf16[48,128,128]{2,1,0:T(8,128)(2,1)S(1)}, bf16[48,16,128]{2,1,0:T(8,128)(2,1)S(1)}) custom-call(s32[1,384]{1,0:T(1,128)S(1)} %get-tuple-element.19.items_ref.refs_1_, bf16[19,16,128]{2,1,0:T(8,128)(2,1)S(1)} %collective-permute-done.1.refs_0_, ...), custom_call_target="tpu_custom_call", output_to_operand_aliasing={{1}: (5, {}), {2}: (6, {})} | custom-call | tf_op jit(solution)/shard_map/near/pallas_call | solution.py:596
  22.7 0.0 collective-permute-done.3.refs_2_
  22.7 0.0 collective-permute-done.4.refs_4_
  22.7 7.2 %incoming.1 = f32[16,8,128]{2,1,0:T(8,128)} custom-call(bf16[19,16,128]{2,1,0:T(8,128)(2,1)S(1)} %collective-permute-done.refs_2_.refs_1_.refs_0_, s32[1,384]{1,0:T(1,128)S(1)} %get-tuple-element.19.items_ref.refs_1_, bf16[43,16,128]{2,1,0:T(8,128)(2,1)S(1)} %collective-permute-done.3.refs_2_, bf16[43,16,128]{2,1,0:T(8,128)(2,1)S(1)} %group.1.refs_3_, ...), custom_call_target="tpu_custom_call" | custom-call | tf_op jit(solution)/shard_map/incoming/pallas_call | solution.py:611
  (1 shorter events, 0.0 us)
Async XLA Ops:
  1.8 10.2 %collective-permute-start = (bf16[19,16,128]{2,1,0:T(8,128)(2,1)S(1)}, bf16[19,16,128]{2,1,0:T(8,128)(2,1)S(1)}, u32[]{:S(2)}, u32[]{:S(2)}) collective-permute-start(bf16[19,16,128]{2,1,0:T(8,128)(2,1)S(1)} %get-tuple-element.18.own_ref), channel_id=1, source_target_pairs={{0,3},{3,0},{1,2},{2,1},{4,7},{7,4},{5,6},{6,5},{8,11},{11,8},{9,1... | collective-permute-start | bytes 233480 | tf_op jit(solution)/shard_map/ppermute | solution.py:32
  6.0 6.0 %collective-permute-start.1 = (bf16[19,16,128]{2,1,0:T(8,128)(2,1)S(1)}, bf16[19,16,128]{2,1,0:T(8,128)(2,1)S(1)}, u32[]{:S(2)}, u32[]{:S(2)}) collective-permute-start(bf16[19,16,128]{2,1,0:T(8,128)(2,1)S(1)} %get-tuple-element.18.own_ref), channel_id=1, source_target_pairs={{0,1},{1,0},{2,3},{3,2},{4,5},{5,4},{6,7},{7,6},{8,9},{9,8},{10,11... | collective-permute-start | bytes 233480 | tf_op jit(solution)/shard_map/ppermute | solution.py:32
  6.0 5.9 %collective-permute-start.2 = (bf16[8,16,128]{2,1,0:T(8,128)(2,1)S(1)}, bf16[8,16,128]{2,1,0:T(8,128)(2,1)S(1)}, u32[]{:S(2)}, u32[]{:S(2)}) collective-permute-start(bf16[8,16,128]{2,1,0:T(8,128)(2,1)S(1)} %get-tuple-element.20.own_ref), channel_id=1, source_target_pairs={{0,2},{2,0},{1,3},{3,1},{4,6},{6,4},{5,7},{7,5},{8,10},{10,8},{9,1... | collective-permute-start | bytes 98312 | tf_op jit(solution)/shard_map/ppermute | solution.py:32
  12.0 10.7 %collective-permute-start.3 = (bf16[43,16,128]{2,1,0:T(8,128)(2,1)S(1)}, bf16[43,16,128]{2,1,0:T(8,128)(2,1)S(1)}, u32[]{:S(2)}, u32[]{:S(2)}) collective-permute-start(bf16[43,16,128]{2,1,0:T(8,128)(2,1)S(1)} %group.1.refs_3_), channel_id=1, source_target_pairs={{0,4},{4,0},{8,12},{12,8},{16,20},{20,16},{24,28},{28,24},{1,5},{5... | collective-permute-start | bytes 528392 | tf_op jit(solution)/shard_map/ppermute | solution.py:32
  13.3 9.4 %collective-permute-start.4 = (bf16[43,16,128]{2,1,0:T(8,128)(2,1)S(1)}, bf16[43,16,128]{2,1,0:T(8,128)(2,1)S(1)}, u32[]{:S(2)}, u32[]{:S(2)}) collective-permute-start(bf16[43,16,128]{2,1,0:T(8,128)(2,1)S(1)} %group.1.refs_3_), channel_id=1, source_target_pairs={{4,8},{8,4},{12,16},{16,12},{20,24},{24,20},{5,9},{9,5},{13,17},{1... | collective-permute-start | bytes 528392 | tf_op jit(solution)/shard_map/ppermute | solution.py:32

commit v8 on v7

--- a/solution.py
+++ b/solution.py
@@ -16,6 +16,14 @@
 TURN = WAVENUMBER / (2.0 * math.pi)
 CHAIN = (-2.2803148655023415, -1.415255674611144, -7.327656729815578, -24.467745134801202)
 LEAD = 0.04087004462557604
+COSINE = (
+    0.9999999999990674, -0.49999999998466105, 0.04166666662512991, -0.0013888888455587084, 2.480156463978284e-05,
+    -2.7556652559151664e-07, 2.08652097543821e-09, -1.135363495216746e-11, 4.13155312368983e-14,
+)
+SINE = (
+    0.9999999999999502, -0.16666666666584865, 0.008333333331120085, -0.00019841269610529892, 2.755730716252212e-06,
+    -2.5051753759896685e-08, 1.6052905945426492e-10, -7.584986682610132e-13, 2.4682378516637708e-15,
+)
 ITEMS = 4
 ROWS = 32
 STAGES = 2
@@ -30,6 +38,13 @@
 
 def swapped(x, axis, pairs):
     return lax.ppermute(x, axis, [way for i, j in pairs for way in ((i, j), (j, i))])
+
+
+def polynomial(coefficients, z):
+    value = jnp.full_like(z, coefficients[-1])
+    for coefficient in coefficients[-2::-1]:
+        value = value * z + coefficient
+    return value
 
 
 def split3(x):
@@ -166,8 +181,9 @@
         imat = imat + jnp.where(idx_ref[s : s + 1, :] == column, wgt_ref[s : s + 1, :], 0.0)
     imat = imat.astype(BF16)
     imat_ref[...] = imat
-    cos_phase = jnp.cos(phase_ref[...])
-    sin_phase = jnp.sin(phase_ref[...])
+    phase = phase_ref[...]
+    cos_phase = polynomial(COSINE, phase * phase)
+    sin_phase = phase * polynomial(SINE, phase * phase)
     cos_ref[...] = cos_phase
     sin_ref[...] = sin_phase
     leaf = nn_dot(x_ref[...].reshape(boxes * waves, width), rad_ref[...]).astype(BF16)
@@ -251,7 +267,7 @@
     boxes, waves, width = out_ref.shape
     count_bits, box_bits, source_bits = code_bits(boxes, entries)
     pair_bits = count_bits + box_bits + source_bits
-    t1_ref[...] = jnp.zeros(t1_ref.shape, BF16)
+    t1_ref[...] = jnp.zeros(t1_ref.shape, F32)
     upper = lax.broadcasted_iota(jnp.int32, (2 * waves, width), 0) < waves
     left = lax.broadcasted_iota(jnp.int32, (width, 128), 1) < 16
     empty = jnp.zeros((16, width), BF16)
@@ -284,12 +300,12 @@
             cosine = t * t + CHAIN[0]
             for constant in CHAIN[1:]:
                 cosine = cosine * cosine + constant
-            t_ref[g, at : at + ROWS] = (cosine * pltpu.reciprocal(q + OFFSET * TURN, approx=True)).astype(BF16)
+            t_ref[g, at : at + ROWS] = cosine * pltpu.reciprocal(q + OFFSET * TURN, approx=True)
 
     def product(chunk, g, t_ref):
         source0, box0, count0 = pair_at(chunk, g, 0)
         source1, box1, count1 = pair_at(chunk, g, 1)
-        currents = jnp.where(upper, win_ref[source0].astype(F32), win_ref[source1 ^ 1].astype(F32)).astype(BF16)
+        currents = jnp.where(upper, win_ref[source0].astype(F32), win_ref[source1 ^ 1].astype(F32))
         got = nn_dot(currents, t_ref[g])
         out_ref[box0] += count0.astype(F32) * got[:waves, :width]
         out_ref[box1] += count1.astype(F32) * got[waves:, width:]
@@ -553,8 +569,8 @@
     near_scratch = [
         pltpu.VMEM((ITEMS, width, 2 * width), F32),
         pltpu.VMEM((ITEMS, width, 2 * width), F32),
-        pltpu.VMEM((ITEMS, width, 2 * width), BF16),
-        pltpu.VMEM((ITEMS, width, 2 * width), BF16),
+        pltpu.VMEM((ITEMS, width, 2 * width), F32),
+        pltpu.VMEM((ITEMS, width, 2 * width), F32),
     ]
     first_sum, observers, sources, ordered, gains = pl.pallas_call(
         functools.partial(prepare_kernel, entries),

time: 30.1 us -> 29.6 us (0.983)
    pallas_call x1, Pallas kernels: 7.21 us -> 6.38 us  [per_device(): pl.pallas_call(functools.partial(incoming_kernel, entries, len(packets) -...]
    pallas_call x1, Pallas kernels: 6.24 us -> 7.06 us  [per_device(): pl.pallas_call(functools.partial(near_kernel, entries), out_shape=(shaped...]
  transfers between devices with their start and end apart: 5 -> 5, of which waited for: 0 -> 0; matrix products, arithmetic and copies ran while one was open for 0% -> 0% of each run, Pallas kernels for 39% -> 42%
where the time goes in v8:
time: 29.6 us; the launch traced here: 29.7 us
  Pallas kernels  20.6 us (70%)
  starting transfers between devices  9.05 us (31%)
    ppermute x5, starting transfers between devices, swapped(): lax.ppermute(x, axis, [way for i, j in pairs for way in ((i, j), (j, i))])  9.05 us
    pallas_call x1, Pallas kernels, per_device(): pl.pallas_call(functools.partial(near_kernel, entries), out_shape=(shaped...  7.06 us
    pallas_call x1, Pallas kernels, per_device(): pl.pallas_call(functools.partial(incoming_kernel, entries, len(packets) -...  6.38 us
    pallas_call x1, Pallas kernels, per_device(): pl.pallas_call(functools.partial(prepare_kernel, entries), out_shape=(sha...  5.39 us
    pallas_call x1, Pallas kernels, per_device(): pl.pallas_call(outgoing_kernel, out_shape=(shaped((own_rows + spectra_row...  1.75 us
  transfers between devices with their start and end apart: 5, of which 0 were waited for; matrix products, arithmetic and copies ran while one was open for 0% of the time, Pallas kernels for 42%

profile of v8, /device:TPU:1, one launch (start us, length us, event | category | flops | bytes accessed | tf_op | source)
XLA Modules:
  0.0 29.7 jit_solution(13103189971514872688)
XLA Ops:
  0.0 1.7 %outgoing.1 = (bf16[19,16,128]{2,1,0:T(8,128)(2,1)S(1)}, bf16[8,16,128]{2,1,0:T(8,128)(2,1)S(1)}, bf16[128,512]{1,0:T(8,128)(2,1)S(1)}, f32[8,512]{1,0:T(8,128)S...) custom-call(bf16[8,16,128]{2,1,0:T(8,128)(2,1)} %bitcast.4, ...), custom_call_target="tpu_custom_call" | custom-call | tf_op jit(solution)/shard_map/outgoing/pallas_call | solution.py:544
  1.8 4.2 %collective-permute-start = (bf16[19,16,128]{2,1,0:T(8,128)(2,1)S(1)}, bf16[19,16,128]{2,1,0:T(8,128)(2,1)S(1)}, u32[]{:S(2)}, u32[]{:S(2)}) collective-permute-start(bf16[19,16,128]{2,1,0:T(8,128)(2,1)S(1)} %get-tuple-element.18.own_ref), channel_id=1, source_target_pairs={{0,3},{3,0},{1,2},{2,1},{4,7},{7,4},{5,6},{6,5},{8,11},{11,8},{9,1... | collective-permute-start | bytes 233480 | tf_op jit(solution)/shard_map/ppermute | solution.py:40
  6.0 0.0 collective-permute-start.1
  6.0 0.4 %collective-permute-start.2 = (bf16[8,16,128]{2,1,0:T(8,128)(2,1)S(1)}, bf16[8,16,128]{2,1,0:T(8,128)(2,1)S(1)}, u32[]{:S(2)}, u32[]{:S(2)}) collective-permute-start(bf16[8,16,128]{2,1,0:T(8,128)(2,1)S(1)} %get-tuple-element.20.own_ref), channel_id=1, source_target_pairs={{0,2},{2,0},{1,3},{3,1},{4,6},{6,4},{5,7},{7,5},{8,10},{10,8},{9,1... | collective-permute-start | bytes 98312 | tf_op jit(solution)/shard_map/ppermute | solution.py:40
  6.3 5.4 %prepare.1 = (f32[16,8,128]{2,1,0:T(8,128)S(1)}, bf16[16,16,128]{2,1,0:T(8,128)(2,1)S(1)}, bf16[48,128,128]{2,1,0:T(8,128)(2,1)S(1)}, bf16[48,16,128]{2,1,0:T(8,128)(2,1)S(1)}, f32[2,24,2,512]{3,2,1,0:T(2,128)S(1)}) custom-call(bf16[19,16,128]{2,1,0:T(8,128)(2,1)S(1)} %get-tuple-element.18.own_ref, s32[1,384]{1,0:T(1,128)S(1)} %get-tuple-element.19.items_ref.refs_1_, ...), custom_call_target="tpu_custom_call" | custom-call | tf_op jit(solution)/shard_map/prepare/pallas_call | solution.py:575
  11.7 0.0 collective-permute-done.2.refs_1_
  11.8 0.0 collective-permute-done.refs_2_.refs_1_.refs_0_
  11.8 0.0 collective-permute-done.1.refs_0_
  11.8 1.3 %collective-permute-start.3 = (bf16[43,16,128]{2,1,0:T(8,128)(2,1)S(1)}, bf16[43,16,128]{2,1,0:T(8,128)(2,1)S(1)}, u32[]{:S(2)}, u32[]{:S(2)}) collective-permute-start(bf16[43,16,128]{2,1,0:T(8,128)(2,1)S(1)} %group.1.refs_3_), channel_id=1, source_target_pairs={{0,4},{4,0},{8,12},{12,8},{16,20},{20,16},{24,28},{28,24},{1,5},{5... | collective-permute-start | bytes 528392 | tf_op jit(solution)/shard_map/ppermute | solution.py:40
  13.1 3.2 %collective-permute-start.4 = (bf16[43,16,128]{2,1,0:T(8,128)(2,1)S(1)}, bf16[43,16,128]{2,1,0:T(8,128)(2,1)S(1)}, u32[]{:S(2)}, u32[]{:S(2)}) collective-permute-start(bf16[43,16,128]{2,1,0:T(8,128)(2,1)S(1)} %group.1.refs_3_), channel_id=1, source_target_pairs={{4,8},{8,4},{12,16},{16,12},{20,24},{24,20},{5,9},{9,5},{13,17},{1... | collective-permute-start | bytes 528392 | tf_op jit(solution)/shard_map/ppermute | solution.py:40
  16.3 7.1 %near.1 = (f32[16,8,128]{2,1,0:T(8,128)S(1)}, bf16[48,128,128]{2,1,0:T(8,128)(2,1)S(1)}, bf16[48,16,128]{2,1,0:T(8,128)(2,1)S(1)}) custom-call(s32[1,384]{1,0:T(1,128)S(1)} %get-tuple-element.19.items_ref.refs_1_, bf16[19,16,128]{2,1,0:T(8,128)(2,1)S(1)} %collective-permute-done.1.refs_0_, ...), custom_call_target="tpu_custom_call", output_to_operand_aliasing={{1}: (5, {}), {2}: (6, {})} | custom-call | tf_op jit(solution)/shard_map/near/pallas_call | solution.py:612
  23.3 0.0 collective-permute-done.3.refs_2_
  23.4 0.0 collective-permute-done.4.refs_4_
  23.4 6.4 %incoming.1 = f32[16,8,128]{2,1,0:T(8,128)} custom-call(bf16[19,16,128]{2,1,0:T(8,128)(2,1)S(1)} %collective-permute-done.refs_2_.refs_1_.refs_0_, s32[1,384]{1,0:T(1,128)S(1)} %get-tuple-element.19.items_ref.refs_1_, bf16[43,16,128]{2,1,0:T(8,128)(2,1)S(1)} %collective-permute-done.3.refs_2_, bf16[43,16,128]{2,1,0:T(8,128)(2,1)S(1)} %group.1.refs_3_, ...), custom_call_target="tpu_custom_call" | custom-call | tf_op jit(solution)/shard_map/incoming/pallas_call | solution.py:627
  (1 shorter events, 0.0 us)
Async XLA Ops:
  1.8 10.0 %collective-permute-start = (bf16[19,16,128]{2,1,0:T(8,128)(2,1)S(1)}, bf16[19,16,128]{2,1,0:T(8,128)(2,1)S(1)}, u32[]{:S(2)}, u32[]{:S(2)}) collective-permute-start(bf16[19,16,128]{2,1,0:T(8,128)(2,1)S(1)} %get-tuple-element.18.own_ref), channel_id=1, source_target_pairs={{0,3},{3,0},{1,2},{2,1},{4,7},{7,4},{5,6},{6,5},{8,11},{11,8},{9,1... | collective-permute-start | bytes 233480 | tf_op jit(solution)/shard_map/ppermute | solution.py:40
  6.0 5.8 %collective-permute-start.1 = (bf16[19,16,128]{2,1,0:T(8,128)(2,1)S(1)}, bf16[19,16,128]{2,1,0:T(8,128)(2,1)S(1)}, u32[]{:S(2)}, u32[]{:S(2)}) collective-permute-start(bf16[19,16,128]{2,1,0:T(8,128)(2,1)S(1)} %get-tuple-element.18.own_ref), channel_id=1, source_target_pairs={{0,1},{1,0},{2,3},{3,2},{4,5},{5,4},{6,7},{7,6},{8,9},{9,8},{10,11... | collective-permute-start | bytes 233480 | tf_op jit(solution)/shard_map/ppermute | solution.py:40
  6.0 5.8 %collective-permute-start.2 = (bf16[8,16,128]{2,1,0:T(8,128)(2,1)S(1)}, bf16[8,16,128]{2,1,0:T(8,128)(2,1)S(1)}, u32[]{:S(2)}, u32[]{:S(2)}) collective-permute-start(bf16[8,16,128]{2,1,0:T(8,128)(2,1)S(1)} %get-tuple-element.20.own_ref), channel_id=1, source_target_pairs={{0,2},{2,0},{1,3},{3,1},{4,6},{6,4},{5,7},{7,5},{8,10},{10,8},{9,1... | collective-permute-start | bytes 98312 | tf_op jit(solution)/shard_map/ppermute | solution.py:40
  11.8 11.6 %collective-permute-start.3 = (bf16[43,16,128]{2,1,0:T(8,128)(2,1)S(1)}, bf16[43,16,128]{2,1,0:T(8,128)(2,1)S(1)}, u32[]{:S(2)}, u32[]{:S(2)}) collective-permute-start(bf16[43,16,128]{2,1,0:T(8,128)(2,1)S(1)} %group.1.refs_3_), channel_id=1, source_target_pairs={{0,4},{4,0},{8,12},{12,8},{16,20},{20,16},{24,28},{28,24},{1,5},{5... | collective-permute-start | bytes 528392 | tf_op jit(solution)/shard_map/ppermute | solution.py:40
  13.1 10.3 %collective-permute-start.4 = (bf16[43,16,128]{2,1,0:T(8,128)(2,1)S(1)}, bf16[43,16,128]{2,1,0:T(8,128)(2,1)S(1)}, u32[]{:S(2)}, u32[]{:S(2)}) collective-permute-start(bf16[43,16,128]{2,1,0:T(8,128)(2,1)S(1)} %group.1.refs_3_), channel_id=1, source_target_pairs={{4,8},{8,4},{12,16},{16,12},{20,24},{24,20},{5,9},{9,5},{13,17},{1... | collective-permute-start | bytes 528392 | tf_op jit(solution)/shard_map/ppermute | solution.py:40

commit v9 on v8

--- a/solution.py
+++ b/solution.py
@@ -256,10 +256,9 @@
 
 def take_currents(x_rows, win_ref, start):
     for k in range(x_rows.shape[0]):
-        both = x_rows[k]
-        wide = both.astype(F32)
-        win_ref[start + 2 * k] = both
-        win_ref[start + 2 * k + 1] = jnp.concatenate([wide[8:], wide[:8]], axis=0).astype(BF16)
+        both = x_rows[k].astype(F32)
+        win_ref[start + 2 * k] = both[:8]
+        win_ref[start + 2 * k + 1] = both[8:]
 
 
 def near_sum(entries, total, item_at, first_source, src_ref, win_ref, obs_ref, out_ref, scratch, ahead=0):
@@ -268,9 +267,9 @@
     count_bits, box_bits, source_bits = code_bits(boxes, entries)
     pair_bits = count_bits + box_bits + source_bits
     t1_ref[...] = jnp.zeros(t1_ref.shape, F32)
-    upper = lax.broadcasted_iota(jnp.int32, (2 * waves, width), 0) < waves
     left = lax.broadcasted_iota(jnp.int32, (width, 128), 1) < 16
     empty = jnp.zeros((16, width), BF16)
+    below = jnp.zeros((128 - 32, 2 * width), BF16)
 
     def pair_at(chunk, g, slot):
         code = item_at(chunk * ITEMS + g) >> (slot * pair_bits)
@@ -287,10 +286,11 @@
             [
                 jnp.concatenate([obs_ref[box0], empty], axis=1),
                 jnp.concatenate([empty, obs_ref[box1]], axis=1),
+                below,
             ],
             axis=0,
         )
-        u_ref[g] = nn_dot(sources[:, :32], observers)
+        u_ref[g] = nn_dot(sources, observers)
 
     def tile(g, u_ref, t_ref):
         for at in range(0, width, ROWS):
@@ -305,7 +305,7 @@
     def product(chunk, g, t_ref):
         source0, box0, count0 = pair_at(chunk, g, 0)
         source1, box1, count1 = pair_at(chunk, g, 1)
-        currents = jnp.where(upper, win_ref[source0].astype(F32), win_ref[source1 ^ 1].astype(F32))
+        currents = jnp.concatenate([win_ref[source0], win_ref[source1]], axis=0)
         got = nn_dot(currents, t_ref[g])
         out_ref[box0] += count0.astype(F32) * got[:waves, :width]
         out_ref[box1] += count1.astype(F32) * got[waves:, width:]
@@ -578,7 +578,7 @@
             shaped((boxes, waves, width), F32),
             shaped((boxes, 16, width), BF16),
             shaped((3 * boxes, width, 128), BF16),
-            shaped((3 * boxes, 16, width), BF16),
+            shaped((3 * boxes, waves, width), F32),
             shaped((parents, window, 2, parent_dirs), F32),
         ),
         in_specs=[vmem] * 2 + [hbm] * 4,
@@ -614,7 +614,7 @@
         out_shape=(
             shaped((boxes, waves, width), F32),
             shaped(sources.shape, BF16),
-            shaped(ordered.shape, BF16),
+            shaped(ordered.shape, F32),
         ),
         in_specs=[vmem] * (5 + len(packets)),
         out_specs=(vmem,) * 3,
@@ -631,7 +631,7 @@
         out_specs=vmem,
         scratch_shapes=[
             pltpu.VMEM((boxes, waves, width), F32),
-            pltpu.VMEM((boxes, 16, width), BF16),
+            pltpu.VMEM((boxes, waves, width), F32),
             pltpu.VMEM((boxes, width, 128), BF16),
             pltpu.VMEM((boxes * waves, parent_dirs), F32),
             pltpu.VMEM((boxes * waves, parent_dirs), F32),

time: 29.6 us -> 29.8 us (level); the launches traced: 29.7 us -> 29.6 us
    pallas_call x1, Pallas kernels: 6.38 us -> 5.98 us  [per_device(): pl.pallas_call(functools.partial(incoming_kernel, entries, len(packets) -...]
    pallas_call x1, Pallas kernels: 7.06 us -> 7.36 us  [per_device(): pl.pallas_call(functools.partial(near_kernel, entries), out_shape=(shaped...]
  transfers between devices with their start and end apart: 5 -> 5, of which waited for: 0 -> 0; matrix products, arithmetic and copies ran while one was open for 0% -> 0% of each run, Pallas kernels for 42% -> 43%
where the time goes in v9:
time: 29.8 us; the launch traced here: 29.6 us
  Pallas kernels  20.5 us (69%)
  starting transfers between devices  9.06 us (30%)
    ppermute x5, starting transfers between devices, swapped(): lax.ppermute(x, axis, [way for i, j in pairs for way in ((i, j), (j, i))])  9.06 us
    pallas_call x1, Pallas kernels, per_device(): pl.pallas_call(functools.partial(near_kernel, entries), out_shape=(shaped...  7.36 us
    pallas_call x1, Pallas kernels, per_device(): pl.pallas_call(functools.partial(incoming_kernel, entries, len(packets) -...  5.98 us
    pallas_call x1, Pallas kernels, per_device(): pl.pallas_call(functools.partial(prepare_kernel, entries), out_shape=(sha...  5.37 us
    pallas_call x1, Pallas kernels, per_device(): pl.pallas_call(outgoing_kernel, out_shape=(shaped((own_rows + spectra_row...  1.75 us
  transfers between devices with their start and end apart: 5, of which 0 were waited for; matrix products, arithmetic and copies ran while one was open for 0% of the time, Pallas kernels for 43%

profile of v9, /device:TPU:1, one launch (start us, length us, event | category | flops | bytes accessed | tf_op | source)
XLA Modules:
  0.0 29.6 jit_solution(17251214794427010208)
XLA Ops:
  0.0 1.7 %outgoing.1 = (bf16[19,16,128]{2,1,0:T(8,128)(2,1)S(1)}, bf16[8,16,128]{2,1,0:T(8,128)(2,1)S(1)}, bf16[128,512]{1,0:T(8,128)(2,1)S(1)}, f32[8,512]{1,0:T(8,128)S...) custom-call(bf16[8,16,128]{2,1,0:T(8,128)(2,1)} %bitcast.4, ...), custom_call_target="tpu_custom_call" | custom-call | tf_op jit(solution)/shard_map/outgoing/pallas_call | solution.py:544
  1.8 4.2 %collective-permute-start = (bf16[19,16,128]{2,1,0:T(8,128)(2,1)S(1)}, bf16[19,16,128]{2,1,0:T(8,128)(2,1)S(1)}, u32[]{:S(2)}, u32[]{:S(2)}) collective-permute-start(bf16[19,16,128]{2,1,0:T(8,128)(2,1)S(1)} %get-tuple-element.18.own_ref), channel_id=1, source_target_pairs={{0,3},{3,0},{1,2},{2,1},{4,7},{7,4},{5,6},{6,5},{8,11},{11,8},{9,1... | collective-permute-start | bytes 233480 | tf_op jit(solution)/shard_map/ppermute | solution.py:40
  6.0 0.0 collective-permute-start.1
  6.0 0.4 %collective-permute-start.2 = (bf16[8,16,128]{2,1,0:T(8,128)(2,1)S(1)}, bf16[8,16,128]{2,1,0:T(8,128)(2,1)S(1)}, u32[]{:S(2)}, u32[]{:S(2)}) collective-permute-start(bf16[8,16,128]{2,1,0:T(8,128)(2,1)S(1)} %get-tuple-element.20.own_ref), channel_id=1, source_target_pairs={{0,2},{2,0},{1,3},{3,1},{4,6},{6,4},{5,7},{7,5},{8,10},{10,8},{9,1... | collective-permute-start | bytes 98312 | tf_op jit(solution)/shard_map/ppermute | solution.py:40
  6.3 5.4 %prepare.1 = (f32[16,8,128]{2,1,0:T(8,128)S(1)}, bf16[16,16,128]{2,1,0:T(8,128)(2,1)S(1)}, bf16[48,128,128]{2,1,0:T(8,128)(2,1)S(1)}, f32[48,8,128]{2,1,0:T(8,128)S(1)}, f32[2,24,2,512]{3,2,1,0:T(2,128)S(1)}) custom-call(bf16[19,16,128]{2,1,0:T(8,128)(2,1)S(1)} %get-tuple-element.18.own_ref, s32[1,384]{1,0:T(1,128)S(1)} %get-tuple-element.19.items_ref.refs_1_, ...), custom_call_target="tpu_custom_call" | custom-call | tf_op jit(solution)/shard_map/prepare/pallas_call | solution.py:575
  11.7 0.0 collective-permute-done.2.refs_1_
  11.7 0.0 collective-permute-done.refs_2_.refs_1_.refs_0_
  11.7 0.0 collective-permute-done.1.refs_0_
  11.8 1.3 %collective-permute-start.3 = (bf16[43,16,128]{2,1,0:T(8,128)(2,1)S(1)}, bf16[43,16,128]{2,1,0:T(8,128)(2,1)S(1)}, u32[]{:S(2)}, u32[]{:S(2)}) collective-permute-start(bf16[43,16,128]{2,1,0:T(8,128)(2,1)S(1)} %group.1.refs_3_), channel_id=1, source_target_pairs={{0,4},{4,0},{8,12},{12,8},{16,20},{20,16},{24,28},{28,24},{1,5},{5... | collective-permute-start | bytes 528392 | tf_op jit(solution)/shard_map/ppermute | solution.py:40
  13.1 3.2 %collective-permute-start.4 = (bf16[43,16,128]{2,1,0:T(8,128)(2,1)S(1)}, bf16[43,16,128]{2,1,0:T(8,128)(2,1)S(1)}, u32[]{:S(2)}, u32[]{:S(2)}) collective-permute-start(bf16[43,16,128]{2,1,0:T(8,128)(2,1)S(1)} %group.1.refs_3_), channel_id=1, source_target_pairs={{4,8},{8,4},{12,16},{16,12},{20,24},{24,20},{5,9},{9,5},{13,17},{1... | collective-permute-start | bytes 528392 | tf_op jit(solution)/shard_map/ppermute | solution.py:40
  16.3 7.4 %near.1 = (f32[16,8,128]{2,1,0:T(8,128)S(1)}, bf16[48,128,128]{2,1,0:T(8,128)(2,1)S(1)}, f32[48,8,128]{2,1,0:T(8,128)S(1)}) custom-call(s32[1,384]{1,0:T(1,128)S(1)} %get-tuple-element.19.items_ref.refs_1_, bf16[19,16,128]{2,1,0:T(8,128)(2,1)S(1)} %collective-permute-done.1.refs_0_, ...), custom_call_target="tpu_custom_call", output_to_operand_aliasing={{1}: (5, {}), {2}: (6, {})} | custom-call | tf_op jit(solution)/shard_map/near/pallas_call | solution.py:612
  23.6 0.0 collective-permute-done.3.refs_2_
  23.6 0.0 collective-permute-done.4.refs_4_
  23.7 6.0 %incoming.1 = f32[16,8,128]{2,1,0:T(8,128)} custom-call(bf16[19,16,128]{2,1,0:T(8,128)(2,1)S(1)} %collective-permute-done.refs_2_.refs_1_.refs_0_, s32[1,384]{1,0:T(1,128)S(1)} %get-tuple-element.19.items_ref.refs_1_, bf16[43,16,128]{2,1,0:T(8,128)(2,1)S(1)} %collective-permute-done.3.refs_2_, bf16[43,16,128]{2,1,0:T(8,128)(2,1)S(1)} %group.1.refs_3_, ...), custom_call_target="tpu_custom_call" | custom-call | tf_op jit(solution)/shard_map/incoming/pallas_call | solution.py:627
  (1 shorter events, 0.0 us)
Async XLA Ops:
  1.8 10.0 %collective-permute-start = (bf16[19,16,128]{2,1,0:T(8,128)(2,1)S(1)}, bf16[19,16,128]{2,1,0:T(8,128)(2,1)S(1)}, u32[]{:S(2)}, u32[]{:S(2)}) collective-permute-start(bf16[19,16,128]{2,1,0:T(8,128)(2,1)S(1)} %get-tuple-element.18.own_ref), channel_id=1, source_target_pairs={{0,3},{3,0},{1,2},{2,1},{4,7},{7,4},{5,6},{6,5},{8,11},{11,8},{9,1... | collective-permute-start | bytes 233480 | tf_op jit(solution)/shard_map/ppermute | solution.py:40
  6.0 5.8 %collective-permute-start.1 = (bf16[19,16,128]{2,1,0:T(8,128)(2,1)S(1)}, bf16[19,16,128]{2,1,0:T(8,128)(2,1)S(1)}, u32[]{:S(2)}, u32[]{:S(2)}) collective-permute-start(bf16[19,16,128]{2,1,0:T(8,128)(2,1)S(1)} %get-tuple-element.18.own_ref), channel_id=1, source_target_pairs={{0,1},{1,0},{2,3},{3,2},{4,5},{5,4},{6,7},{7,6},{8,9},{9,8},{10,11... | collective-permute-start | bytes 233480 | tf_op jit(solution)/shard_map/ppermute | solution.py:40
  6.0 5.7 %collective-permute-start.2 = (bf16[8,16,128]{2,1,0:T(8,128)(2,1)S(1)}, bf16[8,16,128]{2,1,0:T(8,128)(2,1)S(1)}, u32[]{:S(2)}, u32[]{:S(2)}) collective-permute-start(bf16[8,16,128]{2,1,0:T(8,128)(2,1)S(1)} %get-tuple-element.20.own_ref), channel_id=1, source_target_pairs={{0,2},{2,0},{1,3},{3,1},{4,6},{6,4},{5,7},{7,5},{8,10},{10,8},{9,1... | collective-permute-start | bytes 98312 | tf_op jit(solution)/shard_map/ppermute | solution.py:40
  11.8 11.9 %collective-permute-start.3 = (bf16[43,16,128]{2,1,0:T(8,128)(2,1)S(1)}, bf16[43,16,128]{2,1,0:T(8,128)(2,1)S(1)}, u32[]{:S(2)}, u32[]{:S(2)}) collective-permute-start(bf16[43,16,128]{2,1,0:T(8,128)(2,1)S(1)} %group.1.refs_3_), channel_id=1, source_target_pairs={{0,4},{4,0},{8,12},{12,8},{16,20},{20,16},{24,28},{28,24},{1,5},{5... | collective-permute-start | bytes 528392 | tf_op jit(solution)/shard_map/ppermute | solution.py:40
  13.1 10.6 %collective-permute-start.4 = (bf16[43,16,128]{2,1,0:T(8,128)(2,1)S(1)}, bf16[43,16,128]{2,1,0:T(8,128)(2,1)S(1)}, u32[]{:S(2)}, u32[]{:S(2)}) collective-permute-start(bf16[43,16,128]{2,1,0:T(8,128)(2,1)S(1)} %group.1.refs_3_), channel_id=1, source_target_pairs={{4,8},{8,4},{12,16},{16,12},{20,24},{24,20},{5,9},{9,5},{13,17},{1... | collective-permute-start | bytes 528392 | tf_op jit(solution)/shard_map/ppermute | solution.py:40

commit v10 on v9

--- a/solution.py
+++ b/solution.py
@@ -269,7 +269,6 @@
     t1_ref[...] = jnp.zeros(t1_ref.shape, F32)
     left = lax.broadcasted_iota(jnp.int32, (width, 128), 1) < 16
     empty = jnp.zeros((16, width), BF16)
-    below = jnp.zeros((128 - 32, 2 * width), BF16)
 
     def pair_at(chunk, g, slot):
         code = item_at(chunk * ITEMS + g) >> (slot * pair_bits)
@@ -286,11 +285,10 @@
             [
                 jnp.concatenate([obs_ref[box0], empty], axis=1),
                 jnp.concatenate([empty, obs_ref[box1]], axis=1),
-                below,
             ],
             axis=0,
         )
-        u_ref[g] = nn_dot(sources, observers)
+        u_ref[g] = nn_dot(sources[:, :32], observers)
 
     def tile(g, u_ref, t_ref):
         for at in range(0, width, ROWS):
@@ -437,7 +435,7 @@
 
 def incoming(
     entries, items_ref, even_ref, own_ref, odd_ref, gain_ref, cos_ref, sin_ref, imat_ref, rad_ref, obs_ref, near_ref, out_ref,
-    sum_ref, win_ref, src_ref, down_re_ref, down_im_ref, list_ref, u0_ref, u1_ref, t0_ref, t1_ref, sem, other_refs=()
+    sum_ref, win_ref, src_ref, down_ref, list_ref, u0_ref, u1_ref, t0_ref, t1_ref, sem, other_refs=()
 ):
     parents, window, _, parent_dirs = gain_ref.shape
     boxes, waves, width = near_ref.shape
@@ -492,12 +490,12 @@
             for c in range(8):
                 cos, sin = cos_phase[c : c + 1, lanes], sin_phase[c : c + 1, lanes]
                 rows = slice((q * 8 + c) * waves, (q * 8 + c + 1) * waves)
-                down_re_ref[rows, lanes] = cos * re + sin * im
-                down_im_ref[rows, lanes] = cos * im - sin * re
+                down_ref[0, rows, lanes] = cos * re + sin * im
+                down_ref[1, rows, lanes] = cos * im - sin * re
     imat = imat_ref[...]
-    in_re = nt_dot(down_re_ref[...].astype(BF16), imat)
-    in_im = nt_dot(down_im_ref[...].astype(BF16), imat)
-    incoming = jnp.concatenate([in_re, in_im], axis=1).astype(BF16)
+    rows = boxes * waves
+    both = nt_dot(down_ref[...].reshape(2 * rows, parent_dirs).astype(BF16), imat)
+    incoming = jnp.concatenate([both[:rows], both[rows:]], axis=1).astype(BF16)
     far = nt_dot(incoming, rad_ref[...])
     near_sum(
         entries,
@@ -633,8 +631,7 @@
             pltpu.VMEM((boxes, waves, width), F32),
             pltpu.VMEM((boxes, waves, width), F32),
             pltpu.VMEM((boxes, width, 128), BF16),
-            pltpu.VMEM((boxes * waves, parent_dirs), F32),
-            pltpu.VMEM((boxes * waves, parent_dirs), F32),
+            pltpu.VMEM((2, boxes * waves, parent_dirs), F32),
             pltpu.SMEM((1, length), jnp.int32),
         ]
         + near_scratch

time: 29.8 us -> 29.2 us (0.980); the launches traced: 29.6 us -> 28.6 us
  Pallas kernels: 20.5 us -> 19.5 us
    pallas_call x1, Pallas kernels: 7.36 us -> 6.02 us  [per_device(): pl.pallas_call(functools.partial(near_kernel, entries), out_shape=(shaped...]
    pallas_call x1, Pallas kernels: 5.98 us -> 6.35 us  [per_device(): pl.pallas_call(functools.partial(incoming_kernel, entries, len(packets) -...]
  transfers between devices with their start and end apart: 5 -> 5, of which waited for: 0 -> 0; matrix products, arithmetic and copies ran while one was open for 0% -> 0% of each run, Pallas kernels for 43% -> 40%
where the time goes in v10:
time: 29.2 us; the launch traced here: 28.6 us
  Pallas kernels  19.5 us (67%)
  starting transfers between devices  9.05 us (31%)
    ppermute x5, starting transfers between devices, swapped(): lax.ppermute(x, axis, [way for i, j in pairs for way in ((i, j), (j, i))])  9.05 us
    pallas_call x1, Pallas kernels, per_device(): pl.pallas_call(functools.partial(incoming_kernel, entries, len(packets) -...  6.35 us
    pallas_call x1, Pallas kernels, per_device(): pl.pallas_call(functools.partial(near_kernel, entries), out_shape=(shaped...  6.02 us
    pallas_call x1, Pallas kernels, per_device(): pl.pallas_call(functools.partial(prepare_kernel, entries), out_shape=(sha...  5.36 us
    pallas_call x1, Pallas kernels, per_device(): pl.pallas_call(outgoing_kernel, out_shape=(shaped((own_rows + spectra_row...  1.75 us
  transfers between devices with their start and end apart: 5, of which 0 were waited for; matrix products, arithmetic and copies ran while one was open for 0% of the time, Pallas kernels for 40%

profile of v10, /device:TPU:1, one launch (start us, length us, event | category | flops | bytes accessed | tf_op | source)
XLA Modules:
  0.0 28.6 jit_solution(907892445409440482)
XLA Ops:
  0.0 1.7 %outgoing.1 = (bf16[19,16,128]{2,1,0:T(8,128)(2,1)S(1)}, bf16[8,16,128]{2,1,0:T(8,128)(2,1)S(1)}, bf16[128,512]{1,0:T(8,128)(2,1)S(1)}, f32[8,512]{1,0:T(8,128)S...) custom-call(bf16[8,16,128]{2,1,0:T(8,128)(2,1)} %bitcast.4, ...), custom_call_target="tpu_custom_call" | custom-call | tf_op jit(solution)/shard_map/outgoing/pallas_call | solution.py:542
  1.8 4.2 %collective-permute-start = (bf16[19,16,128]{2,1,0:T(8,128)(2,1)S(1)}, bf16[19,16,128]{2,1,0:T(8,128)(2,1)S(1)}, u32[]{:S(2)}, u32[]{:S(2)}) collective-permute-start(bf16[19,16,128]{2,1,0:T(8,128)(2,1)S(1)} %get-tuple-element.18.own_ref), channel_id=1, source_target_pairs={{0,3},{3,0},{1,2},{2,1},{4,7},{7,4},{5,6},{6,5},{8,11},{11,8},{9,1... | collective-permute-start | bytes 233480 | tf_op jit(solution)/shard_map/ppermute | solution.py:40
  6.0 0.0 collective-permute-start.1
  6.0 0.4 %collective-permute-start.2 = (bf16[8,16,128]{2,1,0:T(8,128)(2,1)S(1)}, bf16[8,16,128]{2,1,0:T(8,128)(2,1)S(1)}, u32[]{:S(2)}, u32[]{:S(2)}) collective-permute-start(bf16[8,16,128]{2,1,0:T(8,128)(2,1)S(1)} %get-tuple-element.20.own_ref), channel_id=1, source_target_pairs={{0,2},{2,0},{1,3},{3,1},{4,6},{6,4},{5,7},{7,5},{8,10},{10,8},{9,1... | collective-permute-start | bytes 98312 | tf_op jit(solution)/shard_map/ppermute | solution.py:40
  6.3 5.4 %prepare.1 = (f32[16,8,128]{2,1,0:T(8,128)S(1)}, bf16[16,16,128]{2,1,0:T(8,128)(2,1)S(1)}, bf16[48,128,128]{2,1,0:T(8,128)(2,1)S(1)}, f32[48,8,128]{2,1,0:T(8,128)S(1)}, f32[2,24,2,512]{3,2,1,0:T(2,128)S(1)}) custom-call(bf16[19,16,128]{2,1,0:T(8,128)(2,1)S(1)} %get-tuple-element.18.own_ref, s32[1,384]{1,0:T(1,128)S(1)} %get-tuple-element.19.items_ref.refs_1_, ...), custom_call_target="tpu_custom_call" | custom-call | tf_op jit(solution)/shard_map/prepare/pallas_call | solution.py:573
  11.7 0.0 collective-permute-done.2.refs_1_
  11.7 0.0 collective-permute-done.refs_2_.refs_1_.refs_0_
  11.7 0.0 collective-permute-done.1.refs_0_
  11.8 1.3 %collective-permute-start.3 = (bf16[43,16,128]{2,1,0:T(8,128)(2,1)S(1)}, bf16[43,16,128]{2,1,0:T(8,128)(2,1)S(1)}, u32[]{:S(2)}, u32[]{:S(2)}) collective-permute-start(bf16[43,16,128]{2,1,0:T(8,128)(2,1)S(1)} %group.1.refs_3_), channel_id=1, source_target_pairs={{0,4},{4,0},{8,12},{12,8},{16,20},{20,16},{24,28},{28,24},{1,5},{5... | collective-permute-start | bytes 528392 | tf_op jit(solution)/shard_map/ppermute | solution.py:40
  13.1 3.2 %collective-permute-start.4 = (bf16[43,16,128]{2,1,0:T(8,128)(2,1)S(1)}, bf16[43,16,128]{2,1,0:T(8,128)(2,1)S(1)}, u32[]{:S(2)}, u32[]{:S(2)}) collective-permute-start(bf16[43,16,128]{2,1,0:T(8,128)(2,1)S(1)} %group.1.refs_3_), channel_id=1, source_target_pairs={{4,8},{8,4},{12,16},{16,12},{20,24},{24,20},{5,9},{9,5},{13,17},{1... | collective-permute-start | bytes 528392 | tf_op jit(solution)/shard_map/ppermute | solution.py:40
  16.2 6.0 %near.1 = (f32[16,8,128]{2,1,0:T(8,128)S(1)}, bf16[48,128,128]{2,1,0:T(8,128)(2,1)S(1)}, f32[48,8,128]{2,1,0:T(8,128)S(1)}) custom-call(s32[1,384]{1,0:T(1,128)S(1)} %get-tuple-element.19.items_ref.refs_1_, bf16[19,16,128]{2,1,0:T(8,128)(2,1)S(1)} %collective-permute-done.1.refs_0_, ...), custom_call_target="tpu_custom_call", output_to_operand_aliasing={{1}: (5, {}), {2}: (6, {})} | custom-call | tf_op jit(solution)/shard_map/near/pallas_call | solution.py:610
  22.3 0.0 collective-permute-done.3.refs_2_
  22.3 0.0 collective-permute-done.4.refs_4_
  22.3 6.4 %incoming.1 = f32[16,8,128]{2,1,0:T(8,128)} custom-call(bf16[19,16,128]{2,1,0:T(8,128)(2,1)S(1)} %collective-permute-done.refs_2_.refs_1_.refs_0_, s32[1,384]{1,0:T(1,128)S(1)} %get-tuple-element.19.items_ref.refs_1_, bf16[43,16,128]{2,1,0:T(8,128)(2,1)S(1)} %collective-permute-done.3.refs_2_, bf16[43,16,128]{2,1,0:T(8,128)(2,1)S(1)} %group.1.refs_3_, ...), custom_call_target="tpu_custom_call" | custom-call | tf_op jit(solution)/shard_map/incoming/pallas_call | solution.py:625
  (1 shorter events, 0.0 us)
Async XLA Ops:
  1.8 10.0 %collective-permute-start = (bf16[19,16,128]{2,1,0:T(8,128)(2,1)S(1)}, bf16[19,16,128]{2,1,0:T(8,128)(2,1)S(1)}, u32[]{:S(2)}, u32[]{:S(2)}) collective-permute-start(bf16[19,16,128]{2,1,0:T(8,128)(2,1)S(1)} %get-tuple-element.18.own_ref), channel_id=1, source_target_pairs={{0,3},{3,0},{1,2},{2,1},{4,7},{7,4},{5,6},{6,5},{8,11},{11,8},{9,1... | collective-permute-start | bytes 233480 | tf_op jit(solution)/shard_map/ppermute | solution.py:40
  6.0 5.8 %collective-permute-start.1 = (bf16[19,16,128]{2,1,0:T(8,128)(2,1)S(1)}, bf16[19,16,128]{2,1,0:T(8,128)(2,1)S(1)}, u32[]{:S(2)}, u32[]{:S(2)}) collective-permute-start(bf16[19,16,128]{2,1,0:T(8,128)(2,1)S(1)} %get-tuple-element.18.own_ref), channel_id=1, source_target_pairs={{0,1},{1,0},{2,3},{3,2},{4,5},{5,4},{6,7},{7,6},{8,9},{9,8},{10,11... | collective-permute-start | bytes 233480 | tf_op jit(solution)/shard_map/ppermute | solution.py:40
  6.0 5.7 %collective-permute-start.2 = (bf16[8,16,128]{2,1,0:T(8,128)(2,1)S(1)}, bf16[8,16,128]{2,1,0:T(8,128)(2,1)S(1)}, u32[]{:S(2)}, u32[]{:S(2)}) collective-permute-start(bf16[8,16,128]{2,1,0:T(8,128)(2,1)S(1)} %get-tuple-element.20.own_ref), channel_id=1, source_target_pairs={{0,2},{2,0},{1,3},{3,1},{4,6},{6,4},{5,7},{7,5},{8,10},{10,8},{9,1... | collective-permute-start | bytes 98312 | tf_op jit(solution)/shard_map/ppermute | solution.py:40
  11.8 10.5 %collective-permute-start.3 = (bf16[43,16,128]{2,1,0:T(8,128)(2,1)S(1)}, bf16[43,16,128]{2,1,0:T(8,128)(2,1)S(1)}, u32[]{:S(2)}, u32[]{:S(2)}) collective-permute-start(bf16[43,16,128]{2,1,0:T(8,128)(2,1)S(1)} %group.1.refs_3_), channel_id=1, source_target_pairs={{0,4},{4,0},{8,12},{12,8},{16,20},{20,16},{24,28},{28,24},{1,5},{5... | collective-permute-start | bytes 528392 | tf_op jit(solution)/shard_map/ppermute | solution.py:40
  13.1 9.2 %collective-permute-start.4 = (bf16[43,16,128]{2,1,0:T(8,128)(2,1)S(1)}, bf16[43,16,128]{2,1,0:T(8,128)(2,1)S(1)}, u32[]{:S(2)}, u32[]{:S(2)}) collective-permute-start(bf16[43,16,128]{2,1,0:T(8,128)(2,1)S(1)} %group.1.refs_3_), channel_id=1, source_target_pairs={{4,8},{8,4},{12,16},{16,12},{20,24},{24,20},{5,9},{9,5},{13,17},{1... | collective-permute-start | bytes 528392 | tf_op jit(solution)/shard_map/ppermute | solution.py:40

commit v11 on v10

--- a/solution.py
+++ b/solution.py
@@ -25,7 +25,7 @@
     -2.5051753759896685e-08, 1.6052905945426492e-10, -7.584986682610132e-13, 2.4682378516637708e-15,
 )
 ITEMS = 4
-ROWS = 32
+ROWS = 64
 STAGES = 2
 FIRST_ITEMS = 6
 AHEAD = 2

time: 29.2 us -> 29.8 us (1.021)
  Pallas kernels: 19.5 us -> 20.2 us
    pallas_call x1, Pallas kernels: 6.02 us -> 6.7 us  [per_device(): pl.pallas_call(functools.partial(near_kernel, entries), out_shape=(shaped...]
  transfers between devices with their start and end apart: 5 -> 5, of which waited for: 0 -> 0; matrix products, arithmetic and copies ran while one was open for 0% -> 0% of each run, Pallas kernels for 40% -> 41%
where the time goes in v11:
time: 29.8 us; the launch traced here: 29.3 us
  Pallas kernels  20.2 us (68%)
  starting transfers between devices  9.05 us (30%)
    ppermute x5, starting transfers between devices, swapped(): lax.ppermute(x, axis, [way for i, j in pairs for way in ((i, j), (j, i))])  9.05 us
    pallas_call x1, Pallas kernels, per_device(): pl.pallas_call(functools.partial(near_kernel, entries), out_shape=(shaped...  6.7 us
    pallas_call x1, Pallas kernels, per_device(): pl.pallas_call(functools.partial(incoming_kernel, entries, len(packets) -...  6.34 us
    pallas_call x1, Pallas kernels, per_device(): pl.pallas_call(functools.partial(prepare_kernel, entries), out_shape=(sha...  5.36 us
    pallas_call x1, Pallas kernels, per_device(): pl.pallas_call(outgoing_kernel, out_shape=(shaped((own_rows + spectra_row...  1.75 us
  transfers between devices with their start and end apart: 5, of which 0 were waited for; matrix products, arithmetic and copies ran while one was open for 0% of the time, Pallas kernels for 41%

profile of v11, /device:TPU:1, one launch (start us, length us, event | category | flops | bytes accessed | tf_op | source)
XLA Modules:
  0.0 29.3 jit_solution(4341653405456838289)
XLA Ops:
  0.0 1.7 %outgoing.1 = (bf16[19,16,128]{2,1,0:T(8,128)(2,1)S(1)}, bf16[8,16,128]{2,1,0:T(8,128)(2,1)S(1)}, bf16[128,512]{1,0:T(8,128)(2,1)S(1)}, f32[8,512]{1,0:T(8,128)S...) custom-call(bf16[8,16,128]{2,1,0:T(8,128)(2,1)} %bitcast.4, ...), custom_call_target="tpu_custom_call" | custom-call | tf_op jit(solution)/shard_map/outgoing/pallas_call | solution.py:542
  1.8 4.2 %collective-permute-start = (bf16[19,16,128]{2,1,0:T(8,128)(2,1)S(1)}, bf16[19,16,128]{2,1,0:T(8,128)(2,1)S(1)}, u32[]{:S(2)}, u32[]{:S(2)}) collective-permute-start(bf16[19,16,128]{2,1,0:T(8,128)(2,1)S(1)} %get-tuple-element.18.own_ref), channel_id=1, source_target_pairs={{0,3},{3,0},{1,2},{2,1},{4,7},{7,4},{5,6},{6,5},{8,11},{11,8},{9,1... | collective-permute-start | bytes 233480 | tf_op jit(solution)/shard_map/ppermute | solution.py:40
  6.0 0.0 collective-permute-start.1
  6.0 0.4 %collective-permute-start.2 = (bf16[8,16,128]{2,1,0:T(8,128)(2,1)S(1)}, bf16[8,16,128]{2,1,0:T(8,128)(2,1)S(1)}, u32[]{:S(2)}, u32[]{:S(2)}) collective-permute-start(bf16[8,16,128]{2,1,0:T(8,128)(2,1)S(1)} %get-tuple-element.20.own_ref), channel_id=1, source_target_pairs={{0,2},{2,0},{1,3},{3,1},{4,6},{6,4},{5,7},{7,5},{8,10},{10,8},{9,1... | collective-permute-start | bytes 98312 | tf_op jit(solution)/shard_map/ppermute | solution.py:40
  6.3 5.4 %prepare.1 = (f32[16,8,128]{2,1,0:T(8,128)S(1)}, bf16[16,16,128]{2,1,0:T(8,128)(2,1)S(1)}, bf16[48,128,128]{2,1,0:T(8,128)(2,1)S(1)}, f32[48,8,128]{2,1,0:T(8,128)S(1)}, f32[2,24,2,512]{3,2,1,0:T(2,128)S(1)}) custom-call(bf16[19,16,128]{2,1,0:T(8,128)(2,1)S(1)} %get-tuple-element.18.own_ref, s32[1,384]{1,0:T(1,128)S(1)} %get-tuple-element.19.items_ref.refs_1_, ...), custom_call_target="tpu_custom_call" | custom-call | tf_op jit(solution)/shard_map/prepare/pallas_call | solution.py:573
  11.7 0.0 collective-permute-done.2.refs_1_
  11.7 0.0 collective-permute-done.refs_2_.refs_1_.refs_0_
  11.7 0.0 collective-permute-done.1.refs_0_
  11.8 1.3 %collective-permute-start.3 = (bf16[43,16,128]{2,1,0:T(8,128)(2,1)S(1)}, bf16[43,16,128]{2,1,0:T(8,128)(2,1)S(1)}, u32[]{:S(2)}, u32[]{:S(2)}) collective-permute-start(bf16[43,16,128]{2,1,0:T(8,128)(2,1)S(1)} %group.1.refs_3_), channel_id=1, source_target_pairs={{0,4},{4,0},{8,12},{12,8},{16,20},{20,16},{24,28},{28,24},{1,5},{5... | collective-permute-start | bytes 528392 | tf_op jit(solution)/shard_map/ppermute | solution.py:40
  13.1 3.2 %collective-permute-start.4 = (bf16[43,16,128]{2,1,0:T(8,128)(2,1)S(1)}, bf16[43,16,128]{2,1,0:T(8,128)(2,1)S(1)}, u32[]{:S(2)}, u32[]{:S(2)}) collective-permute-start(bf16[43,16,128]{2,1,0:T(8,128)(2,1)S(1)} %group.1.refs_3_), channel_id=1, source_target_pairs={{4,8},{8,4},{12,16},{16,12},{20,24},{24,20},{5,9},{9,5},{13,17},{1... | collective-permute-start | bytes 528392 | tf_op jit(solution)/shard_map/ppermute | solution.py:40
  16.2 6.7 %near.1 = (f32[16,8,128]{2,1,0:T(8,128)S(1)}, bf16[48,128,128]{2,1,0:T(8,128)(2,1)S(1)}, f32[48,8,128]{2,1,0:T(8,128)S(1)}) custom-call(s32[1,384]{1,0:T(1,128)S(1)} %get-tuple-element.19.items_ref.refs_1_, bf16[19,16,128]{2,1,0:T(8,128)(2,1)S(1)} %collective-permute-done.1.refs_0_, ...), custom_call_target="tpu_custom_call", output_to_operand_aliasing={{1}: (5, {}), {2}: (6, {})} | custom-call | tf_op jit(solution)/shard_map/near/pallas_call | solution.py:610
  23.0 0.0 collective-permute-done.3.refs_2_
  23.0 0.0 collective-permute-done.4.refs_4_
  23.0 6.3 %incoming.1 = f32[16,8,128]{2,1,0:T(8,128)} custom-call(bf16[19,16,128]{2,1,0:T(8,128)(2,1)S(1)} %collective-permute-done.refs_2_.refs_1_.refs_0_, s32[1,384]{1,0:T(1,128)S(1)} %get-tuple-element.19.items_ref.refs_1_, bf16[43,16,128]{2,1,0:T(8,128)(2,1)S(1)} %collective-permute-done.3.refs_2_, bf16[43,16,128]{2,1,0:T(8,128)(2,1)S(1)} %group.1.refs_3_, ...), custom_call_target="tpu_custom_call" | custom-call | tf_op jit(solution)/shard_map/incoming/pallas_call | solution.py:625
  (1 shorter events, 0.0 us)
Async XLA Ops:
  1.8 10.0 %collective-permute-start = (bf16[19,16,128]{2,1,0:T(8,128)(2,1)S(1)}, bf16[19,16,128]{2,1,0:T(8,128)(2,1)S(1)}, u32[]{:S(2)}, u32[]{:S(2)}) collective-permute-start(bf16[19,16,128]{2,1,0:T(8,128)(2,1)S(1)} %get-tuple-element.18.own_ref), channel_id=1, source_target_pairs={{0,3},{3,0},{1,2},{2,1},{4,7},{7,4},{5,6},{6,5},{8,11},{11,8},{9,1... | collective-permute-start | bytes 233480 | tf_op jit(solution)/shard_map/ppermute | solution.py:40
  6.0 5.8 %collective-permute-start.1 = (bf16[19,16,128]{2,1,0:T(8,128)(2,1)S(1)}, bf16[19,16,128]{2,1,0:T(8,128)(2,1)S(1)}, u32[]{:S(2)}, u32[]{:S(2)}) collective-permute-start(bf16[19,16,128]{2,1,0:T(8,128)(2,1)S(1)} %get-tuple-element.18.own_ref), channel_id=1, source_target_pairs={{0,1},{1,0},{2,3},{3,2},{4,5},{5,4},{6,7},{7,6},{8,9},{9,8},{10,11... | collective-permute-start | bytes 233480 | tf_op jit(solution)/shard_map/ppermute | solution.py:40
  6.0 5.7 %collective-permute-start.2 = (bf16[8,16,128]{2,1,0:T(8,128)(2,1)S(1)}, bf16[8,16,128]{2,1,0:T(8,128)(2,1)S(1)}, u32[]{:S(2)}, u32[]{:S(2)}) collective-permute-start(bf16[8,16,128]{2,1,0:T(8,128)(2,1)S(1)} %get-tuple-element.20.own_ref), channel_id=1, source_target_pairs={{0,2},{2,0},{1,3},{3,1},{4,6},{6,4},{5,7},{7,5},{8,10},{10,8},{9,1... | collective-permute-start | bytes 98312 | tf_op jit(solution)/shard_map/ppermute | solution.py:40
  11.8 11.2 %collective-permute-start.3 = (bf16[43,16,128]{2,1,0:T(8,128)(2,1)S(1)}, bf16[43,16,128]{2,1,0:T(8,128)(2,1)S(1)}, u32[]{:S(2)}, u32[]{:S(2)}) collective-permute-start(bf16[43,16,128]{2,1,0:T(8,128)(2,1)S(1)} %group.1.refs_3_), channel_id=1, source_target_pairs={{0,4},{4,0},{8,12},{12,8},{16,20},{20,16},{24,28},{28,24},{1,5},{5... | collective-permute-start | bytes 528392 | tf_op jit(solution)/shard_map/ppermute | solution.py:40
  13.1 9.9 %collective-permute-start.4 = (bf16[43,16,128]{2,1,0:T(8,128)(2,1)S(1)}, bf16[43,16,128]{2,1,0:T(8,128)(2,1)S(1)}, u32[]{:S(2)}, u32[]{:S(2)}) collective-permute-start(bf16[43,16,128]{2,1,0:T(8,128)(2,1)S(1)} %group.1.refs_3_), channel_id=1, source_target_pairs={{4,8},{8,4},{12,16},{16,12},{20,24},{24,20},{5,9},{9,5},{13,17},{1... | collective-permute-start | bytes 528392 | tf_op jit(solution)/shard_map/ppermute | solution.py:40
